TPU v7x, 128 devices: a whole 4x4x4 slice. The times are simulated.
128 devices in a mesh: rep: 2 (over z_hi), row: 2 (over z_lo), col: 32 (over y, x, core).
Axes of the slice: x: 4, y: 4, z: 4 (z_hi: 2, z_lo: 2; z = z_hi * 2 + z_lo), core: 2. Of those that a mesh axis runs over, the one named last changes fastest.
Arguments:
- tokens: bfloat16 [2, 32, 512, 1024], P('rep', 'row', 'col'), may hold values from -6 to 6
- cotangent: bfloat16 [2, 32, 512, 1024], P('rep', 'row', 'col'), may hold values from -6 to 6
- row_field: int32 [2, 32], P('rep'), may hold values from 0 to 8, never falling along the last dimension, each value on 1 to 16 neighbouring positions
- col_field: int32 [2, 512], P('rep'), may hold values from 0 to 63, never falling along the last dimension, each value on 1 to 16 neighbouring positions
- qkv_weight: bfloat16 [1024, 3072], replicated, may hold values from -0.1875 to 0.1875
- qkv_bias: float32 [3072], replicated, may hold values from -3 to 3
- logit_scale: float32 [32], replicated, may hold values from 2 to 20
- position_bias: float32 [32, 64, 64], replicated, may hold values from 0 to 6
- proj_weight: bfloat16 [1024, 1024], replicated, may hold values from -0.1875 to 0.1875
- proj_bias: float32 [1024], replicated, may hold values from -5 to 5
- norm_gain: float32 [1024], replicated, may hold values from 0.5 to 1.5
- norm_shift: float32 [1024], replicated, may hold values from -3 to 3
Outputs:
- block_out: bfloat16 [2, 32, 512, 1024], P('rep', 'row', 'col')
- grad_tokens: bfloat16 [2, 32, 512, 1024], P('rep', 'row', 'col')
- grad_qkv_weight: float32 [1024, 3072], P(('rep', 'row', 'col'))
- grad_proj_weight: float32 [1024, 1024], P(('rep', 'row', 'col'))
- grad_qkv_bias: float32 [3072], replicated
- grad_proj_bias: float32 [1024], replicated
- grad_gain: float32 [1024], replicated
- grad_shift: float32 [1024], replicated
- grad_logit_scale: float32 [32], replicated
- grad_position_bias: float32 [32, 64, 64], replicated
Inputs may be any that keep to these rules, and one draw needn't show every extreme that they name: `row_field`: field numbers never fall along a slab's rows; a field spans one or more consecutive rows. `col_field`: field numbers never fall along a slab's columns; a field spans one or more consecutive columns.
All inputs are finite; a program needn't handle non-finite values.
Results may differ from a plain program's by a relative error of at most 0.012.
The roundings to bfloat16 on the way count: a program that leaves them out, or rounds other values in their place, can miss the bound.
Values may be sent and summed in bfloat16 or wider, within the bound.
No kernel may reach another device: no remote copies, remote signals or barrier semaphores. Data moves between devices by JAX's collectives and lax.ppermute only.
A program may use at most 192 MiB of HBM per device.

v0:
```python
import jax
import jax.numpy as jnp
from jax import lax
from jax.sharding import PartitionSpec as P

HEADS = 32
WIN = 8
SHIFT = 4


norm_epsilon = 1e-05
unit_floor = 1e-12


def passed_along(x, axis, by):
    size = lax.axis_size(axis)
    return lax.ppermute(x, axis, [(i, (i + by) % size) for i in range(size)])


def to_windows(values, row_count, col_count, window):
    pieces, head_count, head_size = (values.shape[1], values.shape[2], values.shape[3])
    values = values.reshape(
        row_count // window, window, col_count // window, window, pieces, head_count, head_size
    )
    values = values.transpose(0, 2, 4, 5, 1, 3, 6)
    return values.reshape(
        row_count // window * (col_count // window), pieces, head_count, window * window, head_size
    )


def from_windows(values, row_count, col_count, window):
    pieces, head_count, head_size = (values.shape[1], values.shape[2], values.shape[4])
    values = values.reshape(
        row_count // window, col_count // window, pieces, head_count, window, window, head_size
    )
    values = values.transpose(0, 4, 1, 5, 2, 3, 6)
    return values.reshape(row_count * col_count, pieces * head_count * head_size)


def unit_rows(raw_rows):
    length = jnp.sqrt(jnp.sum(raw_rows * raw_rows, axis=-1, keepdims=True))
    scale_back = 1.0 / jnp.maximum(length, unit_floor)
    return (raw_rows * scale_back, scale_back)


def field_mask(row_ids, col_ids, window):
    row_blocks = row_ids.reshape(-1, window)
    col_blocks = col_ids.reshape(-1, window)
    grid_shape = (row_blocks.shape[0], col_blocks.shape[0], window, window)
    row_token = jnp.broadcast_to(row_blocks[:, None, :, None], grid_shape).reshape(
        -1, window * window
    )
    col_token = jnp.broadcast_to(col_blocks[None, :, None, :], grid_shape).reshape(
        -1, window * window
    )
    allowed = (row_token[:, :, None] == row_token[:, None, :]) & (
        col_token[:, :, None] == col_token[:, None, :]
    )
    return allowed.astype(jnp.float32)[:, None]


def block_step(
    shifted,
    grad_branch,
    row_ids,
    col_ids,
    qkv_weight,
    qkv_bias,
    logit_scale,
    position_bias,
    proj_weight,
    proj_bias,
    norm_gain,
    norm_shift,
):
    row_count, col_count, model_width = shifted.shape
    window = WIN
    head_size = model_width // HEADS
    flat_rows = shifted.reshape(row_count * col_count, model_width)
    qkv_rows = (
        jnp.dot(flat_rows, qkv_weight, preferred_element_type=jnp.float32) + qkv_bias
    ).astype(jnp.bfloat16)
    windows = to_windows(qkv_rows.reshape(-1, 3, HEADS, head_size), row_count, col_count, window)
    query_raw = windows[:, 0].astype(jnp.float32)
    key_raw = windows[:, 1].astype(jnp.float32)
    value_win = windows[:, 2]
    query_unit, query_inv = unit_rows(query_raw)
    key_unit, key_inv = unit_rows(key_raw)
    query_cast = query_unit.astype(jnp.bfloat16)
    key_cast = key_unit.astype(jnp.bfloat16)
    cosine = jnp.einsum("nhid,nhjd->nhij", query_cast, key_cast, preferred_element_type=jnp.float32)
    scores = logit_scale[None, :, None, None] * cosine + position_bias[None]
    allowed = field_mask(row_ids, col_ids, window)
    weights = jnp.exp(scores) * allowed
    totals = jnp.sum(weights, axis=-1, keepdims=True)
    attention = (weights / totals).astype(jnp.bfloat16)
    attention_f = attention.astype(jnp.float32)
    attended = jnp.einsum(
        "nhij,nhjd->nhid", attention, value_win, preferred_element_type=jnp.float32
    ).astype(jnp.bfloat16)
    mixed_flat = from_windows(attended[:, None], row_count, col_count, window)
    projected = jnp.dot(mixed_flat, proj_weight, preferred_element_type=jnp.float32) + proj_bias
    centre = projected - jnp.mean(projected, axis=-1, keepdims=True)
    variance = jnp.mean(centre * centre, axis=-1, keepdims=True)
    inv_std = lax.rsqrt(variance + norm_epsilon)
    normed = centre * inv_std
    branch = (normed * norm_gain + norm_shift).astype(jnp.bfloat16)
    grad_out = grad_branch.reshape(row_count * col_count, model_width).astype(jnp.float32)
    sum_gain = jnp.sum(grad_out * normed, axis=0)
    sum_shift = jnp.sum(grad_out, axis=0)
    grad_normed = grad_out * norm_gain
    grad_projected = inv_std * (
        grad_normed
        - jnp.mean(grad_normed, axis=-1, keepdims=True)
        - normed * jnp.mean(grad_normed * normed, axis=-1, keepdims=True)
    )
    sum_proj_bias = jnp.sum(grad_projected, axis=0)
    grad_projected_low = grad_projected.astype(jnp.bfloat16)
    grad_mixed = jnp.dot(
        grad_projected_low, proj_weight.T, preferred_element_type=jnp.float32
    ).astype(jnp.bfloat16)
    grad_win = to_windows(
        grad_mixed.reshape(-1, 1, HEADS, head_size), row_count, col_count, window
    )[:, 0]
    grad_attention = jnp.einsum(
        "nhid,nhjd->nhij", grad_win, value_win, preferred_element_type=jnp.float32
    )
    grad_value = jnp.einsum(
        "nhij,nhid->nhjd", attention, grad_win, preferred_element_type=jnp.float32
    )
    grad_scores = attention_f * (
        grad_attention - jnp.sum(grad_attention * attention_f, axis=-1, keepdims=True)
    )
    sum_scale = jnp.sum(grad_scores * cosine, axis=(0, 2, 3))
    sum_bias = jnp.sum(grad_scores, axis=0)
    grad_cosine = (logit_scale[None, :, None, None] * grad_scores).astype(jnp.bfloat16)
    grad_query_unit = jnp.einsum(
        "nhij,nhjd->nhid", grad_cosine, key_cast, preferred_element_type=jnp.float32
    )
    grad_key_unit = jnp.einsum(
        "nhij,nhid->nhjd", grad_cosine, query_cast, preferred_element_type=jnp.float32
    )
    grad_query = query_inv * grad_query_unit - query_raw * query_inv**3 * jnp.sum(
        grad_query_unit * query_raw, axis=-1, keepdims=True
    )
    grad_key = key_inv * grad_key_unit - key_raw * key_inv**3 * jnp.sum(
        grad_key_unit * key_raw, axis=-1, keepdims=True
    )
    grad_windows = jnp.stack((grad_query, grad_key, grad_value), axis=1)
    grad_qkv = from_windows(grad_windows, row_count, col_count, window)
    sum_qkv_bias = jnp.sum(grad_qkv, axis=0)
    grad_qkv_low = grad_qkv.astype(jnp.bfloat16)
    grad_shifted = jnp.dot(grad_qkv_low, qkv_weight.T, preferred_element_type=jnp.float32).astype(
        jnp.bfloat16
    )
    partial_sums = (sum_bias, sum_scale, sum_qkv_bias, sum_proj_bias, sum_gain, sum_shift)
    return (
        branch.reshape(row_count, col_count, model_width),
        grad_shifted.reshape(row_count, col_count, model_width),
        flat_rows,
        mixed_flat,
        grad_projected_low,
        grad_qkv_low,
        partial_sums,
    )


def roll_rows(stacked, direction):
    length = stacked.shape[1]
    rim_rows = stacked[:, :SHIFT] if direction < 0 else stacked[:, length - SHIFT :]
    arrived = passed_along(rim_rows, "row", direction)
    if direction < 0:
        return jnp.concatenate((stacked[:, SHIFT:], arrived), axis=1)
    return jnp.concatenate((arrived, stacked[:, : length - SHIFT]), axis=1)


def roll_cols(stacked, direction):
    length = stacked.shape[2]
    rim_cols = stacked[:, :, :SHIFT] if direction < 0 else stacked[:, :, length - SHIFT :]
    arrived = passed_along(rim_cols, "col", direction)
    if direction < 0:
        return jnp.concatenate((stacked[:, :, SHIFT:], arrived), axis=2)
    return jnp.concatenate((arrived, stacked[:, :, : length - SHIFT]), axis=2)


def roll_both(stacked, direction):
    return roll_cols(roll_rows(stacked, direction), direction)


def per_device(
    tokens,
    cotangent,
    row_field,
    col_field,
    qkv_weight,
    qkv_bias,
    logit_scale,
    position_bias,
    proj_weight,
    proj_bias,
    norm_gain,
    norm_shift,
):
    row_local, col_local, model_width = (tokens.shape[1], tokens.shape[2], tokens.shape[3])
    moved = roll_both(jnp.stack((tokens[0], cotangent[0])), -1)
    row_ids = lax.dynamic_slice_in_dim(
        jnp.roll(row_field[0], -SHIFT), lax.axis_index("row") * row_local, row_local
    )
    col_ids = lax.dynamic_slice_in_dim(
        jnp.roll(col_field[0], -SHIFT), lax.axis_index("col") * col_local, col_local
    )
    branch, grad_shifted, flat_rows, mixed_flat, grad_projected_low, grad_qkv_low, partial_sums = (
        block_step(
            moved[0],
            moved[1],
            row_ids,
            col_ids,
            qkv_weight,
            qkv_bias,
            logit_scale,
            position_bias,
            proj_weight,
            proj_bias,
            norm_gain,
            norm_shift,
        )
    )
    returned = roll_both(jnp.stack((branch, grad_shifted)), 1)
    block_out = (tokens[0].astype(jnp.float32) + returned[0].astype(jnp.float32)).astype(
        jnp.bfloat16
    )[None]
    grad_tokens = (cotangent[0].astype(jnp.float32) + returned[1].astype(jnp.float32)).astype(
        jnp.bfloat16
    )[None]
    contract = (((0,), (0,)), ((), ()))
    qkv_part = lax.dot_general(
        flat_rows, grad_qkv_low, contract, preferred_element_type=jnp.float32
    )
    proj_part = lax.dot_general(
        mixed_flat, grad_projected_low, contract, preferred_element_type=jnp.float32
    )
    weight_grads = lax.psum_scatter(
        jnp.concatenate((qkv_part, proj_part), axis=1),
        ("rep", "row", "col"),
        scatter_dimension=0,
        tiled=True,
    )
    reduced = lax.psum(
        (
            partial_sums[0],
            partial_sums[1],
            partial_sums[2],
            partial_sums[3],
            partial_sums[4],
            partial_sums[5],
        ),
        ("rep", "row", "col"),
    )
    return (
        block_out,
        grad_tokens,
        weight_grads[:, : 3 * model_width],
        weight_grads[:, 3 * model_width :],
        reduced[2],
        reduced[3],
        reduced[4],
        reduced[5],
        reduced[1],
        reduced[0],
    )


def solution(mesh):
    placed = (
        P("rep", "row", "col", None),
        P("rep", "row", "col", None),
        P("rep", None),
        P("rep", None),
        P(),
        P(),
        P(),
        P(),
        P(),
        P(),
        P(),
        P(),
    )
    return jax.shard_map(
        per_device,
        mesh=mesh,
        in_specs=placed,
        out_specs=(
            P("rep", "row", "col", None),
            P("rep", "row", "col", None),
            P(("rep", "row", "col"), None),
            P(("rep", "row", "col"), None),
            P(),
            P(),
            P(),
            P(),
            P(),
            P(),
        ),
        check_vma=False,
    )
```

profile of v0, /device:TPU:0, one launch (start us, length us, event | category | flops | bytes accessed | tf_op | source)
XLA Modules:
  0.0 949.5 jit_solution(959222657102032497)
XLA Ops:
  18.1 4.0 collective-permute-start.1
  28.6 5.7 fusion.3
  34.4 8.4 reshape_reshape.6
  42.8 5.2 copy.49
  48.1 3.5 fusion.41
  60.5 3.4 fusion.4
  67.2 3.3 fusion.18
  73.5 5.4 copy.56
  78.8 4.2 reshape.126
  101.4 3.1 fusion.38
  104.5 6.8 fusion.15
  111.3 6.8 fusion.10
  118.1 4.0 fusion.35
  122.2 3.4 fusion.14
  125.6 4.2 copy.62
  134.7 8.5 fusion.2
  143.2 12.8 %copy.66 = bf16[2,8,2,8,3,32,32]{6,5,4,3,2,1,0:T(8,128)(2,1)} copy(bf16[2,8,2,8,3,32,32]{6,3,1,5,2,0,4:T(8,128)(2,1)} %fusion.2) | data formatting | bytes 3145728 | tf_op jit(solution)/shard_map/convert_element_type | solution.py:152
  155.9 8.6 convert_element_type.113
  166.8 6.0 pad_maximum_fusion
  172.9 4.8 convolution_convert_fusion
  179.3 4.8 collective-permute-done.2
  186.2 69.5 %all-reduce = (f32[3072]{0:T(1024)}, f32[1024]{0:T(1024)}, f32[1024]{0:T(1024)}, f32[1024]{0:T(1024)}, f32[32]{0:T(128)}) all-reduce(f32[3072]{0:T(1024)S(1)} %reduce_sum.157, f32[1024]{0:T(1024)S(1)} %get-tuple-element.31, f32[1024]{0:T(1024)S(1)} %get-tuple-element.22, ...), channel_id=1, replica_groups=mesh['rep'=2,'row'=2,'col'=32] {'rep','row','col'}, use_global_device_ids=true, to_apply=%region_12.13 | all-reduce | flops 6176 | bytes 49408 | tf_op jit(solution)/shard_map/psum | solution.py:248
  255.6 14.9 %all-reduce.3.cloned.1.call-done = f32[32,64,64]{1,2,0:T(8,128)} async-done(((f32[32,64,64]{1,2,0:T(8,128)}), f32[32,64,64]{1,2,0:T(8,128)}) %all-reduce.3.cloned.1.call-update) | async-done | bytes 524304 | tf_op jit(solution)/shard_map/psum | solution.py:248
  277.2 662.4 %reduce-scatter.2.cloned.1.call-done = f32[8,4096]{1,0:T(8,128)} async-done(((f32[1024,4096]{1,0:T(8,128)}), f32[8,4096]{1,0:T(8,128)}) %reduce-scatter.2.cloned.1.call-update) | async-done | bytes 131088 | tf_op jit(solution)/shard_map/reduce_scatter | solution.py:242
  (125 shorter events, 71.0 us)
Async XLA Ops:
  7.2 75.9 %copy-start = (bf16[1024,1024]{1,0:T(8,128)(2,1)S(1)}, bf16[1024,1024]{1,0:T(8,128)(2,1)}, u32[]{:S(2)}) copy-start(bf16[1024,1024]{1,0:T(8,128)(2,1)} %param.20) | copy-start | bytes 6291460
  7.2 4.5 copy-start.28
  7.2 4.9 copy-start.24
  7.2 263.3 %all-reduce.3.cloned.1.call-start = ((), (), s32[]{:S(2)}) async-start(), calls=%async_computation.2 | async-start | bytes 2097152 | tf_op jit(solution)/shard_map/psum | solution.py:248
  9.6 8.4 collective-permute-start
  11.8 10.3 %copy-start.15 = (bf16[2,12,16,1024]{3,2,1,0:T(8,128)(2,1)}, bf16[2,12,16,1024]{3,2,1,0:T(8,128)(2,1)S(1)}, u32[]{:S(2)}) copy-start(bf16[2,12,16,1024]{3,2,1,0:T(8,128)(2,1)S(1)} %slice.104) | copy-start | bytes 2359300
  15.2 10.8 %copy-start.21 = (f32[1024]{0:T(1024)S(1)}, f32[1024]{0:T(1024)}, u32[]{:S(2)}) copy-start(f32[1024]{0:T(1024)} %param.22) | copy-start | bytes 12292
  18.0 4.1 copy-start.20
  18.1 7.9 collective-permute-start.1
  48.1 4.0 copy-start.9
  55.1 5.3 copy-start.25
  78.8 4.3 copy-start.27
  96.3 4.1 copy-start.11
  96.3 5.1 copy-start.6
  118.1 4.1 copy-start.12
  122.1 817.4 %reduce-scatter.2.cloned.1.call-start = ((), (), s32[]{:S(2)}) async-start(), calls=%async_computation.1 | async-start | bytes 16908288 | tf_op jit(solution)/shard_map/reduce_scatter | solution.py:242
  155.9 8.6 copy-start.18
  172.8 4.8 copy-start.14
  172.8 11.5 %copy-start.2 = (f32[4,32,64,32]{3,2,1,0:T(8,128)S(1)}, f32[4,32,64,32]{3,2,1,0:T(8,128)}, u32[]{:S(2)}) copy-start(f32[4,32,64,32]{3,2,1,0:T(8,128)} %fusion.43) | copy-start | bytes 3145732
  172.8 11.5 %copy-start.7 = (f32[4,32,64,32]{3,2,1,0:T(8,128)S(1)}, f32[4,32,64,32]{3,2,1,0:T(8,128)}, u32[]{:S(2)}) copy-start(f32[4,32,64,32]{3,2,1,0:T(8,128)} %copy.62) | copy-start | bytes 3145732
  172.8 11.5 %copy-start.8 = (f32[4,32,64,32]{3,2,1,0:T(8,128)S(1)}, f32[4,32,64,32]{3,2,1,0:T(8,128)}, u32[]{:S(2)}) copy-start(f32[4,32,64,32]{3,2,1,0:T(8,128)} %copy.60) | copy-start | bytes 3145732
  177.7 6.5 collective-permute-start.2
  184.3 88.8 %collective-permute-start.3 = (bf16[2,16,4,1024]{3,2,1,0:T(4,128)(2,1)S(1)}, bf16[2,16,4,1024]{3,2,1,0:T(4,128)(2,1)}, u32[]{:S(2)}, u32[]{:S(2)}) collective-permute-start(bf16[2,16,4,1024]{3,2,1,0:T(4,128)(2,1)S(1)} %pad_maximum_fusion.4), channel_id=1, source_target_pairs={{0,1},{1,2},{2,3},{3,4},{4,5},{5,6},{6,7},{7,8},{8,9},{9,10},{10,1... | collective-permute-start | bytes 786440 | tf_op jit(solution)/shard_map/ppermute | solution.py:17
  273.1 669.4 %copy-start.1 = (bf16[1024,1024]{1,0:T(8,128)(2,1)S(1)}, bf16[1024,1024]{1,0:T(8,128)(2,1)}, u32[]{:S(2)}) copy-start(bf16[1024,1024]{1,0:T(8,128)(2,1)} %param.20) | copy-start | bytes 6291460
  (11 other events, 20.5 us)
Sparse Core Ops, SparseCore 0:
  122.3 148.2 all-reduce.2
  273.1 666.4 reduce-scatter.1
where the time goes:
time: 954 us; the launch traced here: 950 us
  waiting for transfers between devices  687 us (72%)
  local copies, waits for them, and re-layouts  85.4 us (9%)
  blocking collectives  69.5 us (7%)
  matrix products  45.7 us (5%)
  other arithmetic  39 us (4%)
  between operations  14.7 us (2%)
    reduce_scatter x1, waiting for transfers between devices, per_device(): lax.psum_scatter(jnp.concatenate((qkv_part, proj_part), axis=1), ('rep',...  662 us
    psum x1, blocking collectives, per_device(): lax.psum((partial_sums[0], partial_sums[1], partial_sums[2], partial_sums...  69.5 us
    convert_element_type x2, local copies, waits for them, and re-layouts, block_step(): grad_qkv_low = grad_qkv.astype(jnp.bfloat16)  21.4 us
  transfers between devices with their start and end apart: 6, of which 5 were waited for; matrix products, arithmetic and copies ran while one was open for 7% of the time, Pallas kernels for 0%

commit v1 on v0

v1 whole, which is shorter than its diff:
```python
import functools

import jax
import jax.numpy as jnp
import numpy as np
from jax import lax
from jax.experimental import pallas as pl
from jax.experimental.pallas import tpu as pltpu
from jax.sharding import PartitionSpec as P

HEADS = 32
WIN = 8
SHIFT = 4
SIDE = 16
TOK = SIDE * SIDE
D = 1024
HALO = SIDE * SHIFT
CORNER = SHIFT * SHIFT
CAT = TOK + 2 * HALO + CORNER
WIN2 = WIN * WIN
WINDOWS = TOK // WIN2
GROUP = 4
GROUPS = HEADS // GROUP
LANES = 128
WIDE = GROUP * WIN2
AXES = ("rep", "row", "col")

norm_epsilon = 1e-05
unit_floor = 1e-12
f32 = jnp.float32
bf16 = jnp.bfloat16
VMEM_LIMIT = 56 * 1024 * 1024


def window_order():
    order = np.zeros((TOK, CAT), np.float32)
    for r in range(SIDE):
        for c in range(SIDE):
            n = ((r // WIN) * 2 + c // WIN) * WIN2 + (r % WIN) * WIN + c % WIN
            rr, cc = r + SHIFT, c + SHIFT
            if rr < SIDE and cc < SIDE:
                m = rr * SIDE + cc
            elif cc < SIDE:
                m = TOK + (rr - SIDE) * SIDE + cc
            elif rr < SIDE:
                m = TOK + HALO + rr * SHIFT + (cc - SIDE)
            else:
                m = TOK + 2 * HALO + (rr - SIDE) * SHIFT + (cc - SIDE)
            order[n, m] = 1.0
    return order


def border_spread():
    spread = np.zeros((TOK, HALO + CORNER), np.float32)
    for r in range(SIDE):
        for c in range(SHIFT):
            spread[r * SIDE + c, r * SHIFT + c] = 1.0
    for r in range(SHIFT):
        for c in range(SHIFT):
            spread[r * SIDE + c, HALO + r * SHIFT + c] = 1.0
    return spread


def head_mask():
    rows = np.arange(WIDE)[:, None] // WIN2
    cols = np.arange(LANES)[None, :] // (LANES // GROUP)
    return (rows == cols).astype(np.float32)


def head_sums():
    a = np.arange(2 * LANES)[:, None] % LANES // (LANES // GROUP)
    b = np.arange(LANES)[None, :] // (LANES // GROUP)
    return (a == b).astype(np.float32)


def mm(a, b):
    return jnp.dot(a, b, preferred_element_type=f32)


def mm_tb(a, b):
    return lax.dot_general(a, b, (((1,), (1,)), ((), ())), preferred_element_type=f32)


def mm_ta(a, b):
    return lax.dot_general(a, b, (((0,), (0,)), ((), ())), preferred_element_type=f32)


def segment_sums(values, ones):
    high = values.astype(bf16)
    low = (values - high.astype(f32)).astype(bf16)
    return mm(jnp.concatenate((high, low), axis=1), ones)


def inverse_length(raw, ones):
    total = segment_sums(raw * raw, ones)
    return 1.0 / jnp.maximum(jnp.sqrt(total), unit_floor)


def stacked_heads(x, mask):
    return jnp.concatenate((x, x, x, x), axis=0) * mask


def own_heads(wide, mask):
    out = wide[:WIN2] * mask[:WIN2].astype(f32)
    for h in range(1, GROUP):
        out = out + wide[h * WIN2 : (h + 1) * WIN2] * mask[h * WIN2 : (h + 1) * WIN2].astype(f32)
    return out


def forward_kernel(
    fields, tok, tok_row, tok_col, tok_cor, cot, cot_row, cot_col, cot_cor, order, order_t, mask_ref, ones_ref,
    wqkv, bqkv, scale, bias_t, wproj, bproj, gain, shift,
    x_out, qkv, att, mixed, gp, b_own, b_row, b_col, b_cor, sums, cat, branch, grad,
):
    cat[0:TOK] = tok[...]
    cat[TOK : TOK + HALO] = tok_row[...]
    cat[TOK + HALO : TOK + 2 * HALO] = tok_col[...]
    cat[TOK + 2 * HALO : CAT] = tok_cor[...]
    x_out[...] = mm(order[...], cat[...]).astype(bf16)
    cat[0:TOK] = cot[...]
    cat[TOK : TOK + HALO] = cot_row[...]
    cat[TOK + HALO : TOK + 2 * HALO] = cot_col[...]
    cat[TOK + 2 * HALO : CAT] = cot_cor[...]
    grad[...] = mm(order[...], cat[...]).astype(bf16)

    @pl.loop(0, 3 * D // 512)
    def _(n):
        cols = pl.ds(pl.multiple_of(n * 512, 512), 512)
        qkv[:, cols] = (mm(x_out[...], wqkv[:, cols]) + bqkv[:, cols]).astype(bf16)

    sub = lax.broadcasted_iota(jnp.int32, (WIN2, WIDE), 0)
    lane = lax.broadcasted_iota(jnp.int32, (WIN2, WIDE), 1) % WIN2
    allowed = []
    for w in range(WINDOWS):
        id_sub = jnp.zeros((WIN2, WIDE), jnp.int32)
        id_lane = jnp.zeros((WIN2, WIDE), jnp.int32)
        for i in range(WIN):
            rid = fields[0, (w // 2) * WIN + i] * 1024
            cid = fields[1, (w % 2) * WIN + i]
            id_sub = id_sub + jnp.where(sub // WIN == i, rid, 0) + jnp.where(sub % WIN == i, cid, 0)
            id_lane = id_lane + jnp.where(lane // WIN == i, rid, 0) + jnp.where(lane % WIN == i, cid, 0)
        allowed.append((id_sub == id_lane).astype(f32))
    mask = mask_ref[...]
    ones = ones_ref[...]

    @pl.loop(0, GROUPS)
    def _(g):
        at = pl.multiple_of(g * LANES, LANES)
        qs = pl.ds(at, LANES)
        ks = pl.ds(at + D, LANES)
        vs = pl.ds(at + 2 * D, LANES)
        q = qkv[:, qs].astype(f32)
        k = qkv[:, ks].astype(f32)
        v = qkv[:, vs]
        qu = (q * inverse_length(q, ones)).astype(bf16)
        ku = (k * inverse_length(k, ones)).astype(bf16)
        sc = scale[pl.ds(g, 1), :]
        bias = bias_t[g]
        for w in range(WINDOWS):
            rows = slice(w * WIN2, (w + 1) * WIN2)
            cosine = mm_tb(ku[rows], stacked_heads(qu[rows], mask))
            weights = jnp.exp(sc * cosine + bias) * allowed[w]
            total = jnp.sum(weights, axis=0, keepdims=True)
            attention = (weights * (1.0 / total)).astype(bf16)
            att[g, w] = attention
            mixed[rows, qs] = own_heads(mm_ta(attention, v[rows]), mask).astype(bf16)

    gain_v = gain[...]
    shift_v = shift[...]
    sums[...] = jnp.zeros_like(sums)
    for w in range(WINDOWS):
        rows = slice(w * WIN2, (w + 1) * WIN2)
        projected = mm(mixed[rows, :], wproj[...]) + bproj[...]
        centre = projected - jnp.mean(projected, axis=-1, keepdims=True)
        inv_std = lax.rsqrt(jnp.mean(centre * centre, axis=-1, keepdims=True) + norm_epsilon)
        normed = centre * inv_std
        branch[rows, :] = (normed * gain_v + shift_v).astype(bf16)
        go = grad[rows, :].astype(f32)
        gn = go * gain_v
        gpf = inv_std * (
            gn - jnp.mean(gn, axis=-1, keepdims=True) - normed * jnp.mean(gn * normed, axis=-1, keepdims=True)
        )
        gp[rows, :] = gpf.astype(bf16)
        sums[0:1, :] += jnp.sum(gpf, axis=0, keepdims=True)
        sums[1:2, :] += jnp.sum(go * normed, axis=0, keepdims=True)
        sums[2:3, :] += jnp.sum(go, axis=0, keepdims=True)
    put_back(order_t, branch, b_own, b_row, b_col, b_cor)


def put_back(order_t, source, own, row, col, cor):
    src = source[...]
    own[...] = mm(order_t[0:TOK], src).astype(bf16)
    row[...] = mm(order_t[TOK : TOK + HALO], src).astype(bf16)
    col[...] = mm(order_t[TOK + HALO : TOK + 2 * HALO], src).astype(bf16)
    cor[...] = mm(order_t[TOK + 2 * HALO : CAT], src).astype(bf16)


def attention_grad_kernel(
    half, qkv, att, gp, wproj, scale, mask_ref, ones_ref, g_keep, g_send, pos, scale_sums, bias_sums, gm
):
    p = half[0]
    gm[...] = mm_tb(gp[...], wproj[...]).astype(bf16)
    mask = mask_ref[...]
    ones = ones_ref[...]

    @pl.loop(0, GROUPS)
    def _(g):
        at = pl.multiple_of(g * LANES, LANES)
        qs = pl.ds(at, LANES)
        ks = pl.ds(at + D, LANES)
        vs = pl.ds(at + 2 * D, LANES)
        q = qkv[:, qs].astype(f32)
        k = qkv[:, ks].astype(f32)
        v = qkv[:, vs]
        q_inv = inverse_length(q, ones)
        k_inv = inverse_length(k, ones)
        qu = (q * q_inv).astype(bf16)
        ku = (k * k_inv).astype(bf16)
        gmx = gm[:, qs]
        sc = scale[pl.ds(g, 1), :]
        pos_sum = jnp.zeros((WIN2, WIDE), f32)
        sc_sum = jnp.zeros((1, WIDE), f32)
        gqu, gku, gv = [], [], []
        for w in range(WINDOWS):
            rows = slice(w * WIN2, (w + 1) * WIN2)
            q_heads = stacked_heads(qu[rows], mask)
            g_heads = stacked_heads(gmx[rows], mask)
            cosine = mm_tb(ku[rows], q_heads)
            grad_att = mm_tb(v[rows], g_heads)
            attention = att[g, w]
            gv.append(mm(attention, g_heads))
            att_f = attention.astype(f32)
            dots = jnp.sum(grad_att * att_f, axis=0, keepdims=True)
            grad_scores = att_f * (grad_att - dots)
            pos_sum = pos_sum + grad_scores
            sc_sum = sc_sum + jnp.sum(grad_scores * cosine, axis=0, keepdims=True)
            grad_cos = (sc * grad_scores).astype(bf16)
            gku.append(mm(grad_cos, q_heads))
            gqu.append(own_heads(mm_ta(grad_cos, ku[rows]), mask))
        scale_sums[pl.ds(g, 1), :] = sc_sum
        pos[pl.ds(pl.multiple_of(g * WIDE, WIDE), WIDE), :] = pos_sum.T
        gqu = jnp.concatenate(gqu, axis=0)
        gku = jnp.concatenate(gku, axis=0)
        gvf = jnp.concatenate(gv, axis=0)
        gqf = q_inv * gqu - q * (q_inv * q_inv * q_inv) * segment_sums(gqu * q, ones)
        gkf = k_inv * gku - k * (k_inv * k_inv * k_inv) * segment_sums(gku * k, ones)
        bias_sums[0:1, qs] = jnp.sum(gqf, axis=0, keepdims=True)
        bias_sums[1:2, qs] = jnp.sum(gkf, axis=0, keepdims=True)
        bias_sums[2:3, qs] = jnp.sum(gvf, axis=0, keepdims=True)
        side = g // (GROUPS // 2)
        inner = pl.multiple_of((g - side * (GROUPS // 2)) * LANES, LANES)

        def put(ref):
            ref[:, pl.ds(inner, LANES)] = gqf.astype(bf16)
            ref[:, pl.ds(inner + D // 2, LANES)] = gkf.astype(bf16)
            ref[:, pl.ds(inner + D, LANES)] = gvf.astype(bf16)

        pl.when(side == p)(lambda: put(g_keep))
        pl.when(side != p)(lambda: put(g_send))


def input_grad_kernel(half, g_keep, g_send, wqkv, order_t, s_own, s_row, s_col, s_cor, total):
    p = half[0]
    for t in range(3):
        for ref, side in ((g_keep, p), (g_send, 1 - p)):
            cols = pl.ds(pl.multiple_of(t * D + side * (D // 2), D // 2), D // 2)
            term = mm_tb(ref[:, t * (D // 2) : (t + 1) * (D // 2)], wqkv[:, cols])
            if t == 0 and ref is g_keep:
                total[...] = term
            else:
                total[...] += term
    gs = total[...].astype(bf16)
    s_own[...] = mm(order_t[0:TOK], gs).astype(bf16)
    s_row[...] = mm(order_t[TOK : TOK + HALO], gs).astype(bf16)
    s_col[...] = mm(order_t[TOK + HALO : TOK + 2 * HALO], gs).astype(bf16)
    s_cor[...] = mm(order_t[TOK + 2 * HALO : CAT], gs).astype(bf16)


def weight_grad_kernel(a_own, a_other, g_own, g_other, out):
    a = jnp.concatenate((a_own[...], a_other[...]), axis=0)
    g = jnp.concatenate((g_own[...], g_other[...]), axis=0)
    out[...] = mm_ta(a, g).astype(bf16)


def finish_kernel(base, own, row, col, cor, spread, out):
    border = jnp.concatenate((col[...], cor[...]), axis=0)
    moved = own[...].astype(f32) + mm(spread[...], border)
    total = base[...].astype(f32) + moved
    out[HALO:, :] = total[HALO:].astype(bf16)
    out[:HALO, :] = (total[:HALO] + row[...].astype(f32)).astype(bf16)


def sds(shape, dtype):
    return jax.ShapeDtypeStruct(shape, dtype)


VM = pl.BlockSpec(memory_space=pltpu.VMEM)
SM = pl.BlockSpec(memory_space=pltpu.SMEM)


def call(kernel, outs, scratch=(), specs=None, flops=0, bytes_accessed=0):
    return pl.pallas_call(
        kernel,
        out_shape=outs,
        in_specs=specs,
        out_specs=jax.tree.map(lambda _: VM, outs),
        scratch_shapes=list(scratch),
        compiler_params=pltpu.CompilerParams(vmem_limit_bytes=VMEM_LIMIT),
        cost_estimate=pl.CostEstimate(flops=flops, bytes_accessed=bytes_accessed, transcendentals=0),
    )


def neighbour(by_row, by_col):
    rows, cols = lax.axis_size("row"), lax.axis_size("col")
    reps = lax.axis_size("rep")
    pairs = []
    for s in range(reps):
        for r in range(rows):
            for c in range(cols):
                to = (s * rows + (r + by_row) % rows) * cols + (c + by_col) % cols
                pairs.append(((s * rows + r) * cols + c, to))
    return pairs


def swap_cores(x):
    size = lax.axis_size("col")
    return lax.ppermute(x, "col", [(i, i ^ 1) for i in range(size)])


def weight_grad(a_own, a_other, g_own, g_other):
    width = g_own.shape[1]
    block = 256
    return pl.pallas_call(
        weight_grad_kernel,
        grid=(D // block,),
        out_shape=sds((D, width), bf16),
        in_specs=[
            pl.BlockSpec((TOK, block), lambda i: (0, i)),
            pl.BlockSpec((TOK, block), lambda i: (0, i)),
            pl.BlockSpec((TOK, width), lambda i: (0, 0)),
            pl.BlockSpec((TOK, width), lambda i: (0, 0)),
        ],
        out_specs=pl.BlockSpec((block, width), lambda i: (i, 0)),
        compiler_params=pltpu.CompilerParams(vmem_limit_bytes=VMEM_LIMIT),
        cost_estimate=pl.CostEstimate(flops=4 * TOK * D * width, bytes_accessed=4 * D * width, transcendentals=0),
    )(a_own, a_other, g_own, g_other)


def per_device(
    tokens, cotangent, row_field, col_field, qkv_weight, qkv_bias, logit_scale, position_bias,
    proj_weight, proj_bias, norm_gain, norm_shift,
):
    devices = lax.axis_size(AXES)
    order = jnp.asarray(window_order(), bf16)
    order_t = jnp.asarray(window_order().T, bf16)
    spread = jnp.asarray(border_spread(), bf16)
    mask = jnp.asarray(head_mask(), bf16)
    ones = jnp.asarray(head_sums(), bf16)

    both = jnp.stack((tokens[0], cotangent[0]))
    row_in = lax.ppermute(both[:, :SHIFT].reshape(2, HALO, D), AXES, neighbour(-1, 0))
    col_in = lax.ppermute(both[:, :, :SHIFT].reshape(2, HALO, D), AXES, neighbour(0, -1))
    cor_in = lax.ppermute(both[:, :SHIFT, :SHIFT].reshape(2, CORNER, D), AXES, neighbour(-1, -1))

    row_ids = lax.dynamic_slice_in_dim(jnp.roll(row_field[0], -SHIFT), lax.axis_index("row") * SIDE, SIDE)
    col_ids = lax.dynamic_slice_in_dim(jnp.roll(col_field[0], -SHIFT), lax.axis_index("col") * SIDE, SIDE)
    fields = jnp.stack((row_ids, col_ids))
    half = (lax.axis_index("col") % 2).astype(jnp.int32).reshape(1)
    scale = jnp.repeat(logit_scale, WIN2).reshape(GROUPS, WIDE)
    bias_t = position_bias.reshape(GROUPS, GROUP, WIN2, WIN2).transpose(0, 3, 1, 2).reshape(GROUPS, WIN2, WIDE)
    tok = tokens[0].reshape(TOK, D)
    cot = cotangent[0].reshape(TOK, D)

    x, qkv, att, mixed, gp, b_own, b_row, b_col, b_cor, sums = call(
        forward_kernel,
        (
            sds((TOK, D), bf16), sds((TOK, 3 * D), bf16), sds((GROUPS, WINDOWS, WIN2, WIDE), bf16),
            sds((TOK, D), bf16), sds((TOK, D), bf16), sds((TOK, D), bf16), sds((HALO, D), bf16),
            sds((HALO, D), bf16), sds((CORNER, D), bf16), sds((8, D), f32),
        ),
        [pltpu.VMEM((CAT, D), bf16), pltpu.VMEM((TOK, D), bf16), pltpu.VMEM((TOK, D), bf16)],
        [SM] + [VM] * 20,
        flops=3 * 10**9, bytes_accessed=16 * 2**20,
    )(
        fields, tok, row_in[0], col_in[0], cor_in[0], cot, row_in[1], col_in[1], cor_in[1],
        order, order_t, mask, ones, qkv_weight, qkv_bias.reshape(1, -1), scale, bias_t,
        proj_weight, proj_bias.reshape(1, -1), norm_gain.reshape(1, -1), norm_shift.reshape(1, -1),
    )
    x_other = swap_cores(x)
    mixed_other = swap_cores(mixed)
    gp_keep = lax.dynamic_slice_in_dim(gp, half[0] * (D // 2), D // 2, axis=1)
    gp_send = lax.dynamic_slice_in_dim(gp, (1 - half[0]) * (D // 2), D // 2, axis=1)
    gp_other = swap_cores(gp_send)
    proj_part = weight_grad(mixed, mixed_other, gp_keep, gp_other)
    proj_got = lax.all_to_all(proj_part.reshape(devices, -1, D // 2), AXES, 0, 0, tiled=True)

    def sent_back(own, row, col, cor, base):
        row = lax.ppermute(row, AXES, neighbour(1, 0))
        col = lax.ppermute(col, AXES, neighbour(0, 1))
        cor = lax.ppermute(cor, AXES, neighbour(1, 1))
        out = call(finish_kernel, sds((TOK, D), bf16), (), [VM] * 6, flops=10**8, bytes_accessed=2**21)(
            base, own, row, col, cor, spread
        )
        return out.reshape(1, SIDE, SIDE, D)

    block_out = sent_back(b_own, b_row, b_col, b_cor, tok)

    g_keep, g_send, pos, scale_sums, bias_sums = call(
        attention_grad_kernel,
        (
            sds((TOK, 3 * D // 2), bf16), sds((TOK, 3 * D // 2), bf16), sds((HEADS * WIN2, WIN2), f32),
            sds((GROUPS, WIDE), f32), sds((8, D), f32),
        ),
        [pltpu.VMEM((TOK, D), bf16)],
        [SM] + [VM] * 7,
        flops=10**9, bytes_accessed=8 * 2**20,
    )(half, qkv, att, gp, proj_weight, scale, mask, ones)
    g_other = swap_cores(g_send)
    qkv_part = weight_grad(x, x_other, g_keep, g_other)
    qkv_got = lax.all_to_all(qkv_part.reshape(devices, -1, 3 * D // 2), AXES, 0, 0, tiled=True)

    vector = jnp.concatenate((
        bias_sums[:3].reshape(-1), sums[:3].reshape(-1), scale_sums.reshape(HEADS, WIN2).sum(axis=1),
        jnp.zeros(8192 - 6 * D - HEADS, f32),
    ))
    vec_rows = 128 // devices
    pos_rows = HEADS * WIN2 // devices
    vector = jnp.pad(vector.reshape(devices, vec_rows, 64), ((0, 0), (0, pos_rows - vec_rows), (0, 0)))
    small = jnp.concatenate((pos.reshape(devices, pos_rows, WIN2), vector), axis=2).astype(bf16)
    small = lax.all_to_all(small, AXES, 0, 0, tiled=True)
    small = jnp.sum(small.astype(f32), axis=0).astype(bf16)
    small = lax.all_to_all(jnp.broadcast_to(small[None], (devices,) + small.shape), AXES, 0, 0, tiled=True)
    grad_position = small[:, :, :WIN2].astype(f32).reshape(HEADS, WIN2, WIN2)
    vector = small[:, :vec_rows, WIN2:].astype(f32).reshape(-1)

    s_own, s_row, s_col, s_cor = call(
        input_grad_kernel,
        (sds((TOK, D), bf16), sds((HALO, D), bf16), sds((HALO, D), bf16), sds((CORNER, D), bf16)),
        [pltpu.VMEM((TOK, D), f32)],
        [SM] + [VM] * 4,
        flops=2 * 10**9, bytes_accessed=9 * 2**20,
    )(half, g_keep, g_send, qkv_weight, order_t)
    grad_tokens = sent_back(s_own, s_row, s_col, s_cor, cot)

    def summed(got, width):
        total = jnp.sum(got.astype(f32).reshape(devices // 2, 2, -1, got.shape[-1]), axis=0)
        parts = total.reshape(2, total.shape[1], -1, D // 2)
        return parts.transpose(1, 2, 0, 3).reshape(total.shape[1], width)

    grad_qkv_weight = summed(qkv_got, 3 * D)
    grad_proj_weight = summed(proj_got, D)
    return (
        block_out, grad_tokens, grad_qkv_weight, grad_proj_weight, vector[: 3 * D], vector[3 * D : 4 * D],
        vector[4 * D : 5 * D], vector[5 * D : 6 * D], vector[6 * D : 6 * D + HEADS], grad_position,
    )


def solution(mesh):
    grid = P("rep", "row", "col", None)
    rows = P(AXES, None)
    return jax.shard_map(
        per_device,
        mesh=mesh,
        in_specs=(grid, grid, P("rep", None), P("rep", None)) + (P(),) * 8,
        out_specs=(grid, grid, rows, rows) + (P(),) * 6,
        check_vma=False,
    )
```

time: 954 us -> 193 us (0.20)
  waiting for transfers between devices: 687 us -> 72.8 us
  blocking collectives: 69.5 us -> 0 us
  local copies, waits for them, and re-layouts: 85.4 us -> 22.4 us
  Pallas kernels: 0 us -> 53.6 us
  matrix products: 45.7 us -> 0 us
  other arithmetic: 39 us -> 9.35 us
  starting transfers between devices: 7.91 us -> 33.3 us
  between operations: 14.7 us -> 1.01 us
    reduce_scatter x1 -> x0, waiting for transfers between devices: 662 us -> none  [per_device(): lax.psum_scatter(jnp.concatenate((qkv_part, proj_part), axis=1), ('rep',...]
    psum x1 -> x0, blocking collectives: 69.5 us -> none  [per_device(): lax.psum((partial_sums[0], partial_sums[1], partial_sums[2], partial_sums...]
    pallas_call x0 -> x7, Pallas kernels: none -> 53.6 us  [the longest x1 16.9 us: per_device(): call(forward_kernel, (sds((TOK, D), bf16), sds((TOK, 3 * D), bf16), sds((...]
    dot_general x12 -> x0, matrix products: 45.7 us -> none  [the longest x1 6.81 us: block_step(): jnp.einsum('nhij,nhjd->nhid', grad_cosine, key_cast, preferred_element_ty...]
    ppermute x4 -> x13, waiting for transfers between devices: 9.88 us -> 43.8 us  [the longest x2 36.9 us: sent_back(): cor = lax.ppermute(cor, AXES, neighbour(1, 1))]
    all_to_all x0 -> x4, waiting for transfers between devices: none -> 29 us  [the longest x1 13.4 us: per_device(): small = lax.all_to_all(small, AXES, 0, 0, tiled=True)]
    convert_element_type x3 -> x0, local copies, waits for them, and re-layouts: 24.3 us -> none  [the longest x2 21.4 us: block_step(): grad_qkv_low = grad_qkv.astype(jnp.bfloat16)]
    all_to_all x0 -> x4, starting transfers between devices: none -> 21 us  [the longest x1 6.8 us: per_device(): small = lax.all_to_all(small, AXES, 0, 0, tiled=True)]
  transfers between devices with their start and end apart: 6 -> 17, of which waited for: 5 -> 8; matrix products, arithmetic and copies ran while one was open for 7% -> 9% of each run, Pallas kernels for 0% -> 11%
where the time goes in v1:
time: 193 us; the launch traced here: 192 us
  waiting for transfers between devices  72.8 us (38%)
  Pallas kernels  53.6 us (28%)
  starting transfers between devices  33.3 us (17%)
  local copies, waits for them, and re-layouts  22.4 us (12%)
  other arithmetic  9.35 us (5%)
    ppermute x2, waiting for transfers between devices, sent_back(): cor = lax.ppermute(cor, AXES, neighbour(1, 1))  36.9 us
    pallas_call x1, Pallas kernels, per_device(): call(forward_kernel, (sds((TOK, D), bf16), sds((TOK, 3 * D), bf16), sds((...  16.9 us
    pallas_call x1, Pallas kernels, per_device(): call(attention_grad_kernel, (sds((TOK, 3 * D // 2), bf16), sds((TOK, 3 *...  15.9 us
    all_to_all x1, waiting for transfers between devices, per_device(): small = lax.all_to_all(small, AXES, 0, 0, tiled=True)  13.4 us
    pallas_call x2, Pallas kernels, weight_grad(): pl.pallas_call(weight_grad_kernel, grid=(D // block,), out_shape=sds((D,...  9.73 us
    all_to_all x1, waiting for transfers between devices, per_device(): lax.all_to_all(proj_part.reshape(devices, -1, D // 2), AXES, 0, 0, tiled=...  9.46 us
    all_to_all x1, starting transfers between devices, per_device(): small = lax.all_to_all(small, AXES, 0, 0, tiled=True)  6.8 us
    unnamed x47, local copies, waits for them, and re-layouts  6.27 us
  transfers between devices with their start and end apart: 17, of which 8 were waited for; matrix products, arithmetic and copies ran while one was open for 9% of the time, Pallas kernels for 11%

profile of v1, /device:TPU:0, one launch (start us, length us, event | category | flops | bytes accessed | tf_op | source)
XLA Modules:
  0.0 192.4 jit_solution(10082270095839807305)
XLA Ops:
  3.0 6.2 %collective-permute-start.2 = (bf16[2,16,1024]{2,1,0:T(8,128)(2,1)S(1)}, bf16[2,16,1024]{2,1,0:T(8,128)(2,1)S(1)}, u32[]{:S(2)}, u32[]{:S(2)}) collective-permute-start(bf16[2,16,1024]{2,1,0:T(8,128)(2,1)S(1)} %reshape.127), channel_id=1, source_target_pairs={{0,63},{1,32},{2,33},{3,34},{4,35},{5,36},{6,37},{7,38},{8,39},{9,... | collective-permute-start | bytes 196616 | tf_op jit(solution)/shard_map/ppermute | solution.py:363
  12.9 1.4 reshape.130.bias_t
  15.7 2.8 %collective-permute-done = bf16[2,64,1024]{2,1,0:T(8,128)(2,1)S(1)} collective-permute-done((bf16[2,64,1024]{2,1,0:T(8,128)(2,1)S(1)}, bf16[2,64,1024]{2,1,0:T(8,128)(2,1)S(1)}, u32[]{:S(2)}, u32[]{:S(2)}) %collective-permute-start) | collective-permute-done | bytes 262176 | tf_op jit(solution)/shard_map/ppermute | solution.py:361
  19.2 16.9 %shard_map.240 = (bf16[256,1024]{1,0:T(8,128)(2,1)}, bf16[256,3072]{1,0:T(8,128)(2,1)}, bf16[8,4,64,256]{3,2,1,0:T(8,128)(2,1)}, bf16[256,1024]{1,0:T(8,128)(2,1...) custom-call(s32[2,16]{1,0:T(2,128)} %pad_add_fusion.1.fields, ...), custom_call_target="tpu_custom_call" | custom-call | flops 3000000000 | bytes 16777216 | tf_op jit(solution)/shard_map/pallas_call | solution.py:374
  36.9 15.9 %shard_map.242 = (bf16[256,1536]{1,0:T(8,128)(2,1)}, bf16[256,1536]{1,0:T(8,128)(2,1)}, f32[2048,64]{1,0:T(8,128)}, f32[8,256]{1,0:T(8,128)}, f32[8,1024]{1,0:T(8,128)}) custom-call(s32[1]{0:T(128)} %bitcast.23.half, bf16[256,3072]{1,0:T(8,128)(2,1)} %get-tuple-element.33.qkv, bf16[8,4,64,256]{3,2,1,0:T(8,128)(2,1)} %get-tuple-element.34.att, ...), custom_call_target="tpu_custom_call" | custom-call | flops 1000000000 | bytes 8388608 | tf_op jit(solution)/shard_map/pallas_call | solution.py:408
  57.5 6.8 %all-to-all-start.2 = ((bf16[128,16,128]{2,1,0:T(8,128)(2,1)}), bf16[128,16,128]{2,1,0:T(8,128)(2,1)S(1)}, u32[]{:S(2)}, u32[]{:S(2)}) async-start(bf16[128,16,128]{2,1,0:T(8,128)(2,1)} %copy.44), calls=%async_computation.2 | async-start | bytes 1048576 | tf_op jit(solution)/shard_map/all_to_all | solution.py:430
  64.5 13.4 %all-to-all-done.2 = bf16[128,16,128]{2,1,0:T(8,128)(2,1)S(1)} async-done(((bf16[128,16,128]{2,1,0:T(8,128)(2,1)}), bf16[128,16,128]{2,1,0:T(8,128)(2,1)S(1)}, u32[]{:S(2)}, u32[]{:S(2)}) %all-to-all-start.2) | async-done | bytes 524320 | tf_op jit(solution)/shard_map/all_to_all | solution.py:430
  78.9 4.7 %all-to-all-start.3 = ((bf16[128,16,128]{2,1,0:T(8,128)(2,1)}), bf16[128,16,128]{2,1,0:T(8,128)(2,1)S(1)}, u32[]{:S(2)}, u32[]{:S(2)}) async-start(bf16[128,16,128]{2,1,0:T(8,128)(2,1)} %broadcast_in_dim.20), calls=%async_computation.3 | async-start | bytes 1048576 | tf_op jit(solution)/shard_map/all_to_all | solution.py:432
  84.4 1.5 collective-permute-done.12.g_other
  86.8 4.2 %shard_map.246 = bf16[1024,512]{1,0:T(8,128)(2,1)} custom-call(bf16[256,1024]{1,0:T(8,128)(2,1)} %get-tuple-element.43.a_own, bf16[256,1024]{1,0:T(8,128)(2,1)} %copy-done.6, bf16[256,512]{1,0:T(8,128)(2,1)} %get-tuple-element.52.g_own, bf16[256,512]{1,0:T(8,128)(2,1)} %copy-done.7), custom_call_target="tpu_custom_call" | custom-call | flops 536870912 | bytes 2097152 | tf_op jit(solution)/shard_map/pallas_call | solution.py:333
  91.0 6.1 %all-to-all-done.3 = bf16[128,16,128]{2,1,0:T(8,128)(2,1)S(1)} async-done(((bf16[128,16,128]{2,1,0:T(8,128)(2,1)}), bf16[128,16,128]{2,1,0:T(8,128)(2,1)S(1)}, u32[]{:S(2)}, u32[]{:S(2)}) %all-to-all-start.3) | async-done | bytes 524320 | tf_op jit(solution)/shard_map/all_to_all | solution.py:432
  97.9 4.8 %all-to-all-start.1 = ((bf16[128,8,512]{2,1,0:T(8,128)(2,1)}), bf16[128,8,512]{2,1,0:T(8,128)(2,1)S(1)}, u32[]{:S(2)}, u32[]{:S(2)}) async-start(bf16[128,8,512]{2,1,0:T(8,128)(2,1)} %bitcast.60), calls=%async_computation.1 | async-start | bytes 2097152 | tf_op jit(solution)/shard_map/all_to_all | solution.py:395
  103.3 2.5 %collective-permute-done.9.a_other = bf16[256,1024]{1,0:T(8,128)(2,1)S(1)} collective-permute-done((bf16[256,1024]{1,0:T(8,128)(2,1)S(1)}, bf16[256,1024]{1,0:T(8,128)(2,1)S(1)}, u32[]{:S(2)}, u32[]{:S(2)}) %collective-permute-start.9) | collective-permute-done | bytes 524320 | tf_op jit(solution)/shard_map/ppermute | solution.py:327
  106.9 5.5 %shard_map.245 = bf16[1024,1536]{1,0:T(8,128)(2,1)} custom-call(bf16[256,1024]{1,0:T(8,128)(2,1)} %get-tuple-element.42.a_own, bf16[256,1024]{1,0:T(8,128)(2,1)} %copy-done.18, bf16[256,1536]{1,0:T(8,128)(2,1)} %get-tuple-element.36.g_keep.g_own, bf16[256,1536]{1,0:T(8,128)(2,1)} %copy-done.16), custom_call_target="tpu_custom_call" | custom-call | flops 1610612736 | bytes 6291456 | tf_op jit(solution)/shard_map/pallas_call | solution.py:333
  112.4 9.5 %all-to-all-done.1 = bf16[128,8,512]{2,1,0:T(8,128)(2,1)S(1)} async-done(((bf16[128,8,512]{2,1,0:T(8,128)(2,1)}), bf16[128,8,512]{2,1,0:T(8,128)(2,1)S(1)}, u32[]{:S(2)}, u32[]{:S(2)}) %all-to-all-start.1) | async-done | bytes 1048608 | tf_op jit(solution)/shard_map/all_to_all | solution.py:395
  122.8 4.7 %all-to-all-start = ((bf16[128,8,1536]{2,1,0:T(8,128)(2,1)}), bf16[128,8,1536]{2,1,0:T(8,128)(2,1)S(1)}, u32[]{:S(2)}, u32[]{:S(2)}) async-start(bf16[128,8,1536]{2,1,0:T(8,128)(2,1)} %bitcast.62), calls=%async_computation | async-start | bytes 6291456 | tf_op jit(solution)/shard_map/all_to_all | solution.py:420
  128.7 6.2 %shard_map.243 = (bf16[256,1024]{1,0:T(8,128)(2,1)}, bf16[64,1024]{1,0:T(8,128)(2,1)}, bf16[64,1024]{1,0:T(8,128)(2,1)}, bf16[16,1024]{1,0:T(8,128)(2,1)}) custom-call(s32[1]{0:T(128)} %bitcast.23.half, bf16[256,1536]{1,0:T(8,128)(2,1)} %get-tuple-element.36.g_keep.g_own, bf16[256,1536]{1,0:T(8,128)(2,1)} %get-tuple-element.37.g_send, ...), custom_call_target="tpu_custom_call" | custom-call | flops 2000000000 | bytes 9437184 | tf_op jit(solution)/shard_map/pallas_call | solution.py:436
  136.5 1.6 collective-permute-start.5
  138.2 32.2 %collective-permute-done.5.cor = bf16[16,1024]{1,0:T(8,128)(2,1)S(1)} collective-permute-done((bf16[16,1024]{1,0:T(8,128)(2,1)S(1)}, bf16[16,1024]{1,0:T(8,128)(2,1)S(1)}, u32[]{:S(2)}, u32[]{:S(2)}) %collective-permute-start.5) | collective-permute-done | bytes 32800 | tf_op jit(solution)/shard_map/ppermute | solution.py:400
  171.1 2.4 %shard_map.241 = bf16[256,1024]{1,0:T(8,128)(2,1)} custom-call(bf16[256,1024]{1,0:T(8,128)(2,1)} %bitcast.56, bf16[256,1024]{1,0:T(8,128)(2,1)} %get-tuple-element.29.own, bf16[64,1024]{1,0:T(8,128)(2,1)} %copy-done.9, bf16[64,1024]{1,0:T(8,128)(2,1)} %copy-done.11, bf16[16,1024]{1,0:T(8,128)(2,1)} %copy-done.13, bf16[256,80]{1,0:T(8,128)(2,1)} %constant.51.clone.spread), custom_call_target="tpu_custom_call" | custom-call | flops 100000000 | bytes 2097152 | tf_op jit(solution)/shard_map/pallas_call | solution.py:401
  173.5 4.7 %collective-permute-done.8.cor = bf16[16,1024]{1,0:T(8,128)(2,1)S(1)} collective-permute-done((bf16[16,1024]{1,0:T(8,128)(2,1)}, bf16[16,1024]{1,0:T(8,128)(2,1)S(1)}, u32[]{:S(2)}, u32[]{:S(2)}) %collective-permute-start.8) | collective-permute-done | bytes 32800 | tf_op jit(solution)/shard_map/ppermute | solution.py:400
  178.9 2.4 %shard_map.244 = bf16[256,1024]{1,0:T(8,128)(2,1)} custom-call(bf16[256,1024]{1,0:T(8,128)(2,1)} %bitcast.58, bf16[256,1024]{1,0:T(8,128)(2,1)} %get-tuple-element.38.own, bf16[64,1024]{1,0:T(8,128)(2,1)} %copy-done.8, bf16[64,1024]{1,0:T(8,128)(2,1)} %copy-done.10, bf16[16,1024]{1,0:T(8,128)(2,1)} %copy-done.12, bf16[256,80]{1,0:T(8,128)(2,1)} %constant.51.clone.spread), custom_call_target="tpu_custom_call" | custom-call | flops 100000000 | bytes 2097152 | tf_op jit(solution)/shard_map/pallas_call | solution.py:401
  186.9 2.1 %bitcast_convert_fusion = f32[32,64,64]{2,1,0:T(8,128)} fusion(bf16[32,64,64]{2,1,0:T(8,128)(2,1)} %bitcast.63), kind=kLoop, calls=%fused_computation.5 | loop fusion | flops 131072 | bytes 786432 | tf_op jit(solution)/shard_map/reshape | solution.py:433
  189.1 2.0 %convert_reduce_fusion.1 = f32[2,8,512]{2,1,0:T(8,128)} fusion(bf16[64,2,8,512]{3,2,1,0:T(8,128)(2,1)} %bitcast.59), kind=kLoop, calls=%fused_computation.1 | loop fusion | flops 1040384 | bytes 1081344 | tf_op jit(solution)/shard_map/reduce_sum | solution.py:446
  (119 shorter events, 30.8 us)
Async XLA Ops:
  0.7 10.1 %copy-start.14 = (s32[1,512]{1,0:T(1,128)S(1)}, s32[1,512]{1,0:T(1,128)}, u32[]{:S(2)}) copy-start(s32[1,512]{1,0:T(1,128)} %param.20) | copy-start | bytes 6148
  0.7 11.0 %copy-start.15 = (f32[32]{0:T(128)S(1)}, f32[32]{0:T(128)}, u32[]{:S(2)}) copy-start(f32[32]{0:T(128)} %param.23) | copy-start | bytes 388
  0.7 11.8 %copy-start.3 = (f32[32,64,64]{2,1,0:T(8,128)S(1)}, f32[32,64,64]{2,1,0:T(8,128)}, u32[]{:S(2)}) copy-start(f32[32,64,64]{2,1,0:T(8,128)} %param.24) | copy-start | bytes 1572868
  3.0 11.3 %collective-permute-start.2 = (bf16[2,16,1024]{2,1,0:T(8,128)(2,1)S(1)}, bf16[2,16,1024]{2,1,0:T(8,128)(2,1)S(1)}, u32[]{:S(2)}, u32[]{:S(2)}) collective-permute-start(bf16[2,16,1024]{2,1,0:T(8,128)(2,1)S(1)} %reshape.127), channel_id=1, source_target_pairs={{0,63},{1,32},{2,33},{3,34},{4,35},{5,36},{6,37},{7,38},{8,39},{9,... | collective-permute-start | bytes 196616 | tf_op jit(solution)/shard_map/ppermute | solution.py:363
  9.6 5.4 %collective-permute-start.1 = (bf16[2,64,1024]{2,1,0:T(8,128)(2,1)S(1)}, bf16[2,64,1024]{2,1,0:T(8,128)(2,1)S(1)}, u32[]{:S(2)}, u32[]{:S(2)}) collective-permute-start(bf16[2,64,1024]{2,1,0:T(8,128)(2,1)S(1)} %copy.40), channel_id=1, source_target_pairs={{0,31},{1,0},{2,1},{3,2},{4,3},{5,4},{6,5},{7,6},{8,7},{9,8},{10,9... | collective-permute-start | bytes 786440 | tf_op jit(solution)/shard_map/ppermute | solution.py:362
  10.5 8.0 %collective-permute-start = (bf16[2,64,1024]{2,1,0:T(8,128)(2,1)S(1)}, bf16[2,64,1024]{2,1,0:T(8,128)(2,1)S(1)}, u32[]{:S(2)}, u32[]{:S(2)}) collective-permute-start(bf16[2,64,1024]{2,1,0:T(8,128)(2,1)S(1)} %bitcast.70), channel_id=1, source_target_pairs={{0,32},{1,33},{2,34},{3,35},{4,36},{5,37},{6,38},{7,39},{8,40},{9,... | collective-permute-start | bytes 786440 | tf_op jit(solution)/shard_map/ppermute | solution.py:361
  52.8 11.5 %copy-start.5 = (bf16[256,1024]{1,0:T(8,128)(2,1)S(1)}, bf16[256,1024]{1,0:T(8,128)(2,1)}, u32[]{:S(2)}) copy-start(bf16[256,1024]{1,0:T(8,128)(2,1)} %get-tuple-element.43.a_own) | copy-start | bytes 1572868
  54.2 29.4 %copy-start.2 = (bf16[256,1024]{1,0:T(8,128)(2,1)S(1)}, bf16[256,1024]{1,0:T(8,128)(2,1)}, u32[]{:S(2)}) copy-start(bf16[256,1024]{1,0:T(8,128)(2,1)} %get-tuple-element.35.gp) | copy-start | bytes 1572868
  57.5 20.3 %all-to-all-start.2 = ((bf16[128,16,128]{2,1,0:T(8,128)(2,1)}), bf16[128,16,128]{2,1,0:T(8,128)(2,1)S(1)}, u32[]{:S(2)}, u32[]{:S(2)}) async-start(bf16[128,16,128]{2,1,0:T(8,128)(2,1)} %copy.44), calls=%async_computation.2 | async-start | bytes 1048576 | tf_op jit(solution)/shard_map/all_to_all | solution.py:430
  64.4 21.6 %collective-permute-start.11 = (bf16[256,1024]{1,0:T(8,128)(2,1)S(1)}, bf16[256,1024]{1,0:T(8,128)(2,1)S(1)}, u32[]{:S(2)}, u32[]{:S(2)}) collective-permute-start(bf16[256,1024]{1,0:T(8,128)(2,1)S(1)} %copy-done.5), channel_id=1, source_target_pairs={{0,1},{1,0},{2,3},{3,2},{4,5},{5,4},{6,7},{7,6},{8,9},{9,8},{10,11... | collective-permute-start | bytes 1572872 | tf_op jit(solution)/shard_map/ppermute | solution.py:327
  78.9 18.2 %all-to-all-start.3 = ((bf16[128,16,128]{2,1,0:T(8,128)(2,1)}), bf16[128,16,128]{2,1,0:T(8,128)(2,1)S(1)}, u32[]{:S(2)}, u32[]{:S(2)}) async-start(bf16[128,16,128]{2,1,0:T(8,128)(2,1)} %broadcast_in_dim.20), calls=%async_computation.3 | async-start | bytes 1048576 | tf_op jit(solution)/shard_map/all_to_all | solution.py:432
  83.6 19.2 %copy-start.4 = (bf16[256,1536]{1,0:T(8,128)(2,1)S(1)}, bf16[256,1536]{1,0:T(8,128)(2,1)}, u32[]{:S(2)}) copy-start(bf16[256,1536]{1,0:T(8,128)(2,1)} %get-tuple-element.37.g_send) | copy-start | bytes 2359300
  83.6 19.2 %copy-start.17 = (bf16[256,1024]{1,0:T(8,128)(2,1)S(1)}, bf16[256,1024]{1,0:T(8,128)(2,1)}, u32[]{:S(2)}) copy-start(bf16[256,1024]{1,0:T(8,128)(2,1)} %get-tuple-element.42.a_own) | copy-start | bytes 1572868
  84.4 1.5 collective-permute-start.12
  97.9 24.0 %all-to-all-start.1 = ((bf16[128,8,512]{2,1,0:T(8,128)(2,1)}), bf16[128,8,512]{2,1,0:T(8,128)(2,1)S(1)}, u32[]{:S(2)}, u32[]{:S(2)}) async-start(bf16[128,8,512]{2,1,0:T(8,128)(2,1)} %bitcast.60), calls=%async_computation.1 | async-start | bytes 2097152 | tf_op jit(solution)/shard_map/all_to_all | solution.py:395
  102.7 3.1 %collective-permute-start.10 = (bf16[256,1536]{1,0:T(8,128)(2,1)S(1)}, bf16[256,1536]{1,0:T(8,128)(2,1)S(1)}, u32[]{:S(2)}, u32[]{:S(2)}) collective-permute-start(bf16[256,1536]{1,0:T(8,128)(2,1)S(1)} %copy-done.4), channel_id=1, source_target_pairs={{0,1},{1,0},{2,3},{3,2},{4,5},{5,4},{6,7},{7,6},{8,9},{9,8},{10,11... | collective-permute-start | bytes 2359304 | tf_op jit(solution)/shard_map/ppermute | solution.py:327
  102.9 3.0 %collective-permute-start.9 = (bf16[256,1024]{1,0:T(8,128)(2,1)S(1)}, bf16[256,1024]{1,0:T(8,128)(2,1)S(1)}, u32[]{:S(2)}, u32[]{:S(2)}) collective-permute-start(bf16[256,1024]{1,0:T(8,128)(2,1)S(1)} %copy-done.17), channel_id=1, source_target_pairs={{0,1},{1,0},{2,3},{3,2},{4,5},{5,4},{6,7},{7,6},{8,9},{9,8},{10,11... | collective-permute-start | bytes 1572872 | tf_op jit(solution)/shard_map/ppermute | solution.py:327
  122.8 68.2 %all-to-all-start = ((bf16[128,8,1536]{2,1,0:T(8,128)(2,1)}), bf16[128,8,1536]{2,1,0:T(8,128)(2,1)S(1)}, u32[]{:S(2)}, u32[]{:S(2)}) async-start(bf16[128,8,1536]{2,1,0:T(8,128)(2,1)} %bitcast.62), calls=%async_computation | async-start | bytes 6291456 | tf_op jit(solution)/shard_map/all_to_all | solution.py:420
  127.5 42.9 %collective-permute-start.3 = (bf16[64,1024]{1,0:T(8,128)(2,1)S(1)}, bf16[64,1024]{1,0:T(8,128)(2,1)S(1)}, u32[]{:S(2)}, u32[]{:S(2)}) collective-permute-start(bf16[64,1024]{1,0:T(8,128)(2,1)S(1)} %copy-done.20), channel_id=1, source_target_pairs={{0,32},{1,33},{2,34},{3,35},{4,36},{5,37},{6,38},{7,39},{8,40},{9,... | collective-permute-start | bytes 393224 | tf_op jit(solution)/shard_map/ppermute | solution.py:398
  128.7 41.7 %collective-permute-start.4 = (bf16[64,1024]{1,0:T(8,128)(2,1)S(1)}, bf16[64,1024]{1,0:T(8,128)(2,1)S(1)}, u32[]{:S(2)}, u32[]{:S(2)}) collective-permute-start(bf16[64,1024]{1,0:T(8,128)(2,1)S(1)} %copy-done.19), channel_id=1, source_target_pairs={{0,1},{1,2},{2,3},{3,4},{4,5},{5,6},{6,7},{7,8},{8,9},{9,10},{10,1... | collective-permute-start | bytes 393224 | tf_op jit(solution)/shard_map/ppermute | solution.py:399
  134.9 43.2 %collective-permute-start.6 = (bf16[64,1024]{1,0:T(8,128)(2,1)}, bf16[64,1024]{1,0:T(8,128)(2,1)S(1)}, u32[]{:S(2)}, u32[]{:S(2)}) collective-permute-start(bf16[64,1024]{1,0:T(8,128)(2,1)} %get-tuple-element.39), channel_id=1, source_target_pairs={{0,32},{1,33},{2,34},{3,35},{4,36},{5,37},{6,38},{7,39},{8,40},{9,... | collective-permute-start | bytes 393224 | tf_op jit(solution)/shard_map/ppermute | solution.py:398
  135.9 42.3 %collective-permute-start.7 = (bf16[64,1024]{1,0:T(8,128)(2,1)}, bf16[64,1024]{1,0:T(8,128)(2,1)S(1)}, u32[]{:S(2)}, u32[]{:S(2)}) collective-permute-start(bf16[64,1024]{1,0:T(8,128)(2,1)} %get-tuple-element.40), channel_id=1, source_target_pairs={{0,1},{1,2},{2,3},{3,4},{4,5},{5,6},{6,7},{7,8},{8,9},{9,10},{10,1... | collective-permute-start | bytes 393224 | tf_op jit(solution)/shard_map/ppermute | solution.py:399
  136.5 33.8 %collective-permute-start.5 = (bf16[16,1024]{1,0:T(8,128)(2,1)S(1)}, bf16[16,1024]{1,0:T(8,128)(2,1)S(1)}, u32[]{:S(2)}, u32[]{:S(2)}) collective-permute-start(bf16[16,1024]{1,0:T(8,128)(2,1)S(1)} %copy-done.21), channel_id=1, source_target_pairs={{0,33},{1,34},{2,35},{3,36},{4,37},{5,38},{6,39},{7,40},{8,41},{9,... | collective-permute-start | bytes 98312 | tf_op jit(solution)/shard_map/ppermute | solution.py:400
  170.4 7.8 %collective-permute-start.8 = (bf16[16,1024]{1,0:T(8,128)(2,1)}, bf16[16,1024]{1,0:T(8,128)(2,1)S(1)}, u32[]{:S(2)}, u32[]{:S(2)}) collective-permute-start(bf16[16,1024]{1,0:T(8,128)(2,1)} %get-tuple-element.41), channel_id=1, source_target_pairs={{0,33},{1,34},{2,35},{3,36},{4,37},{5,38},{6,39},{7,40},{8,41},{9,... | collective-permute-start | bytes 98312 | tf_op jit(solution)/shard_map/ppermute | solution.py:400
  (16 other events, 39.5 us)

commit v2 on v1

v2 whole, which is shorter than its diff:
```python
import functools

import jax
import jax.numpy as jnp
import numpy as np
from jax import lax
from jax.experimental import pallas as pl
from jax.experimental.pallas import tpu as pltpu
from jax.sharding import PartitionSpec as P

HEADS = 32
WIN = 8
SHIFT = 4
SIDE = 16
TOK = SIDE * SIDE
D = 1024
HALO = SIDE * SHIFT
CORNER = SHIFT * SHIFT
CAT = TOK + 2 * HALO + CORNER
WIN2 = WIN * WIN
WINDOWS = TOK // WIN2
GROUP = 4
GROUPS = HEADS // GROUP
LANES = 128
WIDE = GROUP * WIN2
AXES = ("rep", "row", "col")

norm_epsilon = 1e-05
unit_floor = 1e-12
f32 = jnp.float32
bf16 = jnp.bfloat16
VMEM_LIMIT = 56 * 1024 * 1024


def window_order():
    order = np.zeros((TOK, CAT), np.float32)
    for r in range(SIDE):
        for c in range(SIDE):
            n = ((r // WIN) * 2 + c // WIN) * WIN2 + (r % WIN) * WIN + c % WIN
            rr, cc = r + SHIFT, c + SHIFT
            if rr < SIDE and cc < SIDE:
                m = rr * SIDE + cc
            elif cc < SIDE:
                m = TOK + (rr - SIDE) * SIDE + cc
            elif rr < SIDE:
                m = TOK + HALO + rr * SHIFT + (cc - SIDE)
            else:
                m = TOK + 2 * HALO + (rr - SIDE) * SHIFT + (cc - SIDE)
            order[n, m] = 1.0
    return order


def border_spread():
    spread = np.zeros((TOK, HALO + CORNER), np.float32)
    for r in range(SIDE):
        for c in range(SHIFT):
            spread[r * SIDE + c, r * SHIFT + c] = 1.0
    for r in range(SHIFT):
        for c in range(SHIFT):
            spread[r * SIDE + c, HALO + r * SHIFT + c] = 1.0
    return spread


def head_mask():
    rows = np.arange(WIDE)[:, None] // WIN2
    cols = np.arange(LANES)[None, :] // (LANES // GROUP)
    return (rows == cols).astype(np.float32)


def head_sums():
    a = np.arange(2 * LANES)[:, None] % LANES // (LANES // GROUP)
    b = np.arange(LANES)[None, :] // (LANES // GROUP)
    return (a == b).astype(np.float32)


def mm(a, b):
    return jnp.dot(a, b, preferred_element_type=f32)


def mm_tb(a, b):
    return lax.dot_general(a, b, (((1,), (1,)), ((), ())), preferred_element_type=f32)


def mm_ta(a, b):
    return lax.dot_general(a, b, (((0,), (0,)), ((), ())), preferred_element_type=f32)


def segment_sums(values, ones):
    high = values.astype(bf16)
    low = (values - high.astype(f32)).astype(bf16)
    return mm(jnp.concatenate((high, low), axis=1), ones)


def inverse_length(raw, ones):
    total = segment_sums(raw * raw, ones)
    return 1.0 / jnp.maximum(jnp.sqrt(total), unit_floor)


def stacked_heads(x, mask):
    return jnp.concatenate((x, x, x, x), axis=0) * mask


def pack_kernel(tok, cot, spread_t, row, col, cor):
    for n, ref in enumerate((tok, cot)):
        border = mm(spread_t[...], ref[...]).astype(bf16)
        row[n] = ref[0:HALO, :]
        col[n] = border[:HALO]
        cor[n] = border[HALO:]


def put_back(order_t, src, own, row, col, cor):
    own[...] = mm(order_t[0:TOK], src).astype(bf16)
    row[...] = mm(order_t[TOK : TOK + HALO], src).astype(bf16)
    col[...] = mm(order_t[TOK + HALO : TOK + 2 * HALO], src).astype(bf16)
    cor[...] = mm(order_t[TOK + 2 * HALO : CAT], src).astype(bf16)


def local_kernel(
    place, row_field, col_field, logit_scale, tok, cot, row_in, col_in, cor_in, order, order_t, mask_ref, ones_ref,
    wqkv_hbm, bqkv, bias_hbm, wproj_hbm, bproj, gain, shift,
    keep, send, b_own, b_row, b_col, b_cor, small,
    wqkv, wproj, bias_t, cat, qkv, att, units, inverses, grad, wide, branch, pos, vec, sems,
):
    loads = [
        pltpu.make_async_copy(wqkv_hbm.at[:, pl.ds(t * D, D)], wqkv.at[:, pl.ds(t * D, D)], sems.at[t])
        for t in range(3)
    ]
    loads.append(pltpu.make_async_copy(bias_hbm, bias_t, sems.at[3]))
    loads.append(pltpu.make_async_copy(wproj_hbm, wproj, sems.at[4]))
    for load in loads:
        load.start()

    p = place[2]
    mixed_at, gp_at, g_at = D, 2 * D, 2 * D + D // 2
    for n, ref in enumerate((tok, cot)):
        cat[0:TOK] = ref[...]
        cat[TOK : TOK + HALO] = row_in[n]
        cat[TOK + HALO : TOK + 2 * HALO] = col_in[n]
        cat[TOK + 2 * HALO : CAT] = cor_in[n]
        moved = mm(order[...], cat[...]).astype(bf16)
        if n == 0:
            keep[:, 0:D] = moved
            send[:, 0:D] = moved
        else:
            grad[...] = moved

    sub = lax.broadcasted_iota(jnp.int32, (WIN2, WIDE), 0)
    lane = lax.broadcasted_iota(jnp.int32, (WIN2, WIDE), 1) % WIN2
    row_ids, col_ids = [], []
    for i in range(SIDE):
        row_ids.append(row_field[0, lax.rem(place[0] + SHIFT + i, row_field.shape[1])] * 1024)
        col_ids.append(col_field[0, lax.rem(place[1] + SHIFT + i, col_field.shape[1])])

    def spread_ids(ids, index):
        out = jnp.zeros((WIN2, WIDE), jnp.int32)
        for i in range(WIN):
            out = jnp.where(index == i, ids[i], out)
        return out

    row_same, col_same = [], []
    for n in range(2):
        part = slice(n * WIN, (n + 1) * WIN)
        row_same.append(spread_ids(row_ids[part], sub // WIN) == spread_ids(row_ids[part], lane // WIN))
        col_same.append(spread_ids(col_ids[part], sub % WIN) == spread_ids(col_ids[part], lane % WIN))
    allowed = [(row_same[w // 2] & col_same[w % 2]).astype(f32) for w in range(WINDOWS)]
    mask = mask_ref[...]
    ones = ones_ref[...]
    head_lane = lax.broadcasted_iota(jnp.int32, (WIN2, LANES), 1) // (LANES // GROUP)
    wide_lane = lax.broadcasted_iota(jnp.int32, (1, WIDE), 1) // WIN2

    def own_heads(full):
        out = full[:WIN2]
        for h in range(1, GROUP):
            out = jnp.where(head_lane == h, full[h * WIN2 : (h + 1) * WIN2], out)
        return out

    def scale_of(g):
        out = jnp.zeros((1, WIDE), f32)
        for h in range(GROUP):
            out = jnp.where(wide_lane == h, logit_scale[g * GROUP + h], out)
        return out

    for t in range(3):
        loads[t].wait()

        @pl.loop(0, 2)
        def _(n):
            cols = pl.ds(pl.multiple_of(t * D + n * 512, 512), 512)
            qkv[:, cols] = (mm(keep[:, 0:D], wqkv[:, cols]) + bqkv[:, cols]).astype(bf16)

    loads[3].wait()

    @pl.loop(0, GROUPS)
    def _(g):
        at = pl.multiple_of(g * LANES, LANES)
        qs = pl.ds(at, LANES)
        q = qkv[:, qs].astype(f32)
        k = qkv[:, pl.ds(at + D, LANES)].astype(f32)
        v = qkv[:, pl.ds(at + 2 * D, LANES)]
        q_inv = inverse_length(q, ones)
        k_inv = inverse_length(k, ones)
        qu = (q * q_inv).astype(bf16)
        ku = (k * k_inv).astype(bf16)
        inverses[0, :, qs] = q_inv
        inverses[1, :, qs] = k_inv
        units[0, :, qs] = qu
        units[1, :, qs] = ku
        sc = scale_of(g)
        bias = bias_t[g]
        for w in range(WINDOWS):
            rows = slice(w * WIN2, (w + 1) * WIN2)
            cosine = mm_tb(ku[rows], stacked_heads(qu[rows], mask))
            weights = jnp.exp(sc * cosine + bias) * allowed[w]
            total = jnp.sum(weights, axis=0, keepdims=True)
            attention = (weights * (1.0 / total)).astype(bf16)
            att[g, w] = attention
            mixed = own_heads(mm_ta(attention, v[rows])).astype(bf16)
            keep[rows, pl.ds(at + mixed_at, LANES)] = mixed
            send[rows, pl.ds(at + mixed_at, LANES)] = mixed

    loads[4].wait()

    @pl.loop(0, 4)
    def _(n):
        cols = pl.ds(pl.multiple_of(n * 256, 256), 256)
        wide[:, cols] = mm(keep[:, mixed_at : mixed_at + D], wproj[:, cols]) + bproj[:, cols]

    gain_v = gain[...]
    shift_v = shift[...]
    vec[...] = jnp.zeros_like(vec)

    @pl.loop(0, TOK // 32)
    def _(n):
        rows = pl.ds(pl.multiple_of(n * 32, 32), 32)
        projected = wide[rows, :]
        centre = projected - jnp.mean(projected, axis=-1, keepdims=True)
        inv_std = lax.rsqrt(jnp.mean(centre * centre, axis=-1, keepdims=True) + norm_epsilon)
        normed = centre * inv_std
        branch[rows, :] = (normed * gain_v + shift_v).astype(bf16)
        go = grad[rows, :].astype(f32)
        gn = go * gain_v
        gpf = inv_std * (
            gn - jnp.mean(gn, axis=-1, keepdims=True) - normed * jnp.mean(gn * normed, axis=-1, keepdims=True)
        )
        grad[rows, :] = gpf.astype(bf16)
        vec[:, 3 * D : 4 * D] += jnp.sum(gpf, axis=0, keepdims=True)
        vec[:, 4 * D : 5 * D] += jnp.sum(go * normed, axis=0, keepdims=True)
        vec[:, 5 * D : 6 * D] += jnp.sum(go, axis=0, keepdims=True)

    put_back(order_t, branch[...], b_own, b_row, b_col, b_cor)
    half = D // 2
    keep[:, gp_at : gp_at + half] = grad[:, pl.ds(pl.multiple_of(p * half, half), half)]
    send[:, gp_at : gp_at + half] = grad[:, pl.ds(pl.multiple_of((1 - p) * half, half), half)]

    @pl.loop(0, 4)
    def _(n):
        cols = pl.ds(pl.multiple_of(n * 256, 256), 256)
        branch[:, cols] = mm_tb(grad[...], wproj[cols, :]).astype(bf16)

    @pl.loop(0, GROUPS)
    def _(g):
        at = pl.multiple_of(g * LANES, LANES)
        qs = pl.ds(at, LANES)
        v = qkv[:, pl.ds(at + 2 * D, LANES)]
        qu = units[0, :, qs]
        ku = units[1, :, qs]
        gmx = branch[:, qs]
        sc = scale_of(g)
        pos_sum = jnp.zeros((WIN2, WIDE), f32)
        sc_sum = jnp.zeros((1, WIDE), f32)
        gqu, gku, gv = [], [], []
        for w in range(WINDOWS):
            rows = slice(w * WIN2, (w + 1) * WIN2)
            q_heads = stacked_heads(qu[rows], mask)
            g_heads = stacked_heads(gmx[rows], mask)
            cosine = mm_tb(ku[rows], q_heads)
            grad_att = mm_tb(v[rows], g_heads)
            attention = att[g, w]
            gv.append(mm(attention, g_heads))
            att_f = attention.astype(f32)
            dots = jnp.sum(grad_att * att_f, axis=0, keepdims=True)
            grad_scores = att_f * (grad_att - dots)
            pos_sum = pos_sum + grad_scores
            sc_sum = sc_sum + jnp.sum(grad_scores * cosine, axis=0, keepdims=True)
            grad_cos = (sc * grad_scores).astype(bf16)
            gku.append(mm(grad_cos, q_heads))
            gqu.append(own_heads(mm_ta(grad_cos, ku[rows])))
        vec[:, pl.ds(pl.multiple_of(6 * D + g * WIDE, WIDE), WIDE)] = sc_sum
        turned = pos_sum.T
        for h in range(GROUP):
            upper = turned[h * WIN2 : h * WIN2 + 32]
            lower = turned[h * WIN2 + 32 : (h + 1) * WIN2]
            pos[pl.ds(pl.multiple_of((g * GROUP + h) * 32, 32), 32), :] = jnp.concatenate((upper, lower), axis=1)
        results = []
        for n, got in ((0, gqu), (1, gku)):
            got = jnp.concatenate(got, axis=0)
            inv = inverses[n, :, qs]
            unit = qkv[:, pl.ds(at + n * D, LANES)].astype(f32) * inv
            results.append(inv * (got - unit * segment_sums(got * unit, ones)))
        results.append(jnp.concatenate(gv, axis=0))
        for n in range(3):
            vec[:, pl.ds(at + n * D, LANES)] = jnp.sum(results[n], axis=0, keepdims=True)
        side = g // (GROUPS // 2)
        inner = pl.multiple_of((g - side * (GROUPS // 2)) * LANES, LANES)

        def put(ref):
            for n in range(3):
                ref[:, pl.ds(g_at + n * half + inner, LANES)] = results[n].astype(bf16)

        pl.when(side == p)(lambda: put(keep))
        pl.when(side != p)(lambda: put(send))

    @pl.loop(0, 64)
    def _(n):
        tile = jnp.broadcast_to(vec[:, pl.ds(pl.multiple_of(n * LANES, LANES), LANES)], (8, LANES))
        for m in range(2):
            rows = pl.ds(pl.multiple_of((n + 64 * m) * 8, 8), 8)
            small[n + 64 * m] = jnp.concatenate((pos[rows, :], tile), axis=0).astype(bf16)


def input_grad_kernel(place, keep, send, wqkv, order_t, s_own, s_row, s_col, s_cor, total):
    p = place[2]
    half = D // 2
    for t in range(3):
        for ref, side in ((keep, p), (send, 1 - p)):
            cols = pl.ds(pl.multiple_of(t * D + side * half, half), half)
            at = 2 * D + half + t * half
            term = mm_tb(ref[:, at : at + half], wqkv[:, cols])
            if t == 0 and ref is keep:
                total[...] = term
            else:
                total[...] += term
    put_back(order_t, total[...].astype(bf16), s_own, s_row, s_col, s_cor)


def weight_grad_kernel(keep, other, small, out):
    block = out.shape[0]
    peer_rows, words = small.shape
    for n in range(block // peer_rows):
        out[n * peer_rows : (n + 1) * peer_rows, 2 * D :] = small[...]
    half = D // 2
    at = pl.multiple_of(pl.program_id(0) * block, block)
    for base, first, width, to in ((0, 2 * D + half, 3 * half, 0), (D, 2 * D, half, 3 * half)):
        a = jnp.concatenate((keep[:, pl.ds(at + base, block)], other[:, pl.ds(at + base, block)]), axis=0)
        g = jnp.concatenate((keep[:, first : first + width], other[:, first : first + width]), axis=0)
        out[:, to : to + width] = mm_ta(a, g).astype(bf16)


def sum_kernel(got, qkv_out, proj_out):
    half = D // 2
    for side in range(2):
        total = jnp.sum(got[:, side, :, 0 : 4 * half].astype(f32), axis=0)
        for t in range(3):
            qkv_out[:, t * D + side * half : t * D + (side + 1) * half] = total[:, t * half : (t + 1) * half]
        proj_out[:, side * half : (side + 1) * half] = total[:, 3 * half : 4 * half]


def finish_kernel(base, own, row, col, cor, spread, out):
    border = jnp.concatenate((col[...], cor[...]), axis=0)
    moved = own[...].astype(f32) + mm(spread[...], border)
    total = base[...].astype(f32) + moved
    out[HALO:, :] = total[HALO:].astype(bf16)
    out[:HALO, :] = (total[:HALO] + row[...].astype(f32)).astype(bf16)


def sds(shape, dtype):
    return jax.ShapeDtypeStruct(shape, dtype)


VM = pl.BlockSpec(memory_space=pltpu.VMEM)
SM = pl.BlockSpec(memory_space=pltpu.SMEM)
ANY = pl.BlockSpec(memory_space=pl.ANY)


def call(kernel, outs, scratch=(), specs=None, flops=0, bytes_accessed=0):
    return pl.pallas_call(
        kernel,
        out_shape=outs,
        in_specs=specs,
        out_specs=jax.tree.map(lambda _: VM, outs),
        scratch_shapes=list(scratch),
        compiler_params=pltpu.CompilerParams(vmem_limit_bytes=VMEM_LIMIT),
        cost_estimate=pl.CostEstimate(flops=flops, bytes_accessed=bytes_accessed, transcendentals=0),
    )


def neighbour(by_row, by_col):
    rows, cols = lax.axis_size("row"), lax.axis_size("col")
    reps = lax.axis_size("rep")
    pairs = []
    for s in range(reps):
        for r in range(rows):
            for c in range(cols):
                to = (s * rows + (r + by_row) % rows) * cols + (c + by_col) % cols
                pairs.append(((s * rows + r) * cols + c, to))
    return pairs


def per_device(
    tokens, cotangent, row_field, col_field, qkv_weight, qkv_bias, logit_scale, position_bias,
    proj_weight, proj_bias, norm_gain, norm_shift,
):
    devices = lax.axis_size(AXES)
    order = jnp.asarray(window_order(), bf16)
    order_t = jnp.asarray(window_order().T, bf16)
    spread = jnp.asarray(border_spread(), bf16)
    spread_t = jnp.asarray(border_spread().T, bf16)
    mask = jnp.asarray(head_mask(), bf16)
    ones = jnp.asarray(head_sums(), bf16)
    tok = tokens[0].reshape(TOK, D)
    cot = cotangent[0].reshape(TOK, D)

    row_in, col_in, cor_in = call(
        pack_kernel, (sds((2, HALO, D), bf16), sds((2, HALO, D), bf16), sds((2, CORNER, D), bf16)), (), [VM] * 3,
        flops=10**8, bytes_accessed=2**21,
    )(tok, cot, spread_t)
    row_in = lax.ppermute(row_in, AXES, neighbour(-1, 0))
    col_in = lax.ppermute(col_in, AXES, neighbour(0, -1))
    cor_in = lax.ppermute(cor_in, AXES, neighbour(-1, -1))

    col_index = lax.axis_index("col")
    place = jnp.stack((lax.axis_index("row") * SIDE, col_index * SIDE, col_index % 2)).astype(jnp.int32)
    bias_t = position_bias.reshape(GROUPS, GROUP, WIN2, WIN2).transpose(0, 3, 1, 2).reshape(GROUPS, WIN2, WIDE)

    keep, send, b_own, b_row, b_col, b_cor, small = call(
        local_kernel,
        (
            sds((TOK, 4 * D), bf16), sds((TOK, 4 * D), bf16), sds((TOK, D), bf16), sds((HALO, D), bf16),
            sds((HALO, D), bf16), sds((CORNER, D), bf16), sds((LANES, 16, LANES), bf16),
        ),
        [
            pltpu.VMEM((D, 3 * D), bf16), pltpu.VMEM((D, D), bf16), pltpu.VMEM((GROUPS, WIN2, WIDE), f32),
            pltpu.VMEM((CAT, D), bf16), pltpu.VMEM((TOK, 3 * D), bf16),
            pltpu.VMEM((GROUPS, WINDOWS, WIN2, WIDE), bf16), pltpu.VMEM((2, TOK, D), bf16),
            pltpu.VMEM((2, TOK, D), f32), pltpu.VMEM((TOK, D), bf16), pltpu.VMEM((TOK, D), f32),
            pltpu.VMEM((TOK, D), bf16), pltpu.VMEM((HEADS * 32, LANES), f32), pltpu.VMEM((1, 8 * D), f32),
            pltpu.SemaphoreType.DMA((5,)),
        ],
        [SM] * 4 + [VM] * 9 + [ANY, VM, ANY, ANY, VM, VM, VM],
        flops=5 * 10**9, bytes_accessed=20 * 2**20,
    )(
        place, row_field, col_field, logit_scale, tok, cot, row_in, col_in, cor_in, order, order_t, mask, ones,
        qkv_weight, qkv_bias.reshape(1, -1), bias_t, proj_weight, proj_bias.reshape(1, -1),
        norm_gain.reshape(1, -1), norm_shift.reshape(1, -1),
    )
    chunks = LANES // devices
    small = lax.all_to_all(small.reshape(devices, chunks * 16, LANES), AXES, 0, 0, tiled=True)
    small = jnp.sum(small.astype(f32), axis=0).astype(bf16)

    col_size = lax.axis_size("col")
    other = lax.ppermute(send, "col", [(i, i ^ 1) for i in range(col_size)])
    s_own, s_row, s_col, s_cor = call(
        input_grad_kernel,
        (sds((TOK, D), bf16), sds((HALO, D), bf16), sds((HALO, D), bf16), sds((CORNER, D), bf16)),
        [pltpu.VMEM((TOK, D), f32)],
        [SM] + [VM] * 4,
        flops=2 * 10**9, bytes_accessed=9 * 2**20,
    )(place, keep, send, qkv_weight, order_t)

    def sent_back(row, col, cor):
        return (
            lax.ppermute(row, AXES, neighbour(1, 0)),
            lax.ppermute(col, AXES, neighbour(0, 1)),
            lax.ppermute(cor, AXES, neighbour(1, 1)),
        )

    b_got = sent_back(b_row, b_col, b_cor)
    s_got = sent_back(s_row, s_col, s_cor)

    block = 256
    rows = D // devices
    extra = 2 * LANES
    small = small.reshape(-1, 16, LANES)
    small = jnp.concatenate((small[:, :8], small[:, 8:]), axis=2).reshape(rows, extra)
    part = pl.pallas_call(
        weight_grad_kernel,
        grid=(D // block,),
        out_shape=sds((D, 2 * D + extra), bf16),
        in_specs=[pl.BlockSpec((TOK, 4 * D), lambda i: (0, 0))] * 2
        + [pl.BlockSpec((rows, extra), lambda i: (0, 0))],
        out_specs=pl.BlockSpec((block, 2 * D + extra), lambda i: (i, 0)),
        compiler_params=pltpu.CompilerParams(vmem_limit_bytes=VMEM_LIMIT),
        cost_estimate=pl.CostEstimate(flops=8 * TOK * D * D, bytes_accessed=8 * 2**20, transcendentals=0),
    )(keep, other, small)
    part, b_got, s_got = lax.optimization_barrier((part, b_got, s_got))
    got = lax.all_to_all(part.reshape(devices, rows, 2 * D + extra), AXES, 0, 0, tiled=True)
    def finish(base, own, got):
        out = call(finish_kernel, sds((TOK, D), bf16), (), [VM] * 6, flops=10**8, bytes_accessed=2**21)(
            base, own, *got, spread
        )
        return out.reshape(1, SIDE, SIDE, D)

    block_out = finish(tok, b_own, b_got)
    grad_tokens = finish(cot, s_own, s_got)

    grad_qkv_weight, grad_proj_weight = call(
        sum_kernel, (sds((rows, 3 * D), f32), sds((rows, D), f32)), (), [VM], flops=10**7, bytes_accessed=2**22
    )(got.reshape(devices // 2, 2, rows, 2 * D + extra))
    small = got[:, :, 2 * D :].reshape(LANES, 8, extra)
    grad_position = small[:, :, :LANES].reshape(HEADS, WIN2 // 2, 2, WIN2).transpose(0, 2, 1, 3)
    grad_position = grad_position.reshape(HEADS, WIN2, WIN2).astype(f32)
    vector = small[:64, 0, LANES:].astype(f32).reshape(-1)
    grad_scale = vector[6 * D :].reshape(HEADS, WIN2).sum(axis=1)
    return (
        block_out, grad_tokens, grad_qkv_weight, grad_proj_weight, vector[: 3 * D], vector[3 * D : 4 * D],
        vector[4 * D : 5 * D], vector[5 * D : 6 * D], grad_scale, grad_position,
    )


def solution(mesh):
    grid = P("rep", "row", "col", None)
    rows = P(AXES, None)
    return jax.shard_map(
        per_device,
        mesh=mesh,
        in_specs=(grid, grid, P("rep", None), P("rep", None)) + (P(),) * 8,
        out_specs=(grid, grid, rows, rows) + (P(),) * 6,
        check_vma=False,
    )
```

time: 193 us -> 156 us (0.81)
  waiting for transfers between devices: 72.8 us -> 57 us
  local copies, waits for them, and re-layouts: 22.4 us -> 8.94 us
  other arithmetic: 9.35 us -> 3.86 us
  starting transfers between devices: 33.3 us -> 29.5 us
    ppermute x13 -> x10, waiting for transfers between devices: 43.8 us -> 0.81 us  [the longest x1 0.79 us: per_device(): cor_in = lax.ppermute(cor_in, AXES, neighbour(-1, -1))]
    all_to_all x4 -> x2, waiting for transfers between devices: 29 us -> 56.2 us  [the longest x1 53.3 us: per_device(): lax.all_to_all(part.reshape(devices, rows, 2 * D + extra), AXES, 0, 0, ti...]
    slice x13 -> x2, local copies, waits for them, and re-layouts: 3.92 us -> 0.03 us  [the longest x1 0.02 us: per_device(): grad_scale = vector[6 * D:].reshape(HEADS, WIN2).sum(axis=1)]
    unnamed x47 -> x20, local copies, waits for them, and re-layouts: 6.27 us -> 2.9 us
    all_to_all x4 -> x2, starting transfers between devices: 21 us -> 17.8 us  [the longest x1 10.5 us: per_device(): lax.all_to_all(small.reshape(devices, chunks * 16, LANES), AXES, 0, 0, ti...]
    squeeze x3 -> x0, local copies, waits for them, and re-layouts: 2.07 us -> none  [the longest x1 0.73 us: per_device(): row_in[1]]
    reduce_sum x3 -> x1, other arithmetic: 2.58 us -> 0.63 us  [per_device(): grad_scale = vector[6 * D:].reshape(HEADS, WIN2).sum(axis=1)]
    ppermute x13 -> x10, starting transfers between devices: 12.3 us -> 11.7 us  [the longest x1 4.37 us: per_device(): col_in = lax.ppermute(col_in, AXES, neighbour(0, -1))]
  transfers between devices with their start and end apart: 17 -> 12, of which waited for: 8 -> 3; matrix products, arithmetic and copies ran while one was open for 9% -> 3% of each run, Pallas kernels for 11% -> 12%
where the time goes in v2:
time: 156 us; the launch traced here: 155 us
  waiting for transfers between devices  57 us (37%)
  Pallas kernels  54.9 us (35%)
  starting transfers between devices  29.5 us (19%)
  local copies, waits for them, and re-layouts  8.94 us (6%)
  other arithmetic  3.86 us (2%)
    all_to_all x1, waiting for transfers between devices, per_device(): lax.all_to_all(part.reshape(devices, rows, 2 * D + extra), AXES, 0, 0, ti...  53.3 us
    pallas_call x1, Pallas kernels, per_device(): call(local_kernel, (sds((TOK, 4 * D), bf16), sds((TOK, 4 * D), bf16), sds...  30.8 us
    all_to_all x1, starting transfers between devices, per_device(): lax.all_to_all(small.reshape(devices, chunks * 16, LANES), AXES, 0, 0, ti...  10.5 us
    all_to_all x1, starting transfers between devices, per_device(): lax.all_to_all(part.reshape(devices, rows, 2 * D + extra), AXES, 0, 0, ti...  7.37 us
    pallas_call x1, Pallas kernels, per_device(): call(input_grad_kernel, (sds((TOK, D), bf16), sds((HALO, D), bf16), sds((...  7 us
    pallas_call x1, Pallas kernels, per_device(): pl.pallas_call(weight_grad_kernel, grid=(D // block,), out_shape=sds((D,...  6.56 us
    pallas_call x2, Pallas kernels, finish(): call(finish_kernel, sds((TOK, D), bf16), (), [VM] * 6, flops=10 ** 8, byt...  4.76 us
    ppermute x1, starting transfers between devices, per_device(): col_in = lax.ppermute(col_in, AXES, neighbour(0, -1))  4.37 us
  transfers between devices with their start and end apart: 12, of which 3 were waited for; matrix products, arithmetic and copies ran while one was open for 3% of the time, Pallas kernels for 12%

profile of v2, /device:TPU:0, one launch (start us, length us, event | category | flops | bytes accessed | tf_op | source)
XLA Modules:
  0.0 155.1 jit_solution(5000663652693151993)
XLA Ops:
  0.6 2.2 %shard_map.249 = (bf16[2,64,1024]{2,1,0:T(8,128)(2,1)}, bf16[2,64,1024]{2,1,0:T(8,128)(2,1)}, bf16[2,16,1024]{2,1,0:T(8,128)(2,1)}) custom-call(bf16[256,1024]{1,0:T(8,128)(2,1)} %bitcast.30, bf16[256,1024]{1,0:T(8,128)(2,1)} %bitcast.27, bf16[80,256]{1,0:T(8,128)(2,1)} %constant.43.clone.spread_t), custom_call_target="tpu_custom_call" | custom-call | flops 100000000 | bytes 2097152 | tf_op jit(solution)/shard_map/pallas_call | solution.py:413
  2.9 2.0 %collective-permute-start = (bf16[2,64,1024]{2,1,0:T(8,128)(2,1)}, bf16[2,64,1024]{2,1,0:T(8,128)(2,1)S(1)}, u32[]{:S(2)}, u32[]{:S(2)}) collective-permute-start(bf16[2,64,1024]{2,1,0:T(8,128)(2,1)} %get-tuple-element.33), channel_id=1, source_target_pairs={{0,32},{1,33},{2,34},{3,35},{4,36},{5,37},{6,38},{7,39},{8,40},{9,... | collective-permute-start | bytes 786440 | tf_op jit(solution)/shard_map/ppermute | solution.py:417
  4.9 4.4 %collective-permute-start.1 = (bf16[2,64,1024]{2,1,0:T(8,128)(2,1)}, bf16[2,64,1024]{2,1,0:T(8,128)(2,1)S(1)}, u32[]{:S(2)}, u32[]{:S(2)}) collective-permute-start(bf16[2,64,1024]{2,1,0:T(8,128)(2,1)} %get-tuple-element.34), channel_id=1, source_target_pairs={{0,31},{1,0},{2,1},{3,2},{4,3},{5,4},{6,5},{7,6},{8,7},{9,8},{10,9... | collective-permute-start | bytes 786440 | tf_op jit(solution)/shard_map/ppermute | solution.py:418
  9.8 1.6 %copy.28 = f32[8,4,64,64]{2,1,3,0:T(4,128)S(1)} copy(f32[8,4,64,64]{3,2,1,0:T(8,128)} %bitcast.33) | data formatting | bytes 1048576 | tf_op jit(solution)/shard_map/reshape | solution.py:423
  11.4 1.4 reshape.85.bias_hbm
  13.4 0.8 collective-permute-done.2.cor_in
  15.0 30.8 %shard_map.250 = (bf16[256,4096]{1,0:T(8,128)(2,1)}, bf16[256,4096]{1,0:T(8,128)(2,1)}, bf16[256,1024]{1,0:T(8,128)(2,1)}, bf16[64,1024]{1,0:T(8,128)(2,1)}, bf1...) custom-call(s32[3]{0:T(128)} %pad_add_fusion.place, s32[1,32]{1,0:T(1,128)} %row_field.1, ...), custom_call_target="tpu_custom_call" | custom-call | flops 5000000000 | bytes 20971520 | tf_op jit(solution)/shard_map/pallas_call | solution.py:425
  45.9 10.5 %all-to-all-start = ((bf16[128,16,128]{2,1,0:T(8,128)(2,1)}), bf16[128,16,128]{2,1,0:T(8,128)(2,1)S(1)}, u32[]{:S(2)}, u32[]{:S(2)}) async-start(bf16[128,16,128]{2,1,0:T(8,128)(2,1)} %get-tuple-element.39), calls=%async_computation | async-start | bytes 1048576 | tf_op jit(solution)/shard_map/all_to_all | solution.py:447
  56.3 0.9 collective-permute-start.6
  57.6 1.1 collective-permute-start.5
  58.6 7.0 %shard_map.252 = (bf16[256,1024]{1,0:T(8,128)(2,1)}, bf16[64,1024]{1,0:T(8,128)(2,1)}, bf16[64,1024]{1,0:T(8,128)(2,1)}, bf16[16,1024]{1,0:T(8,128)(2,1)}) custom-call(s32[3]{0:T(128)} %pad_add_fusion.place, bf16[256,4096]{1,0:T(8,128)(2,1)} %get-tuple-element.37.keep, bf16[256,4096]{1,0:T(8,128)(2,1)} %get-tuple-element.38.send, bf16[1024,3072]{1,0:T(8,128)(2,1)} %wqkv.1, ...), custom_call_target="tpu_custom_call" | custom-call | flops 2000000000 | bytes 9437184 | tf_op jit(solution)/shard_map/pallas_call | solution.py:452
  65.6 1.8 %collective-permute-start.9 = (bf16[16,1024]{1,0:T(8,128)(2,1)}, bf16[16,1024]{1,0:T(8,128)(2,1)S(1)}, u32[]{:S(2)}, u32[]{:S(2)}) collective-permute-start(bf16[16,1024]{1,0:T(8,128)(2,1)} %get-tuple-element.45), channel_id=1, source_target_pairs={{0,33},{1,34},{2,35},{3,36},{4,37},{5,38},{6,39},{7,40},{8,41},{9,... | collective-permute-start | bytes 98312 | tf_op jit(solution)/shard_map/ppermute | solution.py:464
  67.5 2.9 %all-to-all-done = bf16[128,16,128]{2,1,0:T(8,128)(2,1)S(1)} async-done(((bf16[128,16,128]{2,1,0:T(8,128)(2,1)}), bf16[128,16,128]{2,1,0:T(8,128)(2,1)S(1)}, u32[]{:S(2)}, u32[]{:S(2)}) %all-to-all-start) | async-done | bytes 524320 | tf_op jit(solution)/shard_map/all_to_all | solution.py:447
  71.1 0.6 collective-permute-start.7
  71.7 1.4 copy-done
  73.1 6.6 %shard_map.251 = bf16[1024,2304]{1,0:T(8,128)(2,1)} custom-call(bf16[256,4096]{1,0:T(8,128)(2,1)} %get-tuple-element.37.keep, bf16[256,4096]{1,0:T(8,128)(2,1)} %copy-done, bf16[8,256]{1,0:T(8,128)(2,1)} %maximum_bitcast_fusion.small), custom_call_target="tpu_custom_call" | custom-call | flops 2147483648 | bytes 8388608 | tf_op jit(solution)/shard_map/pallas_call | solution.py:475
  80.5 7.4 %all-to-all-start.1 = ((bf16[128,8,2304]{2,1,0:T(8,128)(2,1)}), bf16[128,8,2304]{2,1,0:T(8,128)(2,1)}, u32[]{:S(2)}, u32[]{:S(2)}) async-start(bf16[128,8,2304]{2,1,0:T(8,128)(2,1)} %bitcast.25), calls=%async_computation.1 | async-start | bytes 9437184 | tf_op jit(solution)/shard_map/all_to_all | solution.py:486
  87.8 2.4 %shard_map.254 = bf16[256,1024]{1,0:T(8,128)(2,1)} custom-call(bf16[256,1024]{1,0:T(8,128)(2,1)} %bitcast.29, bf16[256,1024]{1,0:T(8,128)(2,1)} %get-tuple-element.49.own, bf16[64,1024]{1,0:T(8,128)(2,1)} %copy-done.3, bf16[64,1024]{1,0:T(8,128)(2,1)} %copy-done.4, bf16[16,1024]{1,0:T(8,128)(2,1)} %copy-done.6, bf16[256,80]{1,0:T(8,128)(2,1)} %constant.42.clone.spread), custom_call_target="tpu_custom_call" | custom-call | flops 100000000 | bytes 2097152 | tf_op jit(solution)/shard_map/pallas_call | solution.py:488
  90.2 2.4 %shard_map.253 = bf16[256,1024]{1,0:T(8,128)(2,1)} custom-call(bf16[256,1024]{1,0:T(8,128)(2,1)} %bitcast.32, bf16[256,1024]{1,0:T(8,128)(2,1)} %get-tuple-element.36.own, bf16[64,1024]{1,0:T(8,128)(2,1)} %copy-done.1, bf16[64,1024]{1,0:T(8,128)(2,1)} %copy-done.2, bf16[16,1024]{1,0:T(8,128)(2,1)} %copy-done.5, bf16[256,80]{1,0:T(8,128)(2,1)} %constant.42.clone.spread), custom_call_target="tpu_custom_call" | custom-call | flops 100000000 | bytes 2097152 | tf_op jit(solution)/shard_map/pallas_call | solution.py:488
  92.6 53.3 %all-to-all-done.1 = bf16[128,8,2304]{2,1,0:T(8,128)(2,1)} async-done(((bf16[128,8,2304]{2,1,0:T(8,128)(2,1)}), bf16[128,8,2304]{2,1,0:T(8,128)(2,1)}, u32[]{:S(2)}, u32[]{:S(2)}) %all-to-all-start.1) | async-done | bytes 4718624 | tf_op jit(solution)/shard_map/all_to_all | solution.py:486
  146.0 0.9 slice_convert_fusion.1
  148.2 3.5 %shard_map.255 = (f32[8,3072]{1,0:T(8,128)}, f32[8,1024]{1,0:T(8,128)}) custom-call(bf16[64,2,8,2304]{3,2,1,0:T(8,128)(2,1)} %bitcast.16.got), custom_call_target="tpu_custom_call" | custom-call | flops 10000000 | bytes 4194304 | tf_op jit(solution)/shard_map/pallas_call | solution.py:496
  151.7 1.0 slice_convert_fusion
  153.3 1.1 copy.29
  (42 shorter events, 6.3 us)
Async XLA Ops:
  2.9 11.3 %collective-permute-start = (bf16[2,64,1024]{2,1,0:T(8,128)(2,1)}, bf16[2,64,1024]{2,1,0:T(8,128)(2,1)S(1)}, u32[]{:S(2)}, u32[]{:S(2)}) collective-permute-start(bf16[2,64,1024]{2,1,0:T(8,128)(2,1)} %get-tuple-element.33), channel_id=1, source_target_pairs={{0,32},{1,33},{2,34},{3,35},{4,36},{5,37},{6,38},{7,39},{8,40},{9,... | collective-permute-start | bytes 786440 | tf_op jit(solution)/shard_map/ppermute | solution.py:417
  4.9 9.3 %collective-permute-start.1 = (bf16[2,64,1024]{2,1,0:T(8,128)(2,1)}, bf16[2,64,1024]{2,1,0:T(8,128)(2,1)S(1)}, u32[]{:S(2)}, u32[]{:S(2)}) collective-permute-start(bf16[2,64,1024]{2,1,0:T(8,128)(2,1)} %get-tuple-element.34), channel_id=1, source_target_pairs={{0,31},{1,0},{2,1},{3,2},{4,3},{5,4},{6,5},{7,6},{8,7},{9,8},{10,9... | collective-permute-start | bytes 786440 | tf_op jit(solution)/shard_map/ppermute | solution.py:418
  9.3 4.9 %collective-permute-start.2 = (bf16[2,16,1024]{2,1,0:T(8,128)(2,1)}, bf16[2,16,1024]{2,1,0:T(8,128)(2,1)S(1)}, u32[]{:S(2)}, u32[]{:S(2)}) collective-permute-start(bf16[2,16,1024]{2,1,0:T(8,128)(2,1)} %get-tuple-element.35), channel_id=1, source_target_pairs={{0,63},{1,32},{2,33},{3,34},{4,35},{5,36},{6,37},{7,38},{8,39},{9,... | collective-permute-start | bytes 196616 | tf_op jit(solution)/shard_map/ppermute | solution.py:419
  14.2 0.6 copy-start.9
  14.2 0.7 copy-start.7
  14.2 0.8 copy-start.8
  45.8 25.9 %collective-permute-start.3 = (bf16[256,4096]{1,0:T(8,128)(2,1)}, bf16[256,4096]{1,0:T(8,128)(2,1)S(1)}, u32[]{:S(2)}, u32[]{:S(2)}) collective-permute-start(bf16[256,4096]{1,0:T(8,128)(2,1)} %get-tuple-element.38.send), channel_id=1, source_target_pairs={{0,1},{1,0},{2,3},{3,2},{4,5},{5,4},{6,7},{7,6},{8,9},{9,8},{10,11... | collective-permute-start | bytes 6291464 | tf_op jit(solution)/shard_map/ppermute | solution.py:451
  45.9 24.5 %all-to-all-start = ((bf16[128,16,128]{2,1,0:T(8,128)(2,1)}), bf16[128,16,128]{2,1,0:T(8,128)(2,1)S(1)}, u32[]{:S(2)}, u32[]{:S(2)}) async-start(bf16[128,16,128]{2,1,0:T(8,128)(2,1)} %get-tuple-element.39), calls=%async_computation | async-start | bytes 1048576 | tf_op jit(solution)/shard_map/all_to_all | solution.py:447
  56.3 14.8 %collective-permute-start.6 = (bf16[16,1024]{1,0:T(8,128)(2,1)}, bf16[16,1024]{1,0:T(8,128)(2,1)S(1)}, u32[]{:S(2)}, u32[]{:S(2)}) collective-permute-start(bf16[16,1024]{1,0:T(8,128)(2,1)} %get-tuple-element.42), channel_id=1, source_target_pairs={{0,33},{1,34},{2,35},{3,36},{4,37},{5,38},{6,39},{7,40},{8,41},{9,... | collective-permute-start | bytes 98312 | tf_op jit(solution)/shard_map/ppermute | solution.py:464
  57.2 22.5 %collective-permute-start.4 = (bf16[64,1024]{1,0:T(8,128)(2,1)}, bf16[64,1024]{1,0:T(8,128)(2,1)S(1)}, u32[]{:S(2)}, u32[]{:S(2)}) collective-permute-start(bf16[64,1024]{1,0:T(8,128)(2,1)} %get-tuple-element.40), channel_id=1, source_target_pairs={{0,32},{1,33},{2,34},{3,35},{4,36},{5,37},{6,38},{7,39},{8,40},{9,... | collective-permute-start | bytes 393224 | tf_op jit(solution)/shard_map/ppermute | solution.py:462
  57.6 22.1 %collective-permute-start.5 = (bf16[64,1024]{1,0:T(8,128)(2,1)}, bf16[64,1024]{1,0:T(8,128)(2,1)S(1)}, u32[]{:S(2)}, u32[]{:S(2)}) collective-permute-start(bf16[64,1024]{1,0:T(8,128)(2,1)} %get-tuple-element.41), channel_id=1, source_target_pairs={{0,1},{1,2},{2,3},{3,4},{4,5},{5,6},{6,7},{7,8},{8,9},{9,10},{10,1... | collective-permute-start | bytes 393224 | tf_op jit(solution)/shard_map/ppermute | solution.py:463
  65.6 14.0 %collective-permute-start.9 = (bf16[16,1024]{1,0:T(8,128)(2,1)}, bf16[16,1024]{1,0:T(8,128)(2,1)S(1)}, u32[]{:S(2)}, u32[]{:S(2)}) collective-permute-start(bf16[16,1024]{1,0:T(8,128)(2,1)} %get-tuple-element.45), channel_id=1, source_target_pairs={{0,33},{1,34},{2,35},{3,36},{4,37},{5,38},{6,39},{7,40},{8,41},{9,... | collective-permute-start | bytes 98312 | tf_op jit(solution)/shard_map/ppermute | solution.py:464
  71.1 19.2 %copy-start.5 = (bf16[16,1024]{1,0:T(8,128)(2,1)}, bf16[16,1024]{1,0:T(8,128)(2,1)S(1)}, u32[]{:S(2)}) copy-start(bf16[16,1024]{1,0:T(8,128)(2,1)S(1)} %collective-permute-done.6.cor) | copy-start | bytes 98308
  71.1 8.6 %collective-permute-start.7 = (bf16[64,1024]{1,0:T(8,128)(2,1)}, bf16[64,1024]{1,0:T(8,128)(2,1)S(1)}, u32[]{:S(2)}, u32[]{:S(2)}) collective-permute-start(bf16[64,1024]{1,0:T(8,128)(2,1)} %get-tuple-element.43), channel_id=1, source_target_pairs={{0,32},{1,33},{2,34},{3,35},{4,36},{5,37},{6,38},{7,39},{8,40},{9,... | collective-permute-start | bytes 393224 | tf_op jit(solution)/shard_map/ppermute | solution.py:462
  71.7 1.4 copy-start
  71.7 8.0 %collective-permute-start.8 = (bf16[64,1024]{1,0:T(8,128)(2,1)}, bf16[64,1024]{1,0:T(8,128)(2,1)S(1)}, u32[]{:S(2)}, u32[]{:S(2)}) collective-permute-start(bf16[64,1024]{1,0:T(8,128)(2,1)} %get-tuple-element.44), channel_id=1, source_target_pairs={{0,1},{1,2},{2,3},{3,4},{4,5},{5,6},{6,7},{7,8},{8,9},{9,10},{10,1... | collective-permute-start | bytes 393224 | tf_op jit(solution)/shard_map/ppermute | solution.py:463
  79.7 0.6 copy-start.6
  79.7 0.7 copy-start.1
  79.7 0.7 copy-start.2
  79.7 0.7 copy-start.3
  79.7 0.7 copy-start.4
  80.5 65.5 %all-to-all-start.1 = ((bf16[128,8,2304]{2,1,0:T(8,128)(2,1)}), bf16[128,8,2304]{2,1,0:T(8,128)(2,1)}, u32[]{:S(2)}, u32[]{:S(2)}) async-start(bf16[128,8,2304]{2,1,0:T(8,128)(2,1)} %bitcast.25), calls=%async_computation.1 | async-start | bytes 9437184 | tf_op jit(solution)/shard_map/all_to_all | solution.py:486

commit v3 on v2

v3 whole, which is shorter than its diff:
```python
import functools

import jax
import jax.numpy as jnp
import numpy as np
from jax import lax
from jax.experimental import pallas as pl
from jax.experimental.pallas import tpu as pltpu
from jax.sharding import PartitionSpec as P

HEADS = 32
WIN = 8
SHIFT = 4
SIDE = 16
TOK = SIDE * SIDE
D = 1024
HALO = (SIDE - SHIFT) * SHIFT
CORNER = SHIFT * SHIFT
BORDER = 2 * HALO + CORNER
CAT = TOK + BORDER
WIN2 = WIN * WIN
WINDOWS = TOK // WIN2
GROUP = 4
GROUPS = HEADS // GROUP
LANES = 128
WIDE = GROUP * WIN2
FUSED = 4
EXTRA = 2 * LANES
AXES = ("rep", "row", "col")

norm_epsilon = 1e-05
unit_floor = 1e-12
f32 = jnp.float32
bf16 = jnp.bfloat16
VMEM_LIMIT = 56 * 1024 * 1024


def window_order():
    order = np.zeros((TOK, CAT), np.float32)
    for r in range(SIDE):
        for c in range(SIDE):
            n = ((r // WIN) * 2 + c // WIN) * WIN2 + (r % WIN) * WIN + c % WIN
            rr, cc = r + SHIFT, c + SHIFT
            if rr < SIDE and cc < SIDE:
                m = rr * SIDE + cc
            elif cc < SIDE:
                m = TOK + (rr - SIDE) * (SIDE - SHIFT) + cc - SHIFT
            elif rr < SIDE:
                m = TOK + HALO + (rr - SHIFT) * SHIFT + (cc - SIDE)
            else:
                m = TOK + 2 * HALO + (rr - SIDE) * SHIFT + (cc - SIDE)
            order[n, m] = 1.0
    return order


def border_spread():
    spread = np.zeros((TOK, BORDER), np.float32)
    for r in range(SIDE):
        for c in range(SIDE):
            if r < SHIFT and c >= SHIFT:
                spread[r * SIDE + c, r * (SIDE - SHIFT) + c - SHIFT] = 1.0
            elif r >= SHIFT and c < SHIFT:
                spread[r * SIDE + c, HALO + (r - SHIFT) * SHIFT + c] = 1.0
            elif r < SHIFT and c < SHIFT:
                spread[r * SIDE + c, 2 * HALO + r * SHIFT + c] = 1.0
    return spread


def head_mask():
    rows = np.arange(WIDE)[:, None] // WIN2
    cols = np.arange(LANES)[None, :] // (LANES // GROUP)
    return (rows == cols).astype(np.float32)


def head_sums():
    heads = np.arange(2 * LANES) // (LANES // GROUP)
    return (heads[:, None] == heads[None, :]).astype(np.float32)


def mm(a, b):
    return jnp.dot(a, b, preferred_element_type=f32)


def mm_tb(a, b):
    return lax.dot_general(a, b, (((1,), (1,)), ((), ())), preferred_element_type=f32)


def mm_ta(a, b):
    return lax.dot_general(a, b, (((0,), (0,)), ((), ())), preferred_element_type=f32)


def exact_sums(values, ones):
    high = values.astype(bf16)
    low = (values - high.astype(f32)).astype(bf16)
    return mm(high, ones) + mm(low, ones)


def stacked_heads(x, mask):
    return jnp.concatenate((x, x, x, x), axis=0) * mask


def split_border(border, n, row, col, cor):
    row[n] = border[:HALO]
    col[n] = border[HALO : 2 * HALO]
    cor[n] = border[2 * HALO :]


def pack_kernel(tok, cot, spread_t, row, col, cor):
    for n, ref in enumerate((tok, cot)):
        split_border(mm(spread_t[...], ref[...]).astype(bf16), n, row, col, cor)


def local_kernel(
    place, row_field, col_field, logit_scale, tok, cot, row_in, col_in, cor_in, order, order_t, mask_ref, ones_ref,
    wqkv_hbm, bqkv, bias_hbm, wproj_hbm, bproj, gain, shift,
    send, keep, own, row, col, cor, small,
    wqkv, wproj, bias_t, cat, qkv, att, cos, units, inverses, grad, wide, branch, pos, vec,
    x, mixed, gp_send, gp_keep, g_send, g_keep, border, sems, out_sems,
):
    loads = [
        pltpu.make_async_copy(wqkv_hbm.at[:, pl.ds(t * D, D)], wqkv.at[:, pl.ds(t * D, D)], sems.at[t])
        for t in range(3)
    ]
    loads.append(pltpu.make_async_copy(bias_hbm, bias_t, sems.at[3]))
    loads.append(pltpu.make_async_copy(wproj_hbm, wproj, sems.at[4]))
    for load in loads:
        load.start()

    p = place[2]
    half = D // 2
    stores = []

    def write(source, target):
        copy = pltpu.make_async_copy(source, target, out_sems.at[len(stores)])
        copy.start()
        stores.append(copy)

    for n, ref in enumerate((tok, cot)):
        cat[0:TOK] = ref[...]
        cat[TOK : TOK + HALO] = row_in[n]
        cat[TOK + HALO : TOK + 2 * HALO] = col_in[n]
        cat[TOK + 2 * HALO : CAT] = cor_in[n]
        moved = mm(order[...], cat[...]).astype(bf16)
        if n == 0:
            x[...] = moved
            write(x, send.at[:, pl.ds(3 * half, D)])
        else:
            grad[...] = moved

    sub = lax.broadcasted_iota(jnp.int32, (WIN2, WIDE), 0)
    lane = lax.broadcasted_iota(jnp.int32, (WIN2, WIDE), 1) % WIN2
    row_ids, col_ids = [], []
    for i in range(SIDE):
        row_ids.append(row_field[0, lax.rem(place[0] + SHIFT + i, row_field.shape[1])] * 1024)
        col_ids.append(col_field[0, lax.rem(place[1] + SHIFT + i, col_field.shape[1])])

    def spread_ids(ids, index):
        out = jnp.zeros((WIN2, WIDE), jnp.int32)
        for i in range(WIN):
            out = jnp.where(index == i, ids[i], out)
        return out

    row_same, col_same = [], []
    for n in range(2):
        part = slice(n * WIN, (n + 1) * WIN)
        row_same.append(spread_ids(row_ids[part], sub // WIN) == spread_ids(row_ids[part], lane // WIN))
        col_same.append(spread_ids(col_ids[part], sub % WIN) == spread_ids(col_ids[part], lane % WIN))
    allowed = [(row_same[w // 2] & col_same[w % 2]).astype(f32) for w in range(WINDOWS)]
    mask = mask_ref[...]
    mask_pair = jnp.concatenate((mask, mask), axis=1)
    ones = ones_ref[...]
    wide_lane = lax.broadcasted_iota(jnp.int32, (1, WIDE), 1) // WIN2

    odd_head = lax.broadcasted_iota(jnp.int32, (WIN2, LANES), 1) // (LANES // GROUP) % 2 == 1

    def own_heads(full, dtype):
        picked = jnp.concatenate((full[:WIN2, :LANES], full[WIN2:, LANES:]), axis=0).astype(dtype).T
        return jnp.where(odd_head, picked[WIN2:], picked[:WIN2])

    head_lane = lax.broadcasted_iota(jnp.int32, (WIN2, LANES), 1) // (LANES // GROUP)

    def pick_heads(full):
        out = full[:WIN2]
        for h in range(1, GROUP):
            out = jnp.where(head_lane == h, full[h * WIN2 : (h + 1) * WIN2], out)
        return out

    def scale_of(g):
        out = jnp.zeros((1, WIDE), f32)
        for h in range(GROUP):
            out = jnp.where(wide_lane == h, logit_scale[g * GROUP + h], out)
        return out

    for t in range(3):
        loads[t].wait()

        @pl.loop(0, 2)
        def _(n):
            cols = pl.ds(pl.multiple_of(t * D + n * 512, 512), 512)
            qkv[:, cols] = (mm(x[...], wqkv[:, cols]) + bqkv[:, cols]).astype(bf16)

    loads[3].wait()

    def attend(g):
        at = pl.multiple_of(g * LANES, LANES)
        qs = pl.ds(at, LANES)
        q = qkv[:, qs].astype(f32)
        k = qkv[:, pl.ds(at + D, LANES)].astype(f32)
        v = qkv[:, pl.ds(at + 2 * D, LANES)]
        sc = scale_of(g)
        bias = bias_t[g]
        raw = jnp.concatenate((q, k), axis=1)
        inv = lax.rsqrt(jnp.maximum(exact_sums(raw * raw, ones), unit_floor * unit_floor))
        unit = (raw * inv).astype(bf16)
        q_inv, k_inv, qu, ku = inv[:, :LANES], inv[:, LANES:], unit[:, :LANES], unit[:, LANES:]
        cosines, attentions, mixed_parts = [], [], []
        for w in range(WINDOWS):
            rows = slice(w * WIN2, (w + 1) * WIN2)
            cosine = mm_tb(ku[rows], stacked_heads(qu[rows], mask))
            weights = jnp.exp(sc * cosine + bias) * allowed[w]
            total = jnp.sum(weights, axis=0, keepdims=True)
            attention = (weights * (1.0 / total)).astype(bf16)
            cosines.append(cosine)
            attentions.append(attention)
            mixed_parts.append(pick_heads(mm_ta(attention, v[rows])).astype(bf16))

        def store():
            inverses[0, :, qs] = q_inv
            inverses[1, :, qs] = k_inv
            units[0, :, qs] = qu
            units[1, :, qs] = ku
            for w in range(WINDOWS):
                att[g, w] = attentions[w]
                cos[g, w] = cosines[w]
            mixed[:, qs] = jnp.concatenate(mixed_parts, axis=0)

        return store

    @pl.loop(0, GROUPS // FUSED)
    def _(n):
        for store in [attend(n * FUSED + u) for u in range(FUSED)]:
            store()

    write(mixed, send.at[:, pl.ds(0, D)])
    loads[4].wait()

    @pl.loop(0, 4)
    def _(n):
        cols = pl.ds(pl.multiple_of(n * 256, 256), 256)
        wide[:, cols] = mm(mixed[...], wproj[:, cols]) + bproj[:, cols]

    gain_v = gain[...]
    shift_v = shift[...]
    vec[...] = jnp.zeros_like(vec)

    @pl.loop(0, TOK // 32)
    def _(n):
        rows = pl.ds(pl.multiple_of(n * 32, 32), 32)
        projected = wide[rows, :]
        centre = projected - jnp.mean(projected, axis=-1, keepdims=True)
        inv_std = lax.rsqrt(jnp.mean(centre * centre, axis=-1, keepdims=True) + norm_epsilon)
        normed = centre * inv_std
        branch[rows, :] = (normed * gain_v + shift_v).astype(bf16)
        go = grad[rows, :].astype(f32)
        gn = go * gain_v
        gpf = inv_std * (
            gn - jnp.mean(gn, axis=-1, keepdims=True) - normed * jnp.mean(gn * normed, axis=-1, keepdims=True)
        )
        grad[rows, :] = gpf.astype(bf16)
        vec[:, 3 * D : 4 * D] += jnp.sum(gpf, axis=0, keepdims=True)
        vec[:, 4 * D : 5 * D] += jnp.sum(go * normed, axis=0, keepdims=True)
        vec[:, 5 * D : 6 * D] += jnp.sum(go, axis=0, keepdims=True)

    gp_keep[...] = grad[:, pl.ds(pl.multiple_of(p * half, half), half)]
    gp_send[...] = grad[:, pl.ds(pl.multiple_of((1 - p) * half, half), half)]
    write(gp_keep, keep.at[:, pl.ds(0, half)])
    write(gp_send, send.at[:, pl.ds(D, half)])

    def give_back(n, values):
        border[n] = mm(order_t[...], values).astype(bf16)
        first = 0
        for ref, count in ((own, TOK), (row, HALO), (col, HALO), (cor, CORNER)):
            write(border.at[n, pl.ds(first, count), :], ref.at[n])
            first += count

    give_back(0, branch[...])

    @pl.loop(0, 4)
    def _(n):
        cols = pl.ds(pl.multiple_of(n * 256, 256), 256)
        branch[:, cols] = mm_tb(grad[...], wproj[cols, :]).astype(bf16)

    def attend_back(g):
        at = pl.multiple_of(g * LANES, LANES)
        qs = pl.ds(at, LANES)
        v = qkv[:, pl.ds(at + 2 * D, LANES)]
        qu = units[0, :, qs]
        ku = units[1, :, qs]
        gmx = branch[:, qs]
        sc = scale_of(g)
        attentions = [att[g, w] for w in range(WINDOWS)]
        cosines = [cos[g, w] for w in range(WINDOWS)]
        invs = [inverses[n, :, qs] for n in range(2)]
        raws = [qkv[:, pl.ds(at + n * D, LANES)] for n in range(2)]
        pos_sum = jnp.zeros((WIN2, WIDE), f32)
        sc_sum = jnp.zeros((WIN2, WIDE), f32)
        gqu, gku, gv = [], [], []
        for w in range(WINDOWS):
            rows = slice(w * WIN2, (w + 1) * WIN2)
            both = stacked_heads(jnp.concatenate((gmx[rows], qu[rows]), axis=1), mask_pair)
            grad_att = mm_tb(v[rows], both[:, :LANES])
            attention = attentions[w]
            att_f = attention.astype(f32)
            dots = jnp.sum(grad_att * att_f, axis=0, keepdims=True)
            grad_scores = att_f * (grad_att - dots)
            pos_sum = pos_sum + grad_scores
            sc_sum = sc_sum + grad_scores * cosines[w]
            grad_cos = (sc * grad_scores).astype(bf16)
            pair = mm(jnp.concatenate((attention, grad_cos), axis=0), both)
            gv.append(pair[:WIN2, :LANES])
            gku.append(pair[WIN2:, LANES:])
            gqu.append(own_heads(mm_ta(ku[rows], grad_cos), f32))
        turned = pos_sum.T
        pos_parts = []
        for h in range(GROUP):
            upper = turned[h * WIN2 : h * WIN2 + 32]
            lower = turned[h * WIN2 + 32 : (h + 1) * WIN2]
            pos_parts.append(jnp.concatenate((upper, lower), axis=1))
        got = jnp.concatenate((jnp.concatenate(gqu, axis=0), jnp.concatenate(gku, axis=0)), axis=1)
        inv = jnp.concatenate(invs, axis=1)
        unit = jnp.concatenate(raws, axis=1).astype(f32) * inv
        got = inv * (got - unit * mm((got * unit).astype(bf16), ones))
        results = [got[:, :LANES], got[:, LANES:]]
        results.append(jnp.concatenate(gv, axis=0))
        sums = [jnp.sum(result, axis=0, keepdims=True) for result in results]
        sc_row = jnp.sum(sc_sum, axis=0, keepdims=True)
        inner = pl.multiple_of(lax.rem(g, GROUPS // 2) * LANES, LANES)

        def store():
            vec[:, pl.ds(pl.multiple_of(6 * D + g * WIDE, WIDE), WIDE)] = sc_row
            pos[pl.ds(pl.multiple_of(g * LANES, LANES), LANES), :] = jnp.concatenate(pos_parts, axis=0)
            for n in range(3):
                vec[:, pl.ds(at + n * D, LANES)] = sums[n]

            def put(ref):
                for n in range(3):
                    ref[:, pl.ds(n * half + inner, LANES)] = results[n].astype(bf16)

            side = g // (GROUPS // 2)
            pl.when(side == p)(lambda: put(g_keep))
            pl.when(side != p)(lambda: put(g_send))

        return store

    @pl.loop(0, GROUPS // FUSED)
    def _(n):
        for store in [attend_back(n * FUSED + u) for u in range(FUSED)]:
            store()

    write(g_keep, keep.at[:, pl.ds(half, 3 * half)])
    write(g_send, send.at[:, pl.ds(5 * half, 3 * half)])

    @pl.loop(0, 64)
    def _(n):
        rows = pl.ds(pl.multiple_of(n * 16, 16), 16)
        tiles = []
        for m in range(2):
            at = pl.multiple_of(lax.rem(2 * n + m, 64) * LANES, LANES)
            tiles.append(jnp.broadcast_to(vec[:, pl.ds(at, LANES)], (8, LANES)))
        small[rows, :] = jnp.concatenate((pos[rows, :], jnp.concatenate(tiles, axis=0)), axis=1).astype(bf16)

    @pl.loop(0, 4)
    def _(n):
        rows = pl.ds(pl.multiple_of(n * 256, 256), 256)
        total = jnp.zeros((TOK, 256), f32)
        for t in range(3):
            for ref, side in ((g_keep, p), (g_send, 1 - p)):
                cols = pl.ds(pl.multiple_of(t * D + side * half, half), half)
                total = total + mm_tb(ref[:, t * half : (t + 1) * half], wqkv[rows, cols])
        branch[:, rows] = total.astype(bf16)

    give_back(1, branch[...])
    for copy in stores:
        copy.wait()


def weight_grad_kernel(mixed, x, mixed_other, x_other, keep, gp_other, q_other, k_other, v_other, out):
    half = D // 2
    a = jnp.concatenate((x[...], x_other[...]), axis=0)
    for t, ref in enumerate((q_other, k_other, v_other)):
        g = jnp.concatenate((keep[:, (t + 1) * half : (t + 2) * half], ref[...]), axis=0)
        out[:, t * half : (t + 1) * half] = mm_ta(a, g).astype(bf16)
    a = jnp.concatenate((mixed[...], mixed_other[...]), axis=0)
    g = jnp.concatenate((keep[:, 0:half], gp_other[...]), axis=0)
    out[:, 3 * half : 4 * half] = mm_ta(a, g).astype(bf16)


def fold_kernel(got, part, part_out, spread_small, sem):
    devices, rows, _ = got.shape
    small = jnp.sum(got[...].astype(f32), axis=0)
    spread_small[...] = jnp.broadcast_to(small[None], (devices, rows, EXTRA)).reshape(D, EXTRA).astype(bf16)
    copy = pltpu.make_async_copy(spread_small, part_out.at[:, pl.ds(2 * D, EXTRA)], sem)
    copy.start()
    copy.wait()


def last_kernel(got, qkv_out, proj_out, pos_out, qkv_bias, proj_bias, gain, shift, scale, total, small):
    half = D // 2
    step = pl.program_id(0)
    pairs, _, rows, _ = got.shape
    count = 2 * pairs * rows

    @pl.when(step == 0)
    def _():
        total[...] = jnp.zeros_like(total)

    for side in range(2):
        total[side] += jnp.sum(got[:, side, :, 0 : 4 * half].astype(f32), axis=0)
    here = got[:, :, :, 4 * half :].astype(f32).reshape(count, EXTRA)
    small[pl.ds(pl.multiple_of(step * count, count), count), :] = here

    @pl.when(step == pl.num_programs(0) - 1)
    def _():
        for side in range(2):
            for t in range(3):
                first = t * D + side * half
                qkv_out[:, first : first + half] = total[side, :, t * half : (t + 1) * half]
            proj_out[:, side * half : (side + 1) * half] = total[side, :, 3 * half :]
        folded = small[:, 0:LANES].reshape(HEADS, WIN2 // 2, LANES)
        pos_out[:, 0 : WIN2 // 2, :] = folded[:, :, 0:WIN2]
        pos_out[:, WIN2 // 2 :, :] = folded[:, :, WIN2:]
        first = 0
        for ref in (qkv_bias, proj_bias, gain, shift):
            for n in range(ref.shape[0] // LANES):
                ref[n * LANES : (n + 1) * LANES] = small[8 * (first + n), LANES:]
            first += ref.shape[0] // LANES
        lane = lax.broadcasted_iota(jnp.int32, (1, LANES), 1)
        heads = jnp.zeros((1, LANES), f32)
        for n in range(HEADS // 2):
            pair = small[8 * (first + n) : 8 * (first + n) + 1, LANES:]
            heads = jnp.where(lane == 2 * n, jnp.sum(pair[:, :WIN2], axis=1, keepdims=True), heads)
            heads = jnp.where(lane == 2 * n + 1, jnp.sum(pair[:, WIN2:], axis=1, keepdims=True), heads)
        scale[...] = heads[0, :HEADS]


def finish_kernel(tok, cot, own, row, col, cor, spread, block_out, grad_tokens):
    for n, (base, out) in enumerate(((tok, block_out), (cot, grad_tokens))):
        border = jnp.concatenate((row[n], col[n], cor[n]), axis=0)
        moved = own[n].astype(f32) + mm(spread[...], border)
        out[...] = (base[...].astype(f32) + moved).astype(bf16)


def sds(shape, dtype):
    return jax.ShapeDtypeStruct(shape, dtype)


VM = pl.BlockSpec(memory_space=pltpu.VMEM)
SM = pl.BlockSpec(memory_space=pltpu.SMEM)
ANY = pl.BlockSpec(memory_space=pl.ANY)


def call(kernel, outs, scratch=(), specs=None, flops=0, bytes_accessed=0, out_specs=None):
    return pl.pallas_call(
        kernel,
        out_shape=outs,
        in_specs=specs,
        out_specs=out_specs or jax.tree.map(lambda _: VM, outs),
        scratch_shapes=list(scratch),
        compiler_params=pltpu.CompilerParams(vmem_limit_bytes=VMEM_LIMIT),
        cost_estimate=pl.CostEstimate(flops=flops, bytes_accessed=bytes_accessed, transcendentals=0),
    )


def neighbour(by_row, by_col):
    rows, cols = lax.axis_size("row"), lax.axis_size("col")
    reps = lax.axis_size("rep")
    pairs = []
    for s in range(reps):
        for r in range(rows):
            for c in range(cols):
                to = (s * rows + (r + by_row) % rows) * cols + (c + by_col) % cols
                pairs.append(((s * rows + r) * cols + c, to))
    return pairs


def per_device(
    tokens, cotangent, row_field, col_field, qkv_weight, qkv_bias, logit_scale, position_bias,
    proj_weight, proj_bias, norm_gain, norm_shift,
):
    devices = lax.axis_size(AXES)
    order = jnp.asarray(window_order(), bf16)
    order_t = jnp.asarray(window_order().T, bf16)
    spread = jnp.asarray(border_spread(), bf16)
    spread_t = jnp.asarray(border_spread().T, bf16)
    mask = jnp.asarray(head_mask(), bf16)
    ones = jnp.asarray(head_sums(), bf16)
    tok = tokens[0].reshape(TOK, D)
    cot = cotangent[0].reshape(TOK, D)

    row_in, col_in, cor_in = call(
        pack_kernel, (sds((2, HALO, D), bf16), sds((2, HALO, D), bf16), sds((2, CORNER, D), bf16)), (), [VM] * 3,
        flops=10**8, bytes_accessed=2**21,
    )(tok, cot, spread_t)
    row_in = lax.ppermute(row_in, AXES, neighbour(-1, 0))
    col_in = lax.ppermute(col_in, AXES, neighbour(0, -1))
    cor_in = lax.ppermute(cor_in, AXES, neighbour(-1, -1))

    col_index = lax.axis_index("col")
    place = jnp.stack((lax.axis_index("row") * SIDE, col_index * SIDE, col_index % 2)).astype(jnp.int32)
    bias_t = position_bias.reshape(GROUPS, GROUP, WIN2, WIN2).transpose(0, 3, 1, 2).reshape(GROUPS, WIN2, WIDE)

    send, keep, own, row, col, cor, small = call(
        local_kernel,
        (
            sds((TOK, 4 * D), bf16), sds((TOK, 2 * D), bf16),
            sds((2, TOK, D), bf16), sds((2, HALO, D), bf16), sds((2, HALO, D), bf16), sds((2, CORNER, D), bf16),
            sds((D, EXTRA), bf16),
        ),
        [
            pltpu.VMEM((D, 3 * D), bf16), pltpu.VMEM((D, D), bf16), pltpu.VMEM((GROUPS, WIN2, WIDE), f32),
            pltpu.VMEM((CAT, D), bf16), pltpu.VMEM((TOK, 3 * D), bf16),
            pltpu.VMEM((GROUPS, WINDOWS, WIN2, WIDE), bf16), pltpu.VMEM((GROUPS, WINDOWS, WIN2, WIDE), f32),
            pltpu.VMEM((2, TOK, D), bf16), pltpu.VMEM((2, TOK, D), f32), pltpu.VMEM((TOK, D), bf16),
            pltpu.VMEM((TOK, D), f32), pltpu.VMEM((TOK, D), bf16), pltpu.VMEM((HEADS * 32, LANES), f32),
            pltpu.VMEM((1, 8 * D), f32), pltpu.VMEM((TOK, D), bf16), pltpu.VMEM((TOK, D), bf16),
            pltpu.VMEM((TOK, D // 2), bf16), pltpu.VMEM((TOK, D // 2), bf16), pltpu.VMEM((TOK, 3 * D // 2), bf16),
            pltpu.VMEM((TOK, 3 * D // 2), bf16), pltpu.VMEM((2, CAT, D), bf16),
            pltpu.SemaphoreType.DMA((5,)), pltpu.SemaphoreType.DMA((14,)),
        ],
        [SM] * 4 + [VM] * 9 + [ANY, VM, ANY, ANY, VM, VM, VM],
        flops=5 * 10**9, bytes_accessed=20 * 2**20, out_specs=(ANY,) * 6 + (VM,),
    )(
        place, row_field, col_field, logit_scale, tok, cot, row_in, col_in, cor_in, order, order_t, mask, ones,
        qkv_weight, qkv_bias.reshape(1, -1), bias_t, proj_weight, proj_bias.reshape(1, -1),
        norm_gain.reshape(1, -1), norm_shift.reshape(1, -1),
    )
    col_size = lax.axis_size("col")
    cores = [(i, i ^ 1) for i in range(col_size)]
    other = lax.ppermute(send, "col", cores)
    rows = D // devices
    small = lax.all_to_all(small.reshape(devices, rows, EXTRA), AXES, 0, 0, tiled=True)
    row = lax.ppermute(row, AXES, neighbour(1, 0))
    col = lax.ppermute(col, AXES, neighbour(0, 1))
    cor = lax.ppermute(cor, AXES, neighbour(1, 1))
    block = D // 2

    def columns(first, moving):
        return pl.BlockSpec((TOK, block), lambda i: (0, first + (i if moving else 0)))

    part = pl.pallas_call(
        weight_grad_kernel,
        grid=(2,),
        out_shape=sds((D, 2 * D + EXTRA), bf16),
        in_specs=[
            columns(0, True), columns(3, True), columns(0, True), columns(3, True),
            pl.BlockSpec((TOK, 2 * D), lambda i: (0, 0)),
            columns(2, False), columns(5, False), columns(6, False), columns(7, False),
        ],
        out_specs=pl.BlockSpec((block, 2 * D + EXTRA), lambda i: (i, 0)),
        compiler_params=pltpu.CompilerParams(vmem_limit_bytes=VMEM_LIMIT),
        cost_estimate=pl.CostEstimate(flops=8 * TOK * D * D, bytes_accessed=8 * 2**20, transcendentals=0),
    )(send, send, other, other, keep, other, other, other, other)
    part, small = lax.optimization_barrier((part, small))
    part = pl.pallas_call(
        fold_kernel,
        out_shape=sds(part.shape, bf16),
        in_specs=[VM, ANY],
        out_specs=ANY,
        scratch_shapes=[pltpu.VMEM((D, EXTRA), bf16), pltpu.SemaphoreType.DMA],
        input_output_aliases={1: 0},
        compiler_params=pltpu.CompilerParams(vmem_limit_bytes=VMEM_LIMIT),
        cost_estimate=pl.CostEstimate(flops=10**6, bytes_accessed=2**20, transcendentals=0),
    )(small, part)
    part, row, col, cor = lax.optimization_barrier((part, row, col, cor))
    got = lax.all_to_all(part.reshape(devices, rows, -1), AXES, 0, 0, tiled=True)
    block_out, grad_tokens = call(
        finish_kernel, (sds((TOK, D), bf16), sds((TOK, D), bf16)), (), [VM] * 7, flops=10**8, bytes_accessed=2**22
    )(tok, cot, own, row, col, cor, spread)
    steps = 4
    outs = (
        sds((rows, 3 * D), f32), sds((rows, D), f32), sds((HEADS, WIN2, WIN2), f32), sds((3 * D,), f32), sds((D,), f32),
        sds((D,), f32), sds((D,), f32), sds((HEADS,), f32),
    )
    grad_qkv_weight, grad_proj_weight, grad_position, g_qkv_bias, g_proj_bias, g_gain, g_shift, g_scale = pl.pallas_call(
        last_kernel,
        grid=(steps,),
        out_shape=outs,
        in_specs=[pl.BlockSpec((devices // 2 // steps, 2, rows, got.shape[2]), lambda i: (i, 0, 0, 0))],
        out_specs=tuple(pl.BlockSpec(o.shape, lambda i, n=len(o.shape): (0,) * n) for o in outs),
        scratch_shapes=[pltpu.VMEM((2, rows, 2 * D), f32), pltpu.VMEM((D, EXTRA), f32)],
        compiler_params=pltpu.CompilerParams(vmem_limit_bytes=VMEM_LIMIT),
        cost_estimate=pl.CostEstimate(flops=10**7, bytes_accessed=2**22, transcendentals=0),
    )(got.reshape(devices // 2, 2, rows, -1))
    return (
        block_out.reshape(1, SIDE, SIDE, D), grad_tokens.reshape(1, SIDE, SIDE, D), grad_qkv_weight, grad_proj_weight, g_qkv_bias, g_proj_bias,
        g_gain, g_shift, g_scale, grad_position,
    )


def solution(mesh):
    grid = P("rep", "row", "col", None)
    rows = P(AXES, None)
    return jax.shard_map(
        per_device,
        mesh=mesh,
        in_specs=(grid, grid, P("rep", None), P("rep", None)) + (P(),) * 8,
        out_specs=(grid, grid, rows, rows) + (P(),) * 6,
        check_vma=False,
    )
```

time: 156 us -> 145 us (0.929)
  Pallas kernels: 54.9 us -> 50.5 us
  starting transfers between devices: 29.5 us -> 26.2 us
  other arithmetic: 3.86 us -> 0.59 us
  waiting for transfers between devices: 57 us -> 59.6 us
  local copies, waits for them, and re-layouts: 8.94 us -> 6.61 us
    pallas_call x6 -> x5, Pallas kernels: 52.6 us -> 48.2 us  [the longest x1 31.9 us: per_device(): call(local_kernel, (sds((TOK, 4 * D), bf16), sds((TOK, 2 * D), bf16), sds...]
    all_to_all x2, waiting for transfers between devices: 56.2 us -> 59.5 us  [the longest x1 55.2 us: per_device(): lax.all_to_all(part.reshape(devices, rows, -1), AXES, 0, 0, tiled=True)]
    ppermute x7 -> x4, starting transfers between devices: 4.84 us -> 2.41 us  [the longest x1 1.09 us: per_device(): col = lax.ppermute(col, AXES, neighbour(0, 1))]
    convert_element_type x2 -> x0, other arithmetic: 1.91 us -> none  [the longest x1 0.98 us: per_device(): grad_position = grad_position.reshape(HEADS, WIN2, WIN2).astype(f32)]
    convert_element_type x2 -> x0, local copies, waits for them, and re-layouts: 1.71 us -> none  [per_device(): grad_position = grad_position.reshape(HEADS, WIN2, WIN2).astype(f32)]
    unnamed x20 -> x16, local copies, waits for them, and re-layouts: 2.9 us -> 3.57 us
  transfers between devices with their start and end apart: 12 -> 9, of which waited for: 3 -> 3; matrix products, arithmetic and copies ran while one was open for 3% -> 3% of each run, Pallas kernels for 12% -> 8%
where the time goes in v3:
time: 145 us; the launch traced here: 144 us
  waiting for transfers between devices  59.6 us (41%)
  Pallas kernels  50.5 us (35%)
  starting transfers between devices  26.2 us (18%)
  local copies, waits for them, and re-layouts  6.61 us (5%)
    all_to_all x1, waiting for transfers between devices, per_device(): lax.all_to_all(part.reshape(devices, rows, -1), AXES, 0, 0, tiled=True)  55.2 us
    pallas_call x1, Pallas kernels, per_device(): call(local_kernel, (sds((TOK, 4 * D), bf16), sds((TOK, 2 * D), bf16), sds...  31.9 us
    all_to_all x1, starting transfers between devices, per_device(): lax.all_to_all(small.reshape(devices, rows, EXTRA), AXES, 0, 0, tiled=True)  10.5 us
    all_to_all x1, starting transfers between devices, per_device(): lax.all_to_all(part.reshape(devices, rows, -1), AXES, 0, 0, tiled=True)  6.43 us
    pallas_call x1, Pallas kernels, per_device(): pl.pallas_call(weight_grad_kernel, grid=(2,), out_shape=sds((D, 2 * D + E...  6.02 us
    pallas_call x1, Pallas kernels, per_device(): pl.pallas_call(last_kernel, grid=(steps,), out_shape=outs, in_specs=[pl.B...  5.28 us
    ppermute x1, starting transfers between devices, per_device(): col_in = lax.ppermute(col_in, AXES, neighbour(0, -1))  4.37 us
    all_to_all x1, waiting for transfers between devices, per_device(): lax.all_to_all(small.reshape(devices, rows, EXTRA), AXES, 0, 0, tiled=True)  4.35 us
  transfers between devices with their start and end apart: 9, of which 3 were waited for; matrix products, arithmetic and copies ran while one was open for 3% of the time, Pallas kernels for 8%

profile of v3, /device:TPU:0, one launch (start us, length us, event | category | flops | bytes accessed | tf_op | source)
XLA Modules:
  0.0 144.4 jit_solution(15563347845032734415)
XLA Ops:
  0.6 2.3 %shard_map.249 = (bf16[2,48,1024]{2,1,0:T(8,128)(2,1)}, bf16[2,48,1024]{2,1,0:T(8,128)(2,1)}, bf16[2,16,1024]{2,1,0:T(8,128)(2,1)}) custom-call(bf16[256,1024]{1,0:T(8,128)(2,1)} %bitcast.18, bf16[256,1024]{1,0:T(8,128)(2,1)} %bitcast.21, bf16[112,256]{1,0:T(8,128)(2,1)} %constant.39.clone.spread_t), custom_call_target="tpu_custom_call" | custom-call | flops 100000000 | bytes 2097152 | tf_op jit(solution)/shard_map/pallas_call | solution.py:500
  2.9 2.0 %collective-permute-start = (bf16[2,48,1024]{2,1,0:T(8,128)(2,1)}, bf16[2,48,1024]{2,1,0:T(8,128)(2,1)S(1)}, u32[]{:S(2)}, u32[]{:S(2)}) collective-permute-start(bf16[2,48,1024]{2,1,0:T(8,128)(2,1)} %get-tuple-element.36), channel_id=1, source_target_pairs={{0,32},{1,33},{2,34},{3,35},{4,36},{5,37},{6,38},{7,39},{8,40},{9,... | collective-permute-start | bytes 589832 | tf_op jit(solution)/shard_map/ppermute | solution.py:504
  4.9 4.4 %collective-permute-start.1 = (bf16[2,48,1024]{2,1,0:T(8,128)(2,1)}, bf16[2,48,1024]{2,1,0:T(8,128)(2,1)S(1)}, u32[]{:S(2)}, u32[]{:S(2)}) collective-permute-start(bf16[2,48,1024]{2,1,0:T(8,128)(2,1)} %get-tuple-element.37), channel_id=1, source_target_pairs={{0,31},{1,0},{2,1},{3,2},{4,3},{5,4},{6,5},{7,6},{8,7},{9,8},{10,9... | collective-permute-start | bytes 589832 | tf_op jit(solution)/shard_map/ppermute | solution.py:505
  9.3 0.5 collective-permute-start.2
  9.8 1.6 %copy.29 = f32[8,4,64,64]{2,1,3,0:T(4,128)S(1)} copy(f32[8,4,64,64]{3,2,1,0:T(8,128)} %bitcast.24) | data formatting | bytes 1048576 | tf_op jit(solution)/shard_map/reshape | solution.py:510
  11.4 1.4 reshape.55.bias_hbm
  12.8 0.6 pad_add_fusion.place
  13.5 0.6 copy-done.7
  14.3 31.9 %shard_map.250 = (bf16[256,4096]{1,0:T(8,128)(2,1)}, bf16[256,2048]{1,0:T(8,128)(2,1)}, bf16[2,256,1024]{2,1,0:T(8,128)(2,1)}, bf16[2,48,1024]{2,1,0:T(8,128)(2,...) custom-call(s32[3]{0:T(128)} %pad_add_fusion.place, s32[1,32]{1,0:T(1,128)} %row_field.1, ...), custom_call_target="tpu_custom_call" | custom-call | flops 5000000000 | bytes 20971520 | tf_op jit(solution)/shard_map/pallas_call | solution.py:512
  46.2 0.1 collective-permute-start.3
  46.3 10.5 %all-to-all-start = ((bf16[128,8,256]{2,1,0:T(8,128)(2,1)}), bf16[128,8,256]{2,1,0:T(8,128)(2,1)S(1)}, u32[]{:S(2)}, u32[]{:S(2)}) async-start(bf16[128,8,256]{2,1,0:T(8,128)(2,1)} %bitcast.25), calls=%async_computation | async-start | bytes 1048576 | tf_op jit(solution)/shard_map/all_to_all | solution.py:541
  56.7 0.9 collective-permute-start.6
  57.6 0.3 collective-permute-start.4
  58.0 1.1 collective-permute-start.5
  59.1 1.3 copy-done
  60.4 6.0 %shard_map.251.part = bf16[1024,2304]{1,0:T(8,128)(2,1)} custom-call(bf16[256,4096]{1,0:T(8,128)(2,1)} %get-tuple-element.40.mixed.x, bf16[256,4096]{1,0:T(8,128)(2,1)} %get-tuple-element.40.mixed.x, bf16[256,4096]{1,0:T(8,128)(2,1)} %copy-done, bf16[256,4096]{1,0:T(8,128)(2,1)} %copy-done, bf16[256,2048]{1,0:T(8,128)(2,1)} %get-tuple-element.41.keep, ...), custom_call_target="tpu_custom_call" | custom-call | flops 2147483648 | bytes 8388608 | tf_op jit(solution)/shard_map/pallas_call | solution.py:550
  66.4 4.4 %all-to-all-done.got = bf16[128,8,256]{2,1,0:T(8,128)(2,1)S(1)} async-done(((bf16[128,8,256]{2,1,0:T(8,128)(2,1)}), bf16[128,8,256]{2,1,0:T(8,128)(2,1)S(1)}, u32[]{:S(2)}, u32[]{:S(2)}) %all-to-all-start) | async-done | bytes 524320 | tf_op jit(solution)/shard_map/all_to_all | solution.py:541
  70.7 0.8 copy-done.1
  71.5 2.1 %shard_map.252 = bf16[1024,2304]{1,0:T(8,128)(2,1)} custom-call(bf16[128,8,256]{2,1,0:T(8,128)(2,1)} %copy-done.1, bf16[1024,2304]{1,0:T(8,128)(2,1)} %shard_map.251.part), custom_call_target="tpu_custom_call", output_to_operand_aliasing={{}: (1, {})} | custom-call | flops 1000000 | bytes 1048576 | tf_op jit(solution)/shard_map/pallas_call | solution.py:564
  73.7 0.6 copy-done.4
  74.4 6.4 %all-to-all-start.1 = ((bf16[128,8,2304]{2,1,0:T(8,128)(2,1)}), bf16[128,8,2304]{2,1,0:T(8,128)(2,1)}, u32[]{:S(2)}, u32[]{:S(2)}) async-start(bf16[128,8,2304]{2,1,0:T(8,128)(2,1)} %bitcast.16), calls=%async_computation.1 | async-start | bytes 9437184 | tf_op jit(solution)/shard_map/all_to_all | solution.py:575
  80.8 2.9 %shard_map.253 = (bf16[256,1024]{1,0:T(8,128)(2,1)}, bf16[256,1024]{1,0:T(8,128)(2,1)}) custom-call(bf16[256,1024]{1,0:T(8,128)(2,1)} %bitcast.20, bf16[256,1024]{1,0:T(8,128)(2,1)} %bitcast.23, bf16[2,256,1024]{2,1,0:T(8,128)(2,1)} %get-tuple-element.39.own, bf16[2,48,1024]{2,1,0:T(8,128)(2,1)} %copy-done.2, bf16[2,48,1024]{2,1,0:T(8,128)(2,1)} %copy-done.3, ...), custom_call_target="tpu_custom_call" | custom-call | flops 100000000 | bytes 4194304 | tf_op jit(solution)/shard_map/pallas_call | solution.py:576
  83.8 55.2 %all-to-all-done.1 = bf16[128,8,2304]{2,1,0:T(8,128)(2,1)} async-done(((bf16[128,8,2304]{2,1,0:T(8,128)(2,1)}), bf16[128,8,2304]{2,1,0:T(8,128)(2,1)}, u32[]{:S(2)}, u32[]{:S(2)}) %all-to-all-start.1) | async-done | bytes 4718624 | tf_op jit(solution)/shard_map/all_to_all | solution.py:575
  138.9 5.3 %shard_map.254 = (f32[8,3072]{1,0:T(8,128)}, f32[8,1024]{1,0:T(8,128)}, f32[32,64,64]{2,1,0:T(8,128)}, f32[3072]{0:T(1024)}, f32[1024]{0:T(1024)}, /*index=5*/f32[1024]{0:T(1024)}, f32[1024]{0:T(1024)}, f32[32]{0:T(128)}) custom-call(bf16[64,2,8,2304]{3,2,1,0:T(8,128)(2,1)} %bitcast.15.got), custom_call_target="tpu_custom_call" | custom-call | flops 10000000 | bytes 4194304 | tf_op jit(solution)/shard_map/pallas_call | solution.py:584
  (19 shorter events, 0.4 us)
Async XLA Ops:
  2.9 10.6 %collective-permute-start = (bf16[2,48,1024]{2,1,0:T(8,128)(2,1)}, bf16[2,48,1024]{2,1,0:T(8,128)(2,1)S(1)}, u32[]{:S(2)}, u32[]{:S(2)}) collective-permute-start(bf16[2,48,1024]{2,1,0:T(8,128)(2,1)} %get-tuple-element.36), channel_id=1, source_target_pairs={{0,32},{1,33},{2,34},{3,35},{4,36},{5,37},{6,38},{7,39},{8,40},{9,... | collective-permute-start | bytes 589832 | tf_op jit(solution)/shard_map/ppermute | solution.py:504
  4.9 8.6 %collective-permute-start.1 = (bf16[2,48,1024]{2,1,0:T(8,128)(2,1)}, bf16[2,48,1024]{2,1,0:T(8,128)(2,1)S(1)}, u32[]{:S(2)}, u32[]{:S(2)}) collective-permute-start(bf16[2,48,1024]{2,1,0:T(8,128)(2,1)} %get-tuple-element.37), channel_id=1, source_target_pairs={{0,31},{1,0},{2,1},{3,2},{4,3},{5,4},{6,5},{7,6},{8,7},{9,8},{10,9... | collective-permute-start | bytes 589832 | tf_op jit(solution)/shard_map/ppermute | solution.py:505
  9.3 4.2 %collective-permute-start.2 = (bf16[2,16,1024]{2,1,0:T(8,128)(2,1)}, bf16[2,16,1024]{2,1,0:T(8,128)(2,1)S(1)}, u32[]{:S(2)}, u32[]{:S(2)}) collective-permute-start(bf16[2,16,1024]{2,1,0:T(8,128)(2,1)} %get-tuple-element.38), channel_id=1, source_target_pairs={{0,63},{1,32},{2,33},{3,34},{4,35},{5,36},{6,37},{7,38},{8,39},{9,... | collective-permute-start | bytes 196616 | tf_op jit(solution)/shard_map/ppermute | solution.py:506
  13.5 0.6 copy-start.7
  13.5 0.7 copy-start.5
  13.5 0.8 copy-start.6
  46.2 12.9 %collective-permute-start.3 = (bf16[256,4096]{1,0:T(8,128)(2,1)}, bf16[256,4096]{1,0:T(8,128)(2,1)S(1)}, u32[]{:S(2)}, u32[]{:S(2)}) collective-permute-start(bf16[256,4096]{1,0:T(8,128)(2,1)} %get-tuple-element.40.mixed.x), channel_id=1, source_target_pairs={{0,1},{1,0},{2,3},{3,2},{4,5},{5,4},{6,7},{7,6},{8,9},{9,8},{10,11... | collective-permute-start | bytes 6291464 | tf_op jit(solution)/shard_map/ppermute | solution.py:539
  46.3 24.5 %all-to-all-start = ((bf16[128,8,256]{2,1,0:T(8,128)(2,1)}), bf16[128,8,256]{2,1,0:T(8,128)(2,1)S(1)}, u32[]{:S(2)}, u32[]{:S(2)}) async-start(bf16[128,8,256]{2,1,0:T(8,128)(2,1)} %bitcast.25), calls=%async_computation | async-start | bytes 1048576 | tf_op jit(solution)/shard_map/all_to_all | solution.py:541
  56.7 16.9 %collective-permute-start.6 = (bf16[2,16,1024]{2,1,0:T(8,128)(2,1)}, bf16[2,16,1024]{2,1,0:T(8,128)(2,1)S(1)}, u32[]{:S(2)}, u32[]{:S(2)}) collective-permute-start(bf16[2,16,1024]{2,1,0:T(8,128)(2,1)} %get-tuple-element.47), channel_id=1, source_target_pairs={{0,33},{1,34},{2,35},{3,36},{4,37},{5,38},{6,39},{7,40},{8,41},{9,... | collective-permute-start | bytes 196616 | tf_op jit(solution)/shard_map/ppermute | solution.py:544
  57.6 16.0 %collective-permute-start.4 = (bf16[2,48,1024]{2,1,0:T(8,128)(2,1)}, bf16[2,48,1024]{2,1,0:T(8,128)(2,1)S(1)}, u32[]{:S(2)}, u32[]{:S(2)}) collective-permute-start(bf16[2,48,1024]{2,1,0:T(8,128)(2,1)} %get-tuple-element.45), channel_id=1, source_target_pairs={{0,32},{1,33},{2,34},{3,35},{4,36},{5,37},{6,38},{7,39},{8,40},{9,... | collective-permute-start | bytes 589832 | tf_op jit(solution)/shard_map/ppermute | solution.py:542
  58.0 15.7 %collective-permute-start.5 = (bf16[2,48,1024]{2,1,0:T(8,128)(2,1)}, bf16[2,48,1024]{2,1,0:T(8,128)(2,1)S(1)}, u32[]{:S(2)}, u32[]{:S(2)}) collective-permute-start(bf16[2,48,1024]{2,1,0:T(8,128)(2,1)} %get-tuple-element.46), channel_id=1, source_target_pairs={{0,1},{1,2},{2,3},{3,4},{4,5},{5,6},{6,7},{7,8},{8,9},{9,10},{10,1... | collective-permute-start | bytes 589832 | tf_op jit(solution)/shard_map/ppermute | solution.py:543
  59.1 1.3 copy-start
  70.7 0.8 copy-start.1
  73.6 0.6 copy-start.4
  73.6 0.7 copy-start.2
  73.7 0.7 copy-start.3
  74.4 64.6 %all-to-all-start.1 = ((bf16[128,8,2304]{2,1,0:T(8,128)(2,1)}), bf16[128,8,2304]{2,1,0:T(8,128)(2,1)}, u32[]{:S(2)}, u32[]{:S(2)}) async-start(bf16[128,8,2304]{2,1,0:T(8,128)(2,1)} %bitcast.16), calls=%async_computation.1 | async-start | bytes 9437184 | tf_op jit(solution)/shard_map/all_to_all | solution.py:575

commit v4 on v3

--- a/solution.py
+++ b/solution.py
@@ -24,7 +24,7 @@
 GROUPS = HEADS // GROUP
 LANES = 128
 WIDE = GROUP * WIN2
-FUSED = 4
+FUSED = 8
 EXTRA = 2 * LANES
 AXES = ("rep", "row", "col")
 
@@ -99,6 +99,11 @@
     return jnp.concatenate((x, x, x, x), axis=0) * mask
 
 
+def in_step(parts):
+    while parts:
+        parts = [part for part in parts if next(part, parts) is not parts]
+
+
 def split_border(border, n, row, col, cor):
     row[n] = border[:HALO]
     col[n] = border[HALO : 2 * HALO]
@@ -185,6 +190,8 @@
             out = jnp.where(head_lane == h, full[h * WIN2 : (h + 1) * WIN2], out)
         return out
 
+    window_rows = [slice(w * WIN2, (w + 1) * WIN2) for w in range(WINDOWS)]
+
     def scale_of(g):
         out = jnp.zeros((1, WIDE), f32)
         for h in range(GROUP):
@@ -204,42 +211,35 @@
     def attend(g):
         at = pl.multiple_of(g * LANES, LANES)
         qs = pl.ds(at, LANES)
-        q = qkv[:, qs].astype(f32)
-        k = qkv[:, pl.ds(at + D, LANES)].astype(f32)
         v = qkv[:, pl.ds(at + 2 * D, LANES)]
+        raw = jnp.concatenate((qkv[:, qs], qkv[:, pl.ds(at + D, LANES)]), axis=1).astype(f32)
+        total = exact_sums(raw * raw, ones)
+        yield
+        inv = lax.rsqrt(jnp.maximum(total, unit_floor * unit_floor))
+        unit = (raw * inv).astype(bf16)
+        qu, ku = unit[:, :LANES], unit[:, LANES:]
+        cosines = [mm_tb(ku[rows], stacked_heads(qu[rows], mask)) for rows in window_rows]
+        yield
         sc = scale_of(g)
         bias = bias_t[g]
-        raw = jnp.concatenate((q, k), axis=1)
-        inv = lax.rsqrt(jnp.maximum(exact_sums(raw * raw, ones), unit_floor * unit_floor))
-        unit = (raw * inv).astype(bf16)
-        q_inv, k_inv, qu, ku = inv[:, :LANES], inv[:, LANES:], unit[:, :LANES], unit[:, LANES:]
-        cosines, attentions, mixed_parts = [], [], []
+        attentions = []
         for w in range(WINDOWS):
-            rows = slice(w * WIN2, (w + 1) * WIN2)
-            cosine = mm_tb(ku[rows], stacked_heads(qu[rows], mask))
-            weights = jnp.exp(sc * cosine + bias) * allowed[w]
+            weights = jnp.exp(sc * cosines[w] + bias) * allowed[w]
             total = jnp.sum(weights, axis=0, keepdims=True)
-            attention = (weights * (1.0 / total)).astype(bf16)
-            cosines.append(cosine)
-            attentions.append(attention)
-            mixed_parts.append(pick_heads(mm_ta(attention, v[rows])).astype(bf16))
-
-        def store():
-            inverses[0, :, qs] = q_inv
-            inverses[1, :, qs] = k_inv
-            units[0, :, qs] = qu
-            units[1, :, qs] = ku
-            for w in range(WINDOWS):
-                att[g, w] = attentions[w]
-                cos[g, w] = cosines[w]
-            mixed[:, qs] = jnp.concatenate(mixed_parts, axis=0)
-
-        return store
+            attentions.append((weights * (1.0 / total)).astype(bf16))
+        products = [mm_ta(attentions[w], v[window_rows[w]]) for w in range(WINDOWS)]
+        yield
+        for n in range(2):
+            inverses[n, :, qs] = inv[:, n * LANES : (n + 1) * LANES]
+            units[n, :, qs] = unit[:, n * LANES : (n + 1) * LANES]
+        for w in range(WINDOWS):
+            att[g, w] = attentions[w]
+            cos[g, w] = cosines[w]
+        mixed[:, qs] = jnp.concatenate([pick_heads(product).astype(bf16) for product in products], axis=0)
 
     @pl.loop(0, GROUPS // FUSED)
     def _(n):
-        for store in [attend(n * FUSED + u) for u in range(FUSED)]:
-            store()
+        in_step([attend(n * FUSED + u) for u in range(FUSED)])
 
     write(mixed, send.at[:, pl.ds(0, D)])
     loads[4].wait()
@@ -251,25 +251,21 @@
 
     gain_v = gain[...]
     shift_v = shift[...]
-    vec[...] = jnp.zeros_like(vec)
-
-    @pl.loop(0, TOK // 32)
-    def _(n):
-        rows = pl.ds(pl.multiple_of(n * 32, 32), 32)
-        projected = wide[rows, :]
-        centre = projected - jnp.mean(projected, axis=-1, keepdims=True)
-        inv_std = lax.rsqrt(jnp.mean(centre * centre, axis=-1, keepdims=True) + norm_epsilon)
-        normed = centre * inv_std
-        branch[rows, :] = (normed * gain_v + shift_v).astype(bf16)
-        go = grad[rows, :].astype(f32)
-        gn = go * gain_v
-        gpf = inv_std * (
-            gn - jnp.mean(gn, axis=-1, keepdims=True) - normed * jnp.mean(gn * normed, axis=-1, keepdims=True)
-        )
-        grad[rows, :] = gpf.astype(bf16)
-        vec[:, 3 * D : 4 * D] += jnp.sum(gpf, axis=0, keepdims=True)
-        vec[:, 4 * D : 5 * D] += jnp.sum(go * normed, axis=0, keepdims=True)
-        vec[:, 5 * D : 6 * D] += jnp.sum(go, axis=0, keepdims=True)
+
+    projected = wide[...]
+    centre = projected - jnp.mean(projected, axis=-1, keepdims=True)
+    inv_std = lax.rsqrt(jnp.mean(centre * centre, axis=-1, keepdims=True) + norm_epsilon)
+    normed = centre * inv_std
+    branch[...] = (normed * gain_v + shift_v).astype(bf16)
+    go = grad[...].astype(f32)
+    gn = go * gain_v
+    gpf = inv_std * (
+        gn - jnp.mean(gn, axis=-1, keepdims=True) - normed * jnp.mean(gn * normed, axis=-1, keepdims=True)
+    )
+    grad[...] = gpf.astype(bf16)
+    vec[:, 3 * D : 4 * D] = jnp.sum(gpf, axis=0, keepdims=True)
+    vec[:, 4 * D : 5 * D] = jnp.sum(go * normed, axis=0, keepdims=True)
+    vec[:, 5 * D : 6 * D] = jnp.sum(go, axis=0, keepdims=True)
 
     gp_keep[...] = grad[:, pl.ds(pl.multiple_of(p * half, half), half)]
     gp_send[...] = grad[:, pl.ds(pl.multiple_of((1 - p) * half, half), half)]
@@ -297,70 +293,64 @@
         qu = units[0, :, qs]
         ku = units[1, :, qs]
         gmx = branch[:, qs]
+        both = [
+            stacked_heads(jnp.concatenate((gmx[rows], qu[rows]), axis=1), mask_pair) for rows in window_rows
+        ]
+        grad_atts = [mm_tb(v[window_rows[w]], both[w][:, :LANES]) for w in range(WINDOWS)]
+        yield
         sc = scale_of(g)
-        attentions = [att[g, w] for w in range(WINDOWS)]
-        cosines = [cos[g, w] for w in range(WINDOWS)]
-        invs = [inverses[n, :, qs] for n in range(2)]
-        raws = [qkv[:, pl.ds(at + n * D, LANES)] for n in range(2)]
         pos_sum = jnp.zeros((WIN2, WIDE), f32)
         sc_sum = jnp.zeros((WIN2, WIDE), f32)
-        gqu, gku, gv = [], [], []
+        pairs, products = [], []
         for w in range(WINDOWS):
-            rows = slice(w * WIN2, (w + 1) * WIN2)
-            both = stacked_heads(jnp.concatenate((gmx[rows], qu[rows]), axis=1), mask_pair)
-            grad_att = mm_tb(v[rows], both[:, :LANES])
-            attention = attentions[w]
+            attention = att[g, w]
             att_f = attention.astype(f32)
-            dots = jnp.sum(grad_att * att_f, axis=0, keepdims=True)
-            grad_scores = att_f * (grad_att - dots)
+            dots = jnp.sum(grad_atts[w] * att_f, axis=0, keepdims=True)
+            grad_scores = att_f * (grad_atts[w] - dots)
             pos_sum = pos_sum + grad_scores
-            sc_sum = sc_sum + grad_scores * cosines[w]
+            sc_sum = sc_sum + grad_scores * cos[g, w]
             grad_cos = (sc * grad_scores).astype(bf16)
-            pair = mm(jnp.concatenate((attention, grad_cos), axis=0), both)
-            gv.append(pair[:WIN2, :LANES])
-            gku.append(pair[WIN2:, LANES:])
-            gqu.append(own_heads(mm_ta(ku[rows], grad_cos), f32))
+            pairs.append(mm(jnp.concatenate((attention, grad_cos), axis=0), both[w]))
+            products.append(mm_ta(ku[window_rows[w]], grad_cos))
+        yield
+        gqu = jnp.concatenate([own_heads(product, f32) for product in products], axis=0)
+        gku = jnp.concatenate([pair[WIN2:, LANES:] for pair in pairs], axis=0)
+        got = jnp.concatenate((gqu, gku), axis=1)
+        inv = jnp.concatenate((inverses[0, :, qs], inverses[1, :, qs]), axis=1)
+        unit = jnp.concatenate((qkv[:, qs], qkv[:, pl.ds(at + D, LANES)]), axis=1).astype(f32) * inv
+        along = mm((got * unit).astype(bf16), ones)
+        yield
+        got = inv * (got - unit * along)
+        results = [got[:, :LANES], got[:, LANES:], jnp.concatenate([pair[:WIN2, :LANES] for pair in pairs], axis=0)]
         turned = pos_sum.T
         pos_parts = []
         for h in range(GROUP):
             upper = turned[h * WIN2 : h * WIN2 + 32]
             lower = turned[h * WIN2 + 32 : (h + 1) * WIN2]
             pos_parts.append(jnp.concatenate((upper, lower), axis=1))
-        got = jnp.concatenate((jnp.concatenate(gqu, axis=0), jnp.concatenate(gku, axis=0)), axis=1)
-        inv = jnp.concatenate(invs, axis=1)
-        unit = jnp.concatenate(raws, axis=1).astype(f32) * inv
-        got = inv * (got - unit * mm((got * unit).astype(bf16), ones))
-        results = [got[:, :LANES], got[:, LANES:]]
-        results.append(jnp.concatenate(gv, axis=0))
-        sums = [jnp.sum(result, axis=0, keepdims=True) for result in results]
-        sc_row = jnp.sum(sc_sum, axis=0, keepdims=True)
+        pos[pl.ds(pl.multiple_of(g * LANES, LANES), LANES), :] = jnp.concatenate(pos_parts, axis=0)
+        vec[:, pl.ds(pl.multiple_of(6 * D + g * WIDE, WIDE), WIDE)] = jnp.sum(sc_sum, axis=0, keepdims=True)
+        for n in range(3):
+            vec[:, pl.ds(at + n * D, LANES)] = jnp.sum(results[n], axis=0, keepdims=True)
         inner = pl.multiple_of(lax.rem(g, GROUPS // 2) * LANES, LANES)
-
-        def store():
-            vec[:, pl.ds(pl.multiple_of(6 * D + g * WIDE, WIDE), WIDE)] = sc_row
-            pos[pl.ds(pl.multiple_of(g * LANES, LANES), LANES), :] = jnp.concatenate(pos_parts, axis=0)
+        yield
+
+        def put(ref):
             for n in range(3):
-                vec[:, pl.ds(at + n * D, LANES)] = sums[n]
-
-            def put(ref):
-                for n in range(3):
-                    ref[:, pl.ds(n * half + inner, LANES)] = results[n].astype(bf16)
-
-            side = g // (GROUPS // 2)
-            pl.when(side == p)(lambda: put(g_keep))
-            pl.when(side != p)(lambda: put(g_send))
-
-        return store
+                ref[:, pl.ds(n * half + inner, LANES)] = results[n].astype(bf16)
+
+        side = g // (GROUPS // 2)
+        pl.when(side == p)(lambda: put(g_keep))
+        pl.when(side != p)(lambda: put(g_send))
 
     @pl.loop(0, GROUPS // FUSED)
     def _(n):
-        for store in [attend_back(n * FUSED + u) for u in range(FUSED)]:
-            store()
+        in_step([attend_back(n * FUSED + u) for u in range(FUSED)])
 
     write(g_keep, keep.at[:, pl.ds(half, 3 * half)])
     write(g_send, send.at[:, pl.ds(5 * half, 3 * half)])
 
-    @pl.loop(0, 64)
+    @pl.loop(0, 64, unroll=8)
     def _(n):
         rows = pl.ds(pl.multiple_of(n * 16, 16), 16)
         tiles = []
@@ -434,12 +424,13 @@
             for n in range(ref.shape[0] // LANES):
                 ref[n * LANES : (n + 1) * LANES] = small[8 * (first + n), LANES:]
             first += ref.shape[0] // LANES
-        lane = lax.broadcasted_iota(jnp.int32, (1, LANES), 1)
-        heads = jnp.zeros((1, LANES), f32)
-        for n in range(HEADS // 2):
-            pair = small[8 * (first + n) : 8 * (first + n) + 1, LANES:]
-            heads = jnp.where(lane == 2 * n, jnp.sum(pair[:, :WIN2], axis=1, keepdims=True), heads)
-            heads = jnp.where(lane == 2 * n + 1, jnp.sum(pair[:, WIN2:], axis=1, keepdims=True), heads)
+        parts = small[8 * first : 8 * first + LANES, LANES:]
+        lane = lax.broadcasted_iota(jnp.int32, (LANES, LANES), 1)
+        at = lax.broadcasted_iota(jnp.int32, (LANES, LANES), 0)
+        left = jnp.sum(parts[:, :WIN2], axis=1, keepdims=True)
+        right = jnp.sum(parts[:, WIN2:], axis=1, keepdims=True)
+        heads = jnp.where(at == lane // 2 * 8, jnp.where(lane % 2 == 0, left, right), 0.0)
+        heads = jnp.sum(heads, axis=0, keepdims=True)
         scale[...] = heads[0, :HEADS]
 
 
@@ -534,8 +525,7 @@
         qkv_weight, qkv_bias.reshape(1, -1), bias_t, proj_weight, proj_bias.reshape(1, -1),
         norm_gain.reshape(1, -1), norm_shift.reshape(1, -1),
     )
-    col_size = lax.axis_size("col")
-    cores = [(i, i ^ 1) for i in range(col_size)]
+    cores = [(i, i ^ 1) for i in range(lax.axis_size("col"))]
     other = lax.ppermute(send, "col", cores)
     rows = D // devices
     small = lax.all_to_all(small.reshape(devices, rows, EXTRA), AXES, 0, 0, tiled=True)
@@ -576,7 +566,7 @@
     block_out, grad_tokens = call(
         finish_kernel, (sds((TOK, D), bf16), sds((TOK, D), bf16)), (), [VM] * 7, flops=10**8, bytes_accessed=2**22
     )(tok, cot, own, row, col, cor, spread)
-    steps = 4
+    steps = 1
     outs = (
         sds((rows, 3 * D), f32), sds((rows, D), f32), sds((HEADS, WIN2, WIN2), f32), sds((3 * D,), f32), sds((D,), f32),
         sds((D,), f32), sds((D,), f32), sds((HEADS,), f32),

time: 145 us -> 132 us (0.910)
  Pallas kernels: 50.5 us -> 37.5 us
    pallas_call x1, Pallas kernels: 31.9 us -> 20.4 us  [per_device(): call(local_kernel, (sds((TOK, 4 * D), bf16), sds((TOK, 2 * D), bf16), sds...]
where the time goes in v4:
time: 132 us; the launch traced here: 131 us
  waiting for transfers between devices  59.6 us (45%)
  Pallas kernels  37.5 us (28%)
  starting transfers between devices  26.2 us (20%)
  local copies, waits for them, and re-layouts  6.61 us (5%)
    all_to_all x1, waiting for transfers between devices, per_device(): lax.all_to_all(part.reshape(devices, rows, -1), AXES, 0, 0, tiled=True)  55.2 us
    pallas_call x1, Pallas kernels, per_device(): call(local_kernel, (sds((TOK, 4 * D), bf16), sds((TOK, 2 * D), bf16), sds...  20.4 us
    all_to_all x1, starting transfers between devices, per_device(): lax.all_to_all(small.reshape(devices, rows, EXTRA), AXES, 0, 0, tiled=True)  10.5 us
    all_to_all x1, starting transfers between devices, per_device(): lax.all_to_all(part.reshape(devices, rows, -1), AXES, 0, 0, tiled=True)  6.43 us
    pallas_call x1, Pallas kernels, per_device(): pl.pallas_call(weight_grad_kernel, grid=(2,), out_shape=sds((D, 2 * D + E...  6.02 us
    ppermute x1, starting transfers between devices, per_device(): col_in = lax.ppermute(col_in, AXES, neighbour(0, -1))  4.37 us
    all_to_all x1, waiting for transfers between devices, per_device(): lax.all_to_all(small.reshape(devices, rows, EXTRA), AXES, 0, 0, tiled=True)  4.35 us
    pallas_call x1, Pallas kernels, per_device(): pl.pallas_call(last_kernel, grid=(steps,), out_shape=outs, in_specs=[pl.B...  3.85 us
  transfers between devices with their start and end apart: 9, of which 3 were waited for; matrix products, arithmetic and copies ran while one was open for 3% of the time, Pallas kernels for 8%

profile of v4, /device:TPU:0, one launch (start us, length us, event | category | flops | bytes accessed | tf_op | source)
XLA Modules:
  0.0 131.2 jit_solution(18002654483783783371)
XLA Ops:
  0.6 2.3 %shard_map.249 = (bf16[2,48,1024]{2,1,0:T(8,128)(2,1)}, bf16[2,48,1024]{2,1,0:T(8,128)(2,1)}, bf16[2,16,1024]{2,1,0:T(8,128)(2,1)}) custom-call(bf16[256,1024]{1,0:T(8,128)(2,1)} %bitcast.18, bf16[256,1024]{1,0:T(8,128)(2,1)} %bitcast.21, bf16[112,256]{1,0:T(8,128)(2,1)} %constant.39.clone.spread_t), custom_call_target="tpu_custom_call" | custom-call | flops 100000000 | bytes 2097152 | tf_op jit(solution)/shard_map/pallas_call | solution.py:491
  2.9 2.0 %collective-permute-start = (bf16[2,48,1024]{2,1,0:T(8,128)(2,1)}, bf16[2,48,1024]{2,1,0:T(8,128)(2,1)S(1)}, u32[]{:S(2)}, u32[]{:S(2)}) collective-permute-start(bf16[2,48,1024]{2,1,0:T(8,128)(2,1)} %get-tuple-element.36), channel_id=1, source_target_pairs={{0,32},{1,33},{2,34},{3,35},{4,36},{5,37},{6,38},{7,39},{8,40},{9,... | collective-permute-start | bytes 589832 | tf_op jit(solution)/shard_map/ppermute | solution.py:495
  4.9 4.4 %collective-permute-start.1 = (bf16[2,48,1024]{2,1,0:T(8,128)(2,1)}, bf16[2,48,1024]{2,1,0:T(8,128)(2,1)S(1)}, u32[]{:S(2)}, u32[]{:S(2)}) collective-permute-start(bf16[2,48,1024]{2,1,0:T(8,128)(2,1)} %get-tuple-element.37), channel_id=1, source_target_pairs={{0,31},{1,0},{2,1},{3,2},{4,3},{5,4},{6,5},{7,6},{8,7},{9,8},{10,9... | collective-permute-start | bytes 589832 | tf_op jit(solution)/shard_map/ppermute | solution.py:496
  9.3 0.5 collective-permute-start.2
  9.8 1.6 %copy.29 = f32[8,4,64,64]{2,1,3,0:T(4,128)S(1)} copy(f32[8,4,64,64]{3,2,1,0:T(8,128)} %bitcast.24) | data formatting | bytes 1048576 | tf_op jit(solution)/shard_map/reshape | solution.py:501
  11.4 1.4 %reshape.55.bias_hbm = f32[8,64,256]{2,1,0:T(8,128)} reshape(f32[8,64,4,64]{3,2,1,0:T(4,128)S(1)} %bitcast.17) | data formatting | bytes 1048576 | tf_op jit(solution)/shard_map/reshape | solution.py:501
  12.8 0.6 pad_add_fusion.place
  13.5 0.6 copy-done.7
  14.3 20.4 %shard_map.250 = (bf16[256,4096]{1,0:T(8,128)(2,1)}, bf16[256,2048]{1,0:T(8,128)(2,1)}, bf16[2,256,1024]{2,1,0:T(8,128)(2,1)}, bf16[2,48,1024]{2,1,0:T(8,128)(2,...) custom-call(s32[3]{0:T(128)} %pad_add_fusion.place, s32[1,32]{1,0:T(1,128)} %row_field.1, ...), custom_call_target="tpu_custom_call" | custom-call | flops 5000000000 | bytes 20971520 | tf_op jit(solution)/shard_map/pallas_call | solution.py:503
  34.6 0.1 collective-permute-start.3
  34.7 10.5 %all-to-all-start = ((bf16[128,8,256]{2,1,0:T(8,128)(2,1)}), bf16[128,8,256]{2,1,0:T(8,128)(2,1)S(1)}, u32[]{:S(2)}, u32[]{:S(2)}) async-start(bf16[128,8,256]{2,1,0:T(8,128)(2,1)} %bitcast.25), calls=%async_computation | async-start | bytes 1048576 | tf_op jit(solution)/shard_map/all_to_all | solution.py:531
  45.2 0.9 collective-permute-start.6
  46.1 0.3 collective-permute-start.4
  46.4 1.1 collective-permute-start.5
  47.5 1.3 copy-done
  48.8 6.0 %shard_map.251.part = bf16[1024,2304]{1,0:T(8,128)(2,1)} custom-call(bf16[256,4096]{1,0:T(8,128)(2,1)} %get-tuple-element.40.mixed.x, bf16[256,4096]{1,0:T(8,128)(2,1)} %get-tuple-element.40.mixed.x, bf16[256,4096]{1,0:T(8,128)(2,1)} %copy-done, bf16[256,4096]{1,0:T(8,128)(2,1)} %copy-done, bf16[256,2048]{1,0:T(8,128)(2,1)} %get-tuple-element.41.keep, ...), custom_call_target="tpu_custom_call" | custom-call | flops 2147483648 | bytes 8388608 | tf_op jit(solution)/shard_map/pallas_call | solution.py:540
  54.8 4.4 %all-to-all-done.got = bf16[128,8,256]{2,1,0:T(8,128)(2,1)S(1)} async-done(((bf16[128,8,256]{2,1,0:T(8,128)(2,1)}), bf16[128,8,256]{2,1,0:T(8,128)(2,1)S(1)}, u32[]{:S(2)}, u32[]{:S(2)}) %all-to-all-start) | async-done | bytes 524320 | tf_op jit(solution)/shard_map/all_to_all | solution.py:531
  59.2 0.8 copy-done.1
  60.0 2.1 %shard_map.252 = bf16[1024,2304]{1,0:T(8,128)(2,1)} custom-call(bf16[128,8,256]{2,1,0:T(8,128)(2,1)} %copy-done.1, bf16[1024,2304]{1,0:T(8,128)(2,1)} %shard_map.251.part), custom_call_target="tpu_custom_call", output_to_operand_aliasing={{}: (1, {})} | custom-call | flops 1000000 | bytes 1048576 | tf_op jit(solution)/shard_map/pallas_call | solution.py:554
  62.1 0.6 copy-done.4
  62.8 6.4 %all-to-all-start.1 = ((bf16[128,8,2304]{2,1,0:T(8,128)(2,1)}), bf16[128,8,2304]{2,1,0:T(8,128)(2,1)}, u32[]{:S(2)}, u32[]{:S(2)}) async-start(bf16[128,8,2304]{2,1,0:T(8,128)(2,1)} %bitcast.16), calls=%async_computation.1 | async-start | bytes 9437184 | tf_op jit(solution)/shard_map/all_to_all | solution.py:565
  69.3 2.9 %shard_map.253 = (bf16[256,1024]{1,0:T(8,128)(2,1)}, bf16[256,1024]{1,0:T(8,128)(2,1)}) custom-call(bf16[256,1024]{1,0:T(8,128)(2,1)} %bitcast.20, bf16[256,1024]{1,0:T(8,128)(2,1)} %bitcast.23, bf16[2,256,1024]{2,1,0:T(8,128)(2,1)} %get-tuple-element.39.own, bf16[2,48,1024]{2,1,0:T(8,128)(2,1)} %copy-done.2, bf16[2,48,1024]{2,1,0:T(8,128)(2,1)} %copy-done.3, ...), custom_call_target="tpu_custom_call" | custom-call | flops 100000000 | bytes 4194304 | tf_op jit(solution)/shard_map/pallas_call | solution.py:566
  72.2 55.2 %all-to-all-done.1 = bf16[128,8,2304]{2,1,0:T(8,128)(2,1)} async-done(((bf16[128,8,2304]{2,1,0:T(8,128)(2,1)}), bf16[128,8,2304]{2,1,0:T(8,128)(2,1)}, u32[]{:S(2)}, u32[]{:S(2)}) %all-to-all-start.1) | async-done | bytes 4718624 | tf_op jit(solution)/shard_map/all_to_all | solution.py:565
  127.4 3.9 %shard_map.254 = (f32[8,3072]{1,0:T(8,128)}, f32[8,1024]{1,0:T(8,128)}, f32[32,64,64]{2,1,0:T(8,128)}, f32[3072]{0:T(1024)}, f32[1024]{0:T(1024)}, /*index=5*/f32[1024]{0:T(1024)}, f32[1024]{0:T(1024)}, f32[32]{0:T(128)}) custom-call(bf16[64,2,8,2304]{3,2,1,0:T(8,128)(2,1)} %bitcast.15.got), custom_call_target="tpu_custom_call" | custom-call | flops 10000000 | bytes 4194304 | tf_op jit(solution)/shard_map/pallas_call | solution.py:574
  (19 shorter events, 0.4 us)
Async XLA Ops:
  2.9 10.6 %collective-permute-start = (bf16[2,48,1024]{2,1,0:T(8,128)(2,1)}, bf16[2,48,1024]{2,1,0:T(8,128)(2,1)S(1)}, u32[]{:S(2)}, u32[]{:S(2)}) collective-permute-start(bf16[2,48,1024]{2,1,0:T(8,128)(2,1)} %get-tuple-element.36), channel_id=1, source_target_pairs={{0,32},{1,33},{2,34},{3,35},{4,36},{5,37},{6,38},{7,39},{8,40},{9,... | collective-permute-start | bytes 589832 | tf_op jit(solution)/shard_map/ppermute | solution.py:495
  4.9 8.6 %collective-permute-start.1 = (bf16[2,48,1024]{2,1,0:T(8,128)(2,1)}, bf16[2,48,1024]{2,1,0:T(8,128)(2,1)S(1)}, u32[]{:S(2)}, u32[]{:S(2)}) collective-permute-start(bf16[2,48,1024]{2,1,0:T(8,128)(2,1)} %get-tuple-element.37), channel_id=1, source_target_pairs={{0,31},{1,0},{2,1},{3,2},{4,3},{5,4},{6,5},{7,6},{8,7},{9,8},{10,9... | collective-permute-start | bytes 589832 | tf_op jit(solution)/shard_map/ppermute | solution.py:496
  9.3 4.2 %collective-permute-start.2 = (bf16[2,16,1024]{2,1,0:T(8,128)(2,1)}, bf16[2,16,1024]{2,1,0:T(8,128)(2,1)S(1)}, u32[]{:S(2)}, u32[]{:S(2)}) collective-permute-start(bf16[2,16,1024]{2,1,0:T(8,128)(2,1)} %get-tuple-element.38), channel_id=1, source_target_pairs={{0,63},{1,32},{2,33},{3,34},{4,35},{5,36},{6,37},{7,38},{8,39},{9,... | collective-permute-start | bytes 196616 | tf_op jit(solution)/shard_map/ppermute | solution.py:497
  13.5 0.6 copy-start.7
  13.5 0.7 copy-start.5
  13.5 0.8 copy-start.6
  34.6 12.9 %collective-permute-start.3 = (bf16[256,4096]{1,0:T(8,128)(2,1)}, bf16[256,4096]{1,0:T(8,128)(2,1)S(1)}, u32[]{:S(2)}, u32[]{:S(2)}) collective-permute-start(bf16[256,4096]{1,0:T(8,128)(2,1)} %get-tuple-element.40.mixed.x), channel_id=1, source_target_pairs={{0,1},{1,0},{2,3},{3,2},{4,5},{5,4},{6,7},{7,6},{8,9},{9,8},{10,11... | collective-permute-start | bytes 6291464 | tf_op jit(solution)/shard_map/ppermute | solution.py:529
  34.7 24.5 %all-to-all-start = ((bf16[128,8,256]{2,1,0:T(8,128)(2,1)}), bf16[128,8,256]{2,1,0:T(8,128)(2,1)S(1)}, u32[]{:S(2)}, u32[]{:S(2)}) async-start(bf16[128,8,256]{2,1,0:T(8,128)(2,1)} %bitcast.25), calls=%async_computation | async-start | bytes 1048576 | tf_op jit(solution)/shard_map/all_to_all | solution.py:531
  45.2 16.9 %collective-permute-start.6 = (bf16[2,16,1024]{2,1,0:T(8,128)(2,1)}, bf16[2,16,1024]{2,1,0:T(8,128)(2,1)S(1)}, u32[]{:S(2)}, u32[]{:S(2)}) collective-permute-start(bf16[2,16,1024]{2,1,0:T(8,128)(2,1)} %get-tuple-element.47), channel_id=1, source_target_pairs={{0,33},{1,34},{2,35},{3,36},{4,37},{5,38},{6,39},{7,40},{8,41},{9,... | collective-permute-start | bytes 196616 | tf_op jit(solution)/shard_map/ppermute | solution.py:534
  46.1 16.0 %collective-permute-start.4 = (bf16[2,48,1024]{2,1,0:T(8,128)(2,1)}, bf16[2,48,1024]{2,1,0:T(8,128)(2,1)S(1)}, u32[]{:S(2)}, u32[]{:S(2)}) collective-permute-start(bf16[2,48,1024]{2,1,0:T(8,128)(2,1)} %get-tuple-element.45), channel_id=1, source_target_pairs={{0,32},{1,33},{2,34},{3,35},{4,36},{5,37},{6,38},{7,39},{8,40},{9,... | collective-permute-start | bytes 589832 | tf_op jit(solution)/shard_map/ppermute | solution.py:532
  46.4 15.7 %collective-permute-start.5 = (bf16[2,48,1024]{2,1,0:T(8,128)(2,1)}, bf16[2,48,1024]{2,1,0:T(8,128)(2,1)S(1)}, u32[]{:S(2)}, u32[]{:S(2)}) collective-permute-start(bf16[2,48,1024]{2,1,0:T(8,128)(2,1)} %get-tuple-element.46), channel_id=1, source_target_pairs={{0,1},{1,2},{2,3},{3,4},{4,5},{5,6},{6,7},{7,8},{8,9},{9,10},{10,1... | collective-permute-start | bytes 589832 | tf_op jit(solution)/shard_map/ppermute | solution.py:533
  47.5 1.3 copy-start
  59.2 0.8 copy-start.1
  62.1 0.6 copy-start.4
  62.1 0.7 copy-start.2
  62.1 0.7 copy-start.3
  62.8 64.6 %all-to-all-start.1 = ((bf16[128,8,2304]{2,1,0:T(8,128)(2,1)}), bf16[128,8,2304]{2,1,0:T(8,128)(2,1)}, u32[]{:S(2)}, u32[]{:S(2)}) async-start(bf16[128,8,2304]{2,1,0:T(8,128)(2,1)} %bitcast.16), calls=%async_computation.1 | async-start | bytes 9437184 | tf_op jit(solution)/shard_map/all_to_all | solution.py:565

commit v5 on v4

--- a/solution.py
+++ b/solution.py
@@ -122,14 +122,26 @@
     wqkv, wproj, bias_t, cat, qkv, att, cos, units, inverses, grad, wide, branch, pos, vec,
     x, mixed, gp_send, gp_keep, g_send, g_keep, border, sems, out_sems,
 ):
-    loads = [
-        pltpu.make_async_copy(wqkv_hbm.at[:, pl.ds(t * D, D)], wqkv.at[:, pl.ds(t * D, D)], sems.at[t])
-        for t in range(3)
-    ]
-    loads.append(pltpu.make_async_copy(bias_hbm, bias_t, sems.at[3]))
-    loads.append(pltpu.make_async_copy(wproj_hbm, wproj, sems.at[4]))
-    for load in loads:
-        load.start()
+    loads = []
+
+    def load(source, target):
+        copy = pltpu.make_async_copy(source, target, sems.at[len(loads)])
+        copy.start()
+        loads.append(copy)
+        return copy
+
+    def gather(n, whole):
+        first, copies = 0, []
+        for source, count in ((whole, TOK), (row_in.at[n], HALO), (col_in.at[n], HALO), (cor_in.at[n], CORNER)):
+            copies.append(load(source, cat.at[n, pl.ds(first, count), :]))
+            first += count
+        return copies
+
+    tok_loads = gather(0, tok)
+    weight_loads = [load(wqkv_hbm.at[:, pl.ds(t * D, D)], wqkv.at[:, pl.ds(t * D, D)]) for t in range(3)]
+    bias_load = load(bias_hbm, bias_t)
+    cot_loads = gather(1, cot)
+    proj_load = load(wproj_hbm, wproj)
 
     p = place[2]
     half = D // 2
@@ -140,17 +152,10 @@
         copy.start()
         stores.append(copy)
 
-    for n, ref in enumerate((tok, cot)):
-        cat[0:TOK] = ref[...]
-        cat[TOK : TOK + HALO] = row_in[n]
-        cat[TOK + HALO : TOK + 2 * HALO] = col_in[n]
-        cat[TOK + 2 * HALO : CAT] = cor_in[n]
-        moved = mm(order[...], cat[...]).astype(bf16)
-        if n == 0:
-            x[...] = moved
-            write(x, send.at[:, pl.ds(3 * half, D)])
-        else:
-            grad[...] = moved
+    for copy in tok_loads:
+        copy.wait()
+    x[...] = mm(order[...], cat[0]).astype(bf16)
+    write(x, send.at[:, pl.ds(3 * half, D)])
 
     sub = lax.broadcasted_iota(jnp.int32, (WIN2, WIDE), 0)
     lane = lax.broadcasted_iota(jnp.int32, (WIN2, WIDE), 1) % WIN2
@@ -199,14 +204,14 @@
         return out
 
     for t in range(3):
-        loads[t].wait()
+        weight_loads[t].wait()
 
         @pl.loop(0, 2)
         def _(n):
             cols = pl.ds(pl.multiple_of(t * D + n * 512, 512), 512)
             qkv[:, cols] = (mm(x[...], wqkv[:, cols]) + bqkv[:, cols]).astype(bf16)
 
-    loads[3].wait()
+    bias_load.wait()
 
     def attend(g):
         at = pl.multiple_of(g * LANES, LANES)
@@ -242,7 +247,10 @@
         in_step([attend(n * FUSED + u) for u in range(FUSED)])
 
     write(mixed, send.at[:, pl.ds(0, D)])
-    loads[4].wait()
+    proj_load.wait()
+    for copy in cot_loads:
+        copy.wait()
+    grad[...] = mm(order[...], cat[1]).astype(bf16)
 
     @pl.loop(0, 4)
     def _(n):
@@ -374,64 +382,93 @@
         copy.wait()
 
 
-def weight_grad_kernel(mixed, x, mixed_other, x_other, keep, gp_other, q_other, k_other, v_other, out):
+def weight_grad_kernel(send, keep, other, out, own_v, other_v, keep_v, part, in_sems, out_sems):
     half = D // 2
-    a = jnp.concatenate((x[...], x_other[...]), axis=0)
-    for t, ref in enumerate((q_other, k_other, v_other)):
-        g = jnp.concatenate((keep[:, (t + 1) * half : (t + 2) * half], ref[...]), axis=0)
-        out[:, t * half : (t + 1) * half] = mm_ta(a, g).astype(bf16)
-    a = jnp.concatenate((mixed[...], mixed_other[...]), axis=0)
-    g = jnp.concatenate((keep[:, 0:half], gp_other[...]), axis=0)
-    out[:, 3 * half : 4 * half] = mm_ta(a, g).astype(bf16)
-
-
-def fold_kernel(got, part, part_out, spread_small, sem):
-    devices, rows, _ = got.shape
-    small = jnp.sum(got[...].astype(f32), axis=0)
-    spread_small[...] = jnp.broadcast_to(small[None], (devices, rows, EXTRA)).reshape(D, EXTRA).astype(bf16)
-    copy = pltpu.make_async_copy(spread_small, part_out.at[:, pl.ds(2 * D, EXTRA)], sem)
-    copy.start()
-    copy.wait()
-
-
-def last_kernel(got, qkv_out, proj_out, pos_out, qkv_bias, proj_bias, gain, shift, scale, total, small):
+    loads, stores = [], []
+
+    def load(source, target, first, width):
+        cols = pl.ds(first, width)
+        copy = pltpu.make_async_copy(source.at[:, cols], target.at[:, cols], in_sems.at[len(loads)])
+        copy.start()
+        loads.append(copy)
+
+    load(send, own_v, 3 * half, D)
+    load(keep, keep_v, half, half)
+    load(other, other_v, 3 * half, D)
+    load(other, other_v, 5 * half, half)
+    load(keep, keep_v, D, D)
+    load(other, other_v, 6 * half, D)
+    load(send, own_v, 0, D)
+    load(other, other_v, 0, 3 * half)
+    load(keep, keep_v, 0, half)
+
+    def multiply(t, feature, grad_keep, grad_other):
+        grad = jnp.concatenate(
+            (keep_v[:, grad_keep : grad_keep + half], other_v[:, grad_other : grad_other + half]), axis=0
+        )
+        for m in range(2):
+            cols = slice(feature + m * half, feature + (m + 1) * half)
+            value = jnp.concatenate((own_v[:, cols], other_v[:, cols]), axis=0)
+            part[t, m * half : (m + 1) * half, :] = mm_ta(value, grad).astype(bf16)
+        copy = pltpu.make_async_copy(part.at[t], out.at[:, pl.ds(t * half, half)], out_sems.at[t])
+        copy.start()
+        stores.append(copy)
+
+    for n in range(4):
+        loads[n].wait()
+    multiply(0, 3 * half, half, 5 * half)
+    for n in range(4, 6):
+        loads[n].wait()
+    multiply(1, 3 * half, 2 * half, 6 * half)
+    multiply(2, 3 * half, 3 * half, 7 * half)
+    for n in range(6, 9):
+        loads[n].wait()
+    multiply(3, 0, 0, 2 * half)
+    for copy in stores:
+        copy.wait()
+
+
+def last_kernel(
+    got_hbm, qkv_out, proj_out, pos_out, qkv_bias, proj_bias, gain, shift, scale, got, total, small, sems
+):
     half = D // 2
-    step = pl.program_id(0)
     pairs, _, rows, _ = got.shape
-    count = 2 * pairs * rows
-
-    @pl.when(step == 0)
-    def _():
-        total[...] = jnp.zeros_like(total)
-
+    steps = sems.shape[0]
+    each = pairs // steps
+    loads = []
+    for n in range(steps):
+        part = pl.ds(n * each, each)
+        loads.append(pltpu.make_async_copy(got_hbm.at[part], got.at[part], sems.at[n]))
+        loads[n].start()
+    for n in range(steps):
+        loads[n].wait()
+        here = slice(n * each, (n + 1) * each)
+        for side in range(2):
+            value = jnp.sum(got[here, side, :, 0 : 4 * half].astype(f32), axis=0)
+            total[side] = value if n == 0 else total[side] + value
+        count = 2 * each * rows
+        small[n * count : (n + 1) * count, :] = got[here, :, :, 4 * half :].astype(f32).reshape(count, EXTRA)
     for side in range(2):
-        total[side] += jnp.sum(got[:, side, :, 0 : 4 * half].astype(f32), axis=0)
-    here = got[:, :, :, 4 * half :].astype(f32).reshape(count, EXTRA)
-    small[pl.ds(pl.multiple_of(step * count, count), count), :] = here
-
-    @pl.when(step == pl.num_programs(0) - 1)
-    def _():
-        for side in range(2):
-            for t in range(3):
-                first = t * D + side * half
-                qkv_out[:, first : first + half] = total[side, :, t * half : (t + 1) * half]
-            proj_out[:, side * half : (side + 1) * half] = total[side, :, 3 * half :]
-        folded = small[:, 0:LANES].reshape(HEADS, WIN2 // 2, LANES)
-        pos_out[:, 0 : WIN2 // 2, :] = folded[:, :, 0:WIN2]
-        pos_out[:, WIN2 // 2 :, :] = folded[:, :, WIN2:]
-        first = 0
-        for ref in (qkv_bias, proj_bias, gain, shift):
-            for n in range(ref.shape[0] // LANES):
-                ref[n * LANES : (n + 1) * LANES] = small[8 * (first + n), LANES:]
-            first += ref.shape[0] // LANES
-        parts = small[8 * first : 8 * first + LANES, LANES:]
-        lane = lax.broadcasted_iota(jnp.int32, (LANES, LANES), 1)
-        at = lax.broadcasted_iota(jnp.int32, (LANES, LANES), 0)
-        left = jnp.sum(parts[:, :WIN2], axis=1, keepdims=True)
-        right = jnp.sum(parts[:, WIN2:], axis=1, keepdims=True)
-        heads = jnp.where(at == lane // 2 * 8, jnp.where(lane % 2 == 0, left, right), 0.0)
-        heads = jnp.sum(heads, axis=0, keepdims=True)
-        scale[...] = heads[0, :HEADS]
+        for t in range(3):
+            first = t * D + side * half
+            qkv_out[:, first : first + half] = total[side, :, t * half : (t + 1) * half]
+        proj_out[:, side * half : (side + 1) * half] = total[side, :, 3 * half :]
+    folded = small[:, 0:LANES].reshape(HEADS, WIN2 // 2, LANES)
+    pos_out[:, 0 : WIN2 // 2, :] = folded[:, :, 0:WIN2]
+    pos_out[:, WIN2 // 2 :, :] = folded[:, :, WIN2:]
+    first = 0
+    for ref in (qkv_bias, proj_bias, gain, shift):
+        for n in range(ref.shape[0] // LANES):
+            ref[n * LANES : (n + 1) * LANES] = small[8 * (first + n), LANES:]
+        first += ref.shape[0] // LANES
+    parts = small[8 * first : 8 * first + LANES, LANES:]
+    lane = lax.broadcasted_iota(jnp.int32, (LANES, LANES), 1)
+    at = lax.broadcasted_iota(jnp.int32, (LANES, LANES), 0)
+    left = jnp.sum(parts[:, :WIN2], axis=1, keepdims=True)
+    right = jnp.sum(parts[:, WIN2:], axis=1, keepdims=True)
+    heads = jnp.where(at == lane // 2 * 8, jnp.where(lane % 2 == 0, left, right), 0.0)
+    heads = jnp.sum(heads, axis=0, keepdims=True)
+    scale[...] = heads[0, :HEADS]
 
 
 def finish_kernel(tok, cot, own, row, col, cor, spread, block_out, grad_tokens):
@@ -509,16 +546,16 @@
         ),
         [
             pltpu.VMEM((D, 3 * D), bf16), pltpu.VMEM((D, D), bf16), pltpu.VMEM((GROUPS, WIN2, WIDE), f32),
-            pltpu.VMEM((CAT, D), bf16), pltpu.VMEM((TOK, 3 * D), bf16),
+            pltpu.VMEM((2, CAT, D), bf16), pltpu.VMEM((TOK, 3 * D), bf16),
             pltpu.VMEM((GROUPS, WINDOWS, WIN2, WIDE), bf16), pltpu.VMEM((GROUPS, WINDOWS, WIN2, WIDE), f32),
             pltpu.VMEM((2, TOK, D), bf16), pltpu.VMEM((2, TOK, D), f32), pltpu.VMEM((TOK, D), bf16),
             pltpu.VMEM((TOK, D), f32), pltpu.VMEM((TOK, D), bf16), pltpu.VMEM((HEADS * 32, LANES), f32),
             pltpu.VMEM((1, 8 * D), f32), pltpu.VMEM((TOK, D), bf16), pltpu.VMEM((TOK, D), bf16),
             pltpu.VMEM((TOK, D // 2), bf16), pltpu.VMEM((TOK, D // 2), bf16), pltpu.VMEM((TOK, 3 * D // 2), bf16),
             pltpu.VMEM((TOK, 3 * D // 2), bf16), pltpu.VMEM((2, CAT, D), bf16),
-            pltpu.SemaphoreType.DMA((5,)), pltpu.SemaphoreType.DMA((14,)),
+            pltpu.SemaphoreType.DMA((13,)), pltpu.SemaphoreType.DMA((14,)),
         ],
-        [SM] * 4 + [VM] * 9 + [ANY, VM, ANY, ANY, VM, VM, VM],
+        [SM] * 4 + [ANY] * 5 + [VM] * 4 + [ANY, VM, ANY, ANY, VM, VM, VM],
         flops=5 * 10**9, bytes_accessed=20 * 2**20, out_specs=(ANY,) * 6 + (VM,),
     )(
         place, row_field, col_field, logit_scale, tok, cot, row_in, col_in, cor_in, order, order_t, mask, ones,
@@ -532,55 +569,40 @@
     row = lax.ppermute(row, AXES, neighbour(1, 0))
     col = lax.ppermute(col, AXES, neighbour(0, 1))
     cor = lax.ppermute(cor, AXES, neighbour(1, 1))
-    block = D // 2
-
-    def columns(first, moving):
-        return pl.BlockSpec((TOK, block), lambda i: (0, first + (i if moving else 0)))
-
-    part = pl.pallas_call(
+    part = call(
         weight_grad_kernel,
-        grid=(2,),
-        out_shape=sds((D, 2 * D + EXTRA), bf16),
-        in_specs=[
-            columns(0, True), columns(3, True), columns(0, True), columns(3, True),
-            pl.BlockSpec((TOK, 2 * D), lambda i: (0, 0)),
-            columns(2, False), columns(5, False), columns(6, False), columns(7, False),
+        sds((D, 2 * D + EXTRA), bf16),
+        [
+            pltpu.VMEM((TOK, 4 * D), bf16), pltpu.VMEM((TOK, 4 * D), bf16), pltpu.VMEM((TOK, 2 * D), bf16),
+            pltpu.VMEM((4, D, D // 2), bf16), pltpu.SemaphoreType.DMA((9,)), pltpu.SemaphoreType.DMA((4,)),
         ],
-        out_specs=pl.BlockSpec((block, 2 * D + EXTRA), lambda i: (i, 0)),
-        compiler_params=pltpu.CompilerParams(vmem_limit_bytes=VMEM_LIMIT),
-        cost_estimate=pl.CostEstimate(flops=8 * TOK * D * D, bytes_accessed=8 * 2**20, transcendentals=0),
-    )(send, send, other, other, keep, other, other, other, other)
-    part, small = lax.optimization_barrier((part, small))
-    part = pl.pallas_call(
-        fold_kernel,
-        out_shape=sds(part.shape, bf16),
-        in_specs=[VM, ANY],
-        out_specs=ANY,
-        scratch_shapes=[pltpu.VMEM((D, EXTRA), bf16), pltpu.SemaphoreType.DMA],
-        input_output_aliases={1: 0},
-        compiler_params=pltpu.CompilerParams(vmem_limit_bytes=VMEM_LIMIT),
-        cost_estimate=pl.CostEstimate(flops=10**6, bytes_accessed=2**20, transcendentals=0),
-    )(small, part)
+        [ANY] * 3,
+        flops=8 * TOK * D * D, bytes_accessed=9 * 2**20, out_specs=ANY,
+    )(send, keep, other)
+    part, small = lax.optimization_barrier((part.reshape(devices, rows, -1), small))
+    small = jnp.sum(small.astype(f32), axis=0).astype(bf16)
+    part = part.at[:, :, 2 * D :].set(jnp.broadcast_to(small[None], (devices, rows, EXTRA)))
     part, row, col, cor = lax.optimization_barrier((part, row, col, cor))
-    got = lax.all_to_all(part.reshape(devices, rows, -1), AXES, 0, 0, tiled=True)
+    got = lax.all_to_all(part, AXES, 0, 0, tiled=True)
     block_out, grad_tokens = call(
         finish_kernel, (sds((TOK, D), bf16), sds((TOK, D), bf16)), (), [VM] * 7, flops=10**8, bytes_accessed=2**22
     )(tok, cot, own, row, col, cor, spread)
-    steps = 1
     outs = (
         sds((rows, 3 * D), f32), sds((rows, D), f32), sds((HEADS, WIN2, WIN2), f32), sds((3 * D,), f32), sds((D,), f32),
         sds((D,), f32), sds((D,), f32), sds((HEADS,), f32),
     )
-    grad_qkv_weight, grad_proj_weight, grad_position, g_qkv_bias, g_proj_bias, g_gain, g_shift, g_scale = pl.pallas_call(
+    got = got.reshape(devices // 2, 2, rows, 2 * D + EXTRA)
+    steps = min(4, devices // 2)
+    grad_qkv_weight, grad_proj_weight, grad_position, g_qkv_bias, g_proj_bias, g_gain, g_shift, g_scale = call(
         last_kernel,
-        grid=(steps,),
-        out_shape=outs,
-        in_specs=[pl.BlockSpec((devices // 2 // steps, 2, rows, got.shape[2]), lambda i: (i, 0, 0, 0))],
-        out_specs=tuple(pl.BlockSpec(o.shape, lambda i, n=len(o.shape): (0,) * n) for o in outs),
-        scratch_shapes=[pltpu.VMEM((2, rows, 2 * D), f32), pltpu.VMEM((D, EXTRA), f32)],
-        compiler_params=pltpu.CompilerParams(vmem_limit_bytes=VMEM_LIMIT),
-        cost_estimate=pl.CostEstimate(flops=10**7, bytes_accessed=2**22, transcendentals=0),
-    )(got.reshape(devices // 2, 2, rows, -1))
+        outs,
+        [
+            pltpu.VMEM(got.shape, bf16), pltpu.VMEM((2, rows, 2 * D), f32), pltpu.VMEM((D, EXTRA), f32),
+            pltpu.SemaphoreType.DMA((steps,)),
+        ],
+        [ANY],
+        flops=10**7, bytes_accessed=2**22,
+    )(got)
     return (
         block_out.reshape(1, SIDE, SIDE, D), grad_tokens.reshape(1, SIDE, SIDE, D), grad_qkv_weight, grad_proj_weight, g_qkv_bias, g_proj_bias,
         g_gain, g_shift, g_scale, grad_position,

time: 132 us -> 131 us (level)
  Pallas kernels: 37.5 us -> 34.7 us
  starting transfers between devices: 26.2 us -> 28 us
    pallas_call x3 -> x2, Pallas kernels: 11.9 us -> 9.07 us  [the longest x1 5.38 us: per_device(): call(weight_grad_kernel, sds((D, 2 * D + EXTRA), bf16), [pltpu.VMEM((TOK,...]
    all_to_all x1, starting transfers between devices: 6.43 us -> 8.28 us  [per_device(): got = lax.all_to_all(part, AXES, 0, 0, tiled=True)]
    unnamed x16 -> x14, local copies, waits for them, and re-layouts: 3.57 us -> 2.06 us
  transfers between devices with their start and end apart: 9 -> 9, of which waited for: 3 -> 3; matrix products, arithmetic and copies ran while one was open for 3% -> 4% of each run, Pallas kernels for 8% -> 6%
where the time goes in v5:
time: 131 us
  waiting for transfers between devices  60.2 us (46%)
  Pallas kernels  34.7 us (26%)
  starting transfers between devices  28 us (21%)
  local copies, waits for them, and re-layouts  5.97 us (5%)
    all_to_all x1, waiting for transfers between devices, per_device(): got = lax.all_to_all(part, AXES, 0, 0, tiled=True)  55.1 us
    pallas_call x1, Pallas kernels, per_device(): call(local_kernel, (sds((TOK, 4 * D), bf16), sds((TOK, 2 * D), bf16), sds...  20.5 us
    all_to_all x1, starting transfers between devices, per_device(): lax.all_to_all(small.reshape(devices, rows, EXTRA), AXES, 0, 0, tiled=True)  10.5 us
    all_to_all x1, starting transfers between devices, per_device(): got = lax.all_to_all(part, AXES, 0, 0, tiled=True)  8.28 us
    pallas_call x1, Pallas kernels, per_device(): call(weight_grad_kernel, sds((D, 2 * D + EXTRA), bf16), [pltpu.VMEM((TOK,...  5.38 us
    all_to_all x1, waiting for transfers between devices, per_device(): lax.all_to_all(small.reshape(devices, rows, EXTRA), AXES, 0, 0, tiled=True)  4.97 us
    ppermute x1, starting transfers between devices, per_device(): col_in = lax.ppermute(col_in, AXES, neighbour(0, -1))  4.37 us
    pallas_call x1, Pallas kernels, per_device(): call(last_kernel, outs, [pltpu.VMEM(got.shape, bf16), pltpu.VMEM((2, rows...  3.68 us
  transfers between devices with their start and end apart: 9, of which 3 were waited for; matrix products, arithmetic and copies ran while one was open for 4% of the time, Pallas kernels for 6%

profile of v5, /device:TPU:0, one launch (start us, length us, event | category | flops | bytes accessed | tf_op | source)
XLA Modules:
  0.0 130.6 jit_solution(14549948122474127046)
XLA Ops:
  0.6 2.3 %shard_map.249 = (bf16[2,48,1024]{2,1,0:T(8,128)(2,1)}, bf16[2,48,1024]{2,1,0:T(8,128)(2,1)}, bf16[2,16,1024]{2,1,0:T(8,128)(2,1)}) custom-call(bf16[256,1024]{1,0:T(8,128)(2,1)} %bitcast.18, bf16[256,1024]{1,0:T(8,128)(2,1)} %bitcast.21, bf16[112,256]{1,0:T(8,128)(2,1)} %constant.70.clone.spread_t), custom_call_target="tpu_custom_call" | custom-call | flops 100000000 | bytes 2097152 | tf_op jit(solution)/shard_map/pallas_call | solution.py:528
  2.9 2.0 %collective-permute-start = (bf16[2,48,1024]{2,1,0:T(8,128)(2,1)}, bf16[2,48,1024]{2,1,0:T(8,128)(2,1)S(1)}, u32[]{:S(2)}, u32[]{:S(2)}) collective-permute-start(bf16[2,48,1024]{2,1,0:T(8,128)(2,1)} %get-tuple-element.48), channel_id=1, source_target_pairs={{0,32},{1,33},{2,34},{3,35},{4,36},{5,37},{6,38},{7,39},{8,40},{9,... | collective-permute-start | bytes 589832 | tf_op jit(solution)/shard_map/ppermute | solution.py:532
  4.9 4.4 %collective-permute-start.1 = (bf16[2,48,1024]{2,1,0:T(8,128)(2,1)}, bf16[2,48,1024]{2,1,0:T(8,128)(2,1)S(1)}, u32[]{:S(2)}, u32[]{:S(2)}) collective-permute-start(bf16[2,48,1024]{2,1,0:T(8,128)(2,1)} %get-tuple-element.49), channel_id=1, source_target_pairs={{0,31},{1,0},{2,1},{3,2},{4,3},{5,4},{6,5},{7,6},{8,7},{9,8},{10,9... | collective-permute-start | bytes 589832 | tf_op jit(solution)/shard_map/ppermute | solution.py:533
  9.3 0.5 collective-permute-start.2
  9.8 1.6 %copy.28 = f32[8,4,64,64]{2,1,3,0:T(4,128)S(1)} copy(f32[8,4,64,64]{3,2,1,0:T(8,128)} %bitcast.24) | data formatting | bytes 1048576 | tf_op jit(solution)/shard_map/reshape | solution.py:538
  11.4 1.4 %reshape.85.bias_hbm = f32[8,64,256]{2,1,0:T(8,128)} reshape(f32[8,64,4,64]{3,2,1,0:T(4,128)S(1)} %bitcast.17) | data formatting | bytes 1048576 | tf_op jit(solution)/shard_map/reshape | solution.py:538
  12.8 0.6 pad_add_fusion.place
  13.4 0.1 collective-permute-done.2.cor_in
  13.5 0.6 copy-done.6
  14.2 20.5 %shard_map.250 = (bf16[256,4096]{1,0:T(8,128)(2,1)}, bf16[256,2048]{1,0:T(8,128)(2,1)}, bf16[2,256,1024]{2,1,0:T(8,128)(2,1)}, bf16[2,48,1024]{2,1,0:T(8,128)(2,...) custom-call(s32[3]{0:T(128)} %pad_add_fusion.place, s32[1,32]{1,0:T(1,128)} %row_field.1, ...), custom_call_target="tpu_custom_call" | custom-call | flops 5000000000 | bytes 20971520 | tf_op jit(solution)/shard_map/pallas_call | solution.py:540
  34.7 0.1 collective-permute-start.3
  34.8 10.5 %all-to-all-start = ((bf16[128,8,256]{2,1,0:T(8,128)(2,1)}), bf16[128,8,256]{2,1,0:T(8,128)(2,1)S(1)}, u32[]{:S(2)}, u32[]{:S(2)}) async-start(bf16[128,8,256]{2,1,0:T(8,128)(2,1)} %bitcast.25), calls=%async_computation | async-start | bytes 1048576 | tf_op jit(solution)/shard_map/all_to_all | solution.py:568
  45.3 0.9 collective-permute-start.6
  46.2 0.3 collective-permute-start.4
  46.5 1.1 collective-permute-start.5
  47.6 1.3 %copy-done = bf16[256,4096]{1,0:T(8,128)(2,1)} copy-done((bf16[256,4096]{1,0:T(8,128)(2,1)}, bf16[256,4096]{1,0:T(8,128)(2,1)S(1)}, u32[]{:S(2)}) %copy-start) | copy-done | bytes 2097176
  48.9 5.4 %shard_map.251 = bf16[1024,2304]{1,0:T(8,128)(2,1)} custom-call(bf16[256,4096]{1,0:T(8,128)(2,1)} %get-tuple-element.52.send, bf16[256,2048]{1,0:T(8,128)(2,1)} %get-tuple-element.53.keep, bf16[256,4096]{1,0:T(8,128)(2,1)} %copy-done), custom_call_target="tpu_custom_call" | custom-call | flops 2147483648 | bytes 9437184 | tf_op jit(solution)/shard_map/pallas_call | solution.py:572
  54.3 5.0 %all-to-all-done = bf16[128,8,256]{2,1,0:T(8,128)(2,1)S(1)} async-done(((bf16[128,8,256]{2,1,0:T(8,128)(2,1)}), bf16[128,8,256]{2,1,0:T(8,128)(2,1)S(1)}, u32[]{:S(2)}, u32[]{:S(2)}) %all-to-all-start) | async-done | bytes 524320 | tf_op jit(solution)/shard_map/all_to_all | solution.py:568
  59.3 0.1 reduce_sum.12
  59.4 0.9 broadcast_dynamic-update-slice_fusion
  60.4 8.3 %all-to-all-start.1 = ((bf16[128,8,2304]{2,1,0:T(8,128)(2,1)}), bf16[128,8,2304]{2,1,0:T(8,128)(2,1)}, u32[]{:S(2)}, u32[]{:S(2)}) async-start(bf16[128,8,2304]{2,1,0:T(8,128)(2,1)} %broadcast_dynamic-update-slice_fusion), calls=%async_computation.1 | async-start | bytes 9437184 | tf_op jit(solution)/shard_map/all_to_all | solution.py:586
  68.7 2.9 %shard_map.252 = (bf16[256,1024]{1,0:T(8,128)(2,1)}, bf16[256,1024]{1,0:T(8,128)(2,1)}) custom-call(bf16[256,1024]{1,0:T(8,128)(2,1)} %bitcast.20, bf16[256,1024]{1,0:T(8,128)(2,1)} %bitcast.23, bf16[2,256,1024]{2,1,0:T(8,128)(2,1)} %get-tuple-element.51.own, bf16[2,48,1024]{2,1,0:T(8,128)(2,1)} %copy-done.1, bf16[2,48,1024]{2,1,0:T(8,128)(2,1)} %copy-done.2, ...), custom_call_target="tpu_custom_call" | custom-call | flops 100000000 | bytes 4194304 | tf_op jit(solution)/shard_map/pallas_call | solution.py:587
  71.6 55.1 %all-to-all-done.1 = bf16[128,8,2304]{2,1,0:T(8,128)(2,1)} async-done(((bf16[128,8,2304]{2,1,0:T(8,128)(2,1)}), bf16[128,8,2304]{2,1,0:T(8,128)(2,1)}, u32[]{:S(2)}, u32[]{:S(2)}) %all-to-all-start.1) | async-done | bytes 4718624 | tf_op jit(solution)/shard_map/all_to_all | solution.py:586
  126.8 3.7 %shard_map.253 = (f32[8,3072]{1,0:T(8,128)}, f32[8,1024]{1,0:T(8,128)}, f32[32,64,64]{2,1,0:T(8,128)}, f32[3072]{0:T(1024)}, f32[1024]{0:T(1024)}, /*index=5*/f32[1024]{0:T(1024)}, f32[1024]{0:T(1024)}, f32[32]{0:T(128)}) custom-call(bf16[64,2,8,2304]{3,2,1,0:T(8,128)(2,1)} %bitcast.15.got_hbm), custom_call_target="tpu_custom_call" | custom-call | flops 10000000 | bytes 4194304 | tf_op jit(solution)/shard_map/pallas_call | solution.py:596
  (18 shorter events, 0.2 us)
Async XLA Ops:
  2.9 10.6 %collective-permute-start = (bf16[2,48,1024]{2,1,0:T(8,128)(2,1)}, bf16[2,48,1024]{2,1,0:T(8,128)(2,1)S(1)}, u32[]{:S(2)}, u32[]{:S(2)}) collective-permute-start(bf16[2,48,1024]{2,1,0:T(8,128)(2,1)} %get-tuple-element.48), channel_id=1, source_target_pairs={{0,32},{1,33},{2,34},{3,35},{4,36},{5,37},{6,38},{7,39},{8,40},{9,... | collective-permute-start | bytes 589832 | tf_op jit(solution)/shard_map/ppermute | solution.py:532
  4.9 8.6 %collective-permute-start.1 = (bf16[2,48,1024]{2,1,0:T(8,128)(2,1)}, bf16[2,48,1024]{2,1,0:T(8,128)(2,1)S(1)}, u32[]{:S(2)}, u32[]{:S(2)}) collective-permute-start(bf16[2,48,1024]{2,1,0:T(8,128)(2,1)} %get-tuple-element.49), channel_id=1, source_target_pairs={{0,31},{1,0},{2,1},{3,2},{4,3},{5,4},{6,5},{7,6},{8,7},{9,8},{10,9... | collective-permute-start | bytes 589832 | tf_op jit(solution)/shard_map/ppermute | solution.py:533
  9.3 4.2 %collective-permute-start.2 = (bf16[2,16,1024]{2,1,0:T(8,128)(2,1)}, bf16[2,16,1024]{2,1,0:T(8,128)(2,1)S(1)}, u32[]{:S(2)}, u32[]{:S(2)}) collective-permute-start(bf16[2,16,1024]{2,1,0:T(8,128)(2,1)} %get-tuple-element.50), channel_id=1, source_target_pairs={{0,63},{1,32},{2,33},{3,34},{4,35},{5,36},{6,37},{7,38},{8,39},{9,... | collective-permute-start | bytes 196616 | tf_op jit(solution)/shard_map/ppermute | solution.py:534
  13.5 0.6 copy-start.6
  13.5 0.7 copy-start.4
  13.5 0.7 copy-start.5
  34.7 12.9 %collective-permute-start.3 = (bf16[256,4096]{1,0:T(8,128)(2,1)}, bf16[256,4096]{1,0:T(8,128)(2,1)S(1)}, u32[]{:S(2)}, u32[]{:S(2)}) collective-permute-start(bf16[256,4096]{1,0:T(8,128)(2,1)} %get-tuple-element.52.send), channel_id=1, source_target_pairs={{0,1},{1,0},{2,3},{3,2},{4,5},{5,4},{6,7},{7,6},{8,9},{9,8},{10,11... | collective-permute-start | bytes 6291464 | tf_op jit(solution)/shard_map/ppermute | solution.py:566
  34.8 24.5 %all-to-all-start = ((bf16[128,8,256]{2,1,0:T(8,128)(2,1)}), bf16[128,8,256]{2,1,0:T(8,128)(2,1)S(1)}, u32[]{:S(2)}, u32[]{:S(2)}) async-start(bf16[128,8,256]{2,1,0:T(8,128)(2,1)} %bitcast.25), calls=%async_computation | async-start | bytes 1048576 | tf_op jit(solution)/shard_map/all_to_all | solution.py:568
  45.3 15.0 %collective-permute-start.6 = (bf16[2,16,1024]{2,1,0:T(8,128)(2,1)}, bf16[2,16,1024]{2,1,0:T(8,128)(2,1)S(1)}, u32[]{:S(2)}, u32[]{:S(2)}) collective-permute-start(bf16[2,16,1024]{2,1,0:T(8,128)(2,1)} %get-tuple-element.59), channel_id=1, source_target_pairs={{0,33},{1,34},{2,35},{3,36},{4,37},{5,38},{6,39},{7,40},{8,41},{9,... | collective-permute-start | bytes 196616 | tf_op jit(solution)/shard_map/ppermute | solution.py:571
  46.2 14.1 %collective-permute-start.4 = (bf16[2,48,1024]{2,1,0:T(8,128)(2,1)}, bf16[2,48,1024]{2,1,0:T(8,128)(2,1)S(1)}, u32[]{:S(2)}, u32[]{:S(2)}) collective-permute-start(bf16[2,48,1024]{2,1,0:T(8,128)(2,1)} %get-tuple-element.57), channel_id=1, source_target_pairs={{0,32},{1,33},{2,34},{3,35},{4,36},{5,37},{6,38},{7,39},{8,40},{9,... | collective-permute-start | bytes 589832 | tf_op jit(solution)/shard_map/ppermute | solution.py:569
  46.5 13.8 %collective-permute-start.5 = (bf16[2,48,1024]{2,1,0:T(8,128)(2,1)}, bf16[2,48,1024]{2,1,0:T(8,128)(2,1)S(1)}, u32[]{:S(2)}, u32[]{:S(2)}) collective-permute-start(bf16[2,48,1024]{2,1,0:T(8,128)(2,1)} %get-tuple-element.58), channel_id=1, source_target_pairs={{0,1},{1,2},{2,3},{3,4},{4,5},{5,6},{6,7},{7,8},{8,9},{9,10},{10,1... | collective-permute-start | bytes 589832 | tf_op jit(solution)/shard_map/ppermute | solution.py:570
  47.6 1.3 %copy-start = (bf16[256,4096]{1,0:T(8,128)(2,1)}, bf16[256,4096]{1,0:T(8,128)(2,1)S(1)}, u32[]{:S(2)}) copy-start(bf16[256,4096]{1,0:T(8,128)(2,1)S(1)} %collective-permute-done.3.other) | copy-start | bytes 6291460
  60.3 8.3 %copy-start.3 = (bf16[2,16,1024]{2,1,0:T(8,128)(2,1)}, bf16[2,16,1024]{2,1,0:T(8,128)(2,1)S(1)}, u32[]{:S(2)}) copy-start(bf16[2,16,1024]{2,1,0:T(8,128)(2,1)S(1)} %collective-permute-done.6.cor) | copy-start | bytes 196612
  60.3 8.3 %copy-start.1 = (bf16[2,48,1024]{2,1,0:T(8,128)(2,1)}, bf16[2,48,1024]{2,1,0:T(8,128)(2,1)S(1)}, u32[]{:S(2)}) copy-start(bf16[2,48,1024]{2,1,0:T(8,128)(2,1)S(1)} %collective-permute-done.4.row) | copy-start | bytes 589828
  60.3 8.3 %copy-start.2 = (bf16[2,48,1024]{2,1,0:T(8,128)(2,1)}, bf16[2,48,1024]{2,1,0:T(8,128)(2,1)S(1)}, u32[]{:S(2)}) copy-start(bf16[2,48,1024]{2,1,0:T(8,128)(2,1)S(1)} %collective-permute-done.5.col) | copy-start | bytes 589828
  60.4 66.4 %all-to-all-start.1 = ((bf16[128,8,2304]{2,1,0:T(8,128)(2,1)}), bf16[128,8,2304]{2,1,0:T(8,128)(2,1)}, u32[]{:S(2)}, u32[]{:S(2)}) async-start(bf16[128,8,2304]{2,1,0:T(8,128)(2,1)} %broadcast_dynamic-update-slice_fusion), calls=%async_computation.1 | async-start | bytes 9437184 | tf_op jit(solution)/shard_map/all_to_all | solution.py:586

commit v6 on v5

--- a/solution.py
+++ b/solution.py
@@ -487,14 +487,14 @@
 ANY = pl.BlockSpec(memory_space=pl.ANY)
 
 
-def call(kernel, outs, scratch=(), specs=None, flops=0, bytes_accessed=0, out_specs=None):
+def call(kernel, outs, scratch=(), specs=None, flops=0, bytes_accessed=0, out_specs=None, limit=VMEM_LIMIT):
     return pl.pallas_call(
         kernel,
         out_shape=outs,
         in_specs=specs,
         out_specs=out_specs or jax.tree.map(lambda _: VM, outs),
         scratch_shapes=list(scratch),
-        compiler_params=pltpu.CompilerParams(vmem_limit_bytes=VMEM_LIMIT),
+        compiler_params=pltpu.CompilerParams(vmem_limit_bytes=limit),
         cost_estimate=pl.CostEstimate(flops=flops, bytes_accessed=bytes_accessed, transcendentals=0),
     )
 
@@ -582,10 +582,9 @@
     part, small = lax.optimization_barrier((part.reshape(devices, rows, -1), small))
     small = jnp.sum(small.astype(f32), axis=0).astype(bf16)
     part = part.at[:, :, 2 * D :].set(jnp.broadcast_to(small[None], (devices, rows, EXTRA)))
-    part, row, col, cor = lax.optimization_barrier((part, row, col, cor))
     got = lax.all_to_all(part, AXES, 0, 0, tiled=True)
     block_out, grad_tokens = call(
-        finish_kernel, (sds((TOK, D), bf16), sds((TOK, D), bf16)), (), [VM] * 7, flops=10**8, bytes_accessed=2**22
+        finish_kernel, (sds((TOK, D), bf16), sds((TOK, D), bf16)), (), [VM] * 7, flops=10**8, bytes_accessed=2**22, limit=20 * 2**20
     )(tok, cot, own, row, col, cor, spread)
     outs = (
         sds((rows, 3 * D), f32), sds((rows, D), f32), sds((HEADS, WIN2, WIN2), f32), sds((3 * D,), f32), sds((D,), f32),

time: 131 us -> 130 us (level)
  waiting for transfers between devices: 60.2 us -> 63.3 us
  starting transfers between devices: 28 us -> 26 us
  Pallas kernels: 34.7 us -> 33 us
    ppermute x1, waiting for transfers between devices: 0.01 us -> 56.3 us  [per_device(): cor = lax.ppermute(cor, AXES, neighbour(1, 1))]
    all_to_all x1, waiting for transfers between devices: 55.1 us -> 0.01 us  [per_device(): got = lax.all_to_all(part, AXES, 0, 0, tiled=True)]
    all_to_all x1, starting transfers between devices: 8.28 us -> 5.97 us  [per_device(): got = lax.all_to_all(part, AXES, 0, 0, tiled=True)]
    all_to_all x1, waiting for transfers between devices: 4.97 us -> 6.94 us  [per_device(): lax.all_to_all(small.reshape(devices, rows, EXTRA), AXES, 0, 0, tiled=True)]
    pallas_call x1, Pallas kernels: 2.94 us -> 1.31 us  [per_device(): call(finish_kernel, (sds((TOK, D), bf16), sds((TOK, D), bf16)), (), [VM]...]
  transfers between devices with their start and end apart: 9 -> 9, of which waited for: 3 -> 3; matrix products, arithmetic and copies ran while one was open for 4% -> 3% of each run, Pallas kernels for 6% -> 5%
where the time goes in v6:
time: 130 us
  waiting for transfers between devices  63.3 us (49%)
  Pallas kernels  33 us (25%)
  starting transfers between devices  26 us (20%)
  local copies, waits for them, and re-layouts  5.99 us (5%)
    ppermute x1, waiting for transfers between devices, per_device(): cor = lax.ppermute(cor, AXES, neighbour(1, 1))  56.3 us
    pallas_call x1, Pallas kernels, per_device(): call(local_kernel, (sds((TOK, 4 * D), bf16), sds((TOK, 2 * D), bf16), sds...  20.5 us
    all_to_all x1, starting transfers between devices, per_device(): lax.all_to_all(small.reshape(devices, rows, EXTRA), AXES, 0, 0, tiled=True)  10.5 us
    all_to_all x1, waiting for transfers between devices, per_device(): lax.all_to_all(small.reshape(devices, rows, EXTRA), AXES, 0, 0, tiled=True)  6.94 us
    all_to_all x1, starting transfers between devices, per_device(): got = lax.all_to_all(part, AXES, 0, 0, tiled=True)  5.97 us
    pallas_call x1, Pallas kernels, per_device(): call(weight_grad_kernel, sds((D, 2 * D + EXTRA), bf16), [pltpu.VMEM((TOK,...  5.28 us
    ppermute x1, starting transfers between devices, per_device(): col_in = lax.ppermute(col_in, AXES, neighbour(0, -1))  4.37 us
    pallas_call x1, Pallas kernels, per_device(): call(last_kernel, outs, [pltpu.VMEM(got.shape, bf16), pltpu.VMEM((2, rows...  3.68 us
  transfers between devices with their start and end apart: 9, of which 3 were waited for; matrix products, arithmetic and copies ran while one was open for 3% of the time, Pallas kernels for 5%

profile of v6, /device:TPU:0, one launch (start us, length us, event | category | flops | bytes accessed | tf_op | source)
XLA Modules:
  0.0 130.0 jit_solution(18339576906667850390)
XLA Ops:
  0.6 2.3 %shard_map.249 = (bf16[2,48,1024]{2,1,0:T(8,128)(2,1)}, bf16[2,48,1024]{2,1,0:T(8,128)(2,1)}, bf16[2,16,1024]{2,1,0:T(8,128)(2,1)}) custom-call(bf16[256,1024]{1,0:T(8,128)(2,1)} %bitcast.16, bf16[256,1024]{1,0:T(8,128)(2,1)} %bitcast.19, bf16[112,256]{1,0:T(8,128)(2,1)} %constant.70.clone.spread_t), custom_call_target="tpu_custom_call" | custom-call | flops 100000000 | bytes 2097152 | tf_op jit(solution)/shard_map/pallas_call | solution.py:528
  2.9 2.0 %collective-permute-start = (bf16[2,48,1024]{2,1,0:T(8,128)(2,1)}, bf16[2,48,1024]{2,1,0:T(8,128)(2,1)S(1)}, u32[]{:S(2)}, u32[]{:S(2)}) collective-permute-start(bf16[2,48,1024]{2,1,0:T(8,128)(2,1)} %get-tuple-element.44), channel_id=1, source_target_pairs={{0,32},{1,33},{2,34},{3,35},{4,36},{5,37},{6,38},{7,39},{8,40},{9,... | collective-permute-start | bytes 589832 | tf_op jit(solution)/shard_map/ppermute | solution.py:532
  4.9 4.4 %collective-permute-start.1 = (bf16[2,48,1024]{2,1,0:T(8,128)(2,1)}, bf16[2,48,1024]{2,1,0:T(8,128)(2,1)S(1)}, u32[]{:S(2)}, u32[]{:S(2)}) collective-permute-start(bf16[2,48,1024]{2,1,0:T(8,128)(2,1)} %get-tuple-element.45), channel_id=1, source_target_pairs={{0,31},{1,0},{2,1},{3,2},{4,3},{5,4},{6,5},{7,6},{8,7},{9,8},{10,9... | collective-permute-start | bytes 589832 | tf_op jit(solution)/shard_map/ppermute | solution.py:533
  9.3 0.5 collective-permute-start.2
  9.8 1.6 %copy.28 = f32[8,4,64,64]{2,1,3,0:T(4,128)S(1)} copy(f32[8,4,64,64]{3,2,1,0:T(8,128)} %bitcast.24) | data formatting | bytes 1048576 | tf_op jit(solution)/shard_map/reshape | solution.py:538
  11.4 1.4 %reshape.85.bias_hbm = f32[8,64,256]{2,1,0:T(8,128)} reshape(f32[8,64,4,64]{3,2,1,0:T(4,128)S(1)} %bitcast.23) | data formatting | bytes 1048576 | tf_op jit(solution)/shard_map/reshape | solution.py:538
  12.8 0.6 pad_add_fusion.place
  13.4 0.1 collective-permute-done.2.cor_in
  13.5 0.6 copy-done.9
  14.2 0.1 copy-done.6
  14.2 20.5 %shard_map.250 = (bf16[256,4096]{1,0:T(8,128)(2,1)}, bf16[256,2048]{1,0:T(8,128)(2,1)}, bf16[2,256,1024]{2,1,0:T(8,128)(2,1)}, bf16[2,48,1024]{2,1,0:T(8,128)(2,...) custom-call(s32[3]{0:T(128)} %pad_add_fusion.place, s32[1,32]{1,0:T(1,128)} %row_field.1, ...), custom_call_target="tpu_custom_call" | custom-call | flops 5000000000 | bytes 20971520 | tf_op jit(solution)/shard_map/pallas_call | solution.py:540
  34.7 0.1 collective-permute-start.6
  34.8 10.5 %all-to-all-start = ((bf16[128,8,256]{2,1,0:T(8,128)(2,1)}), bf16[128,8,256]{2,1,0:T(8,128)(2,1)S(1)}, u32[]{:S(2)}, u32[]{:S(2)}) async-start(bf16[128,8,256]{2,1,0:T(8,128)(2,1)} %bitcast.25), calls=%async_computation | async-start | bytes 1048576 | tf_op jit(solution)/shard_map/all_to_all | solution.py:568
  45.3 1.3 copy-done.4
  46.6 5.3 %shard_map.252 = bf16[1024,2304]{1,0:T(8,128)(2,1)} custom-call(bf16[256,4096]{1,0:T(8,128)(2,1)} %get-tuple-element.53.send, bf16[256,2048]{1,0:T(8,128)(2,1)} %get-tuple-element.54.keep, bf16[256,4096]{1,0:T(8,128)(2,1)} %copy-done.4), custom_call_target="tpu_custom_call" | custom-call | flops 2147483648 | bytes 9437184 | tf_op jit(solution)/shard_map/pallas_call | solution.py:572
  51.9 6.9 %all-to-all-done = bf16[128,8,256]{2,1,0:T(8,128)(2,1)S(1)} async-done(((bf16[128,8,256]{2,1,0:T(8,128)(2,1)}), bf16[128,8,256]{2,1,0:T(8,128)(2,1)S(1)}, u32[]{:S(2)}, u32[]{:S(2)}) %all-to-all-start) | async-done | bytes 524320 | tf_op jit(solution)/shard_map/all_to_all | solution.py:568
  58.9 0.1 reduce_sum.12
  59.0 0.9 broadcast_dynamic-update-slice_fusion
  59.9 6.0 %all-to-all-start.1 = ((bf16[128,8,2304]{2,1,0:T(8,128)(2,1)}), bf16[128,8,2304]{2,1,0:T(8,128)(2,1)}, u32[]{:S(2)}, u32[]{:S(2)}) async-start(bf16[128,8,2304]{2,1,0:T(8,128)(2,1)} %broadcast_dynamic-update-slice_fusion), calls=%async_computation.1 | async-start | bytes 9437184 | tf_op jit(solution)/shard_map/all_to_all | solution.py:585
  65.9 1.1 collective-permute-start.3
  67.0 1.5 %collective-permute-start.5 = (bf16[2,16,1024]{2,1,0:T(8,128)(2,1)S(1)}, bf16[2,16,1024]{2,1,0:T(8,128)(2,1)S(1)}, u32[]{:S(2)}, u32[]{:S(2)}) collective-permute-start(bf16[2,16,1024]{2,1,0:T(8,128)(2,1)S(1)} %copy-done.10), channel_id=1, source_target_pairs={{0,33},{1,34},{2,35},{3,36},{4,37},{5,38},{6,39},{7,40},{8,41},{9,... | collective-permute-start | bytes 196616 | tf_op jit(solution)/shard_map/ppermute | solution.py:571
  68.5 56.3 %collective-permute-done.5.cor = bf16[2,16,1024]{2,1,0:T(8,128)(2,1)S(1)} collective-permute-done((bf16[2,16,1024]{2,1,0:T(8,128)(2,1)S(1)}, bf16[2,16,1024]{2,1,0:T(8,128)(2,1)S(1)}, u32[]{:S(2)}, u32[]{:S(2)}) %collective-permute-start.5) | collective-permute-done | bytes 65568 | tf_op jit(solution)/shard_map/ppermute | solution.py:571
  124.8 1.3 %shard_map.251 = (bf16[256,1024]{1,0:T(8,128)(2,1)}, bf16[256,1024]{1,0:T(8,128)(2,1)}) custom-call(bf16[256,1024]{1,0:T(8,128)(2,1)S(1)} %bitcast.18, bf16[256,1024]{1,0:T(8,128)(2,1)S(1)} %bitcast.21, bf16[2,256,1024]{2,1,0:T(8,128)(2,1)S(1)} %copy-done.2, bf16[2,48,1024]{2,1,0:T(8,128)(2,1)S(1)} %collective-permute-done.3.row, ...), custom_call_target="tpu_custom_call" | custom-call | flops 100000000 | bytes 4194304 | tf_op jit(solution)/shard_map/pallas_call | solution.py:586
  126.2 3.7 %shard_map.253 = (f32[8,3072]{1,0:T(8,128)}, f32[8,1024]{1,0:T(8,128)}, f32[32,64,64]{2,1,0:T(8,128)}, f32[3072]{0:T(1024)}, f32[1024]{0:T(1024)}, /*index=5*/f32[1024]{0:T(1024)}, f32[1024]{0:T(1024)}, f32[32]{0:T(128)}) custom-call(bf16[64,2,8,2304]{3,2,1,0:T(8,128)(2,1)} %bitcast.15.got_hbm), custom_call_target="tpu_custom_call" | custom-call | flops 10000000 | bytes 4194304 | tf_op jit(solution)/shard_map/pallas_call | solution.py:595
  (26 shorter events, 0.1 us)
Async XLA Ops:
  2.9 10.6 %collective-permute-start = (bf16[2,48,1024]{2,1,0:T(8,128)(2,1)}, bf16[2,48,1024]{2,1,0:T(8,128)(2,1)S(1)}, u32[]{:S(2)}, u32[]{:S(2)}) collective-permute-start(bf16[2,48,1024]{2,1,0:T(8,128)(2,1)} %get-tuple-element.44), channel_id=1, source_target_pairs={{0,32},{1,33},{2,34},{3,35},{4,36},{5,37},{6,38},{7,39},{8,40},{9,... | collective-permute-start | bytes 589832 | tf_op jit(solution)/shard_map/ppermute | solution.py:532
  4.9 8.6 %collective-permute-start.1 = (bf16[2,48,1024]{2,1,0:T(8,128)(2,1)}, bf16[2,48,1024]{2,1,0:T(8,128)(2,1)S(1)}, u32[]{:S(2)}, u32[]{:S(2)}) collective-permute-start(bf16[2,48,1024]{2,1,0:T(8,128)(2,1)} %get-tuple-element.45), channel_id=1, source_target_pairs={{0,31},{1,0},{2,1},{3,2},{4,3},{5,4},{6,5},{7,6},{8,7},{9,8},{10,9... | collective-permute-start | bytes 589832 | tf_op jit(solution)/shard_map/ppermute | solution.py:533
  9.3 4.2 %collective-permute-start.2 = (bf16[2,16,1024]{2,1,0:T(8,128)(2,1)}, bf16[2,16,1024]{2,1,0:T(8,128)(2,1)S(1)}, u32[]{:S(2)}, u32[]{:S(2)}) collective-permute-start(bf16[2,16,1024]{2,1,0:T(8,128)(2,1)} %get-tuple-element.46), channel_id=1, source_target_pairs={{0,63},{1,32},{2,33},{3,34},{4,35},{5,36},{6,37},{7,38},{8,39},{9,... | collective-permute-start | bytes 196616 | tf_op jit(solution)/shard_map/ppermute | solution.py:534
  13.5 0.6 copy-start.9
  13.5 0.7 copy-start.5
  13.5 0.8 copy-start.6
  34.7 10.6 %collective-permute-start.6 = (bf16[256,4096]{1,0:T(8,128)(2,1)}, bf16[256,4096]{1,0:T(8,128)(2,1)S(1)}, u32[]{:S(2)}, u32[]{:S(2)}) collective-permute-start(bf16[256,4096]{1,0:T(8,128)(2,1)} %get-tuple-element.53.send), channel_id=1, source_target_pairs={{0,1},{1,0},{2,3},{3,2},{4,5},{5,4},{6,7},{7,6},{8,9},{9,8},{10,11... | collective-permute-start | bytes 6291464 | tf_op jit(solution)/shard_map/ppermute | solution.py:566
  34.8 24.0 %all-to-all-start = ((bf16[128,8,256]{2,1,0:T(8,128)(2,1)}), bf16[128,8,256]{2,1,0:T(8,128)(2,1)S(1)}, u32[]{:S(2)}, u32[]{:S(2)}) async-start(bf16[128,8,256]{2,1,0:T(8,128)(2,1)} %bitcast.25), calls=%async_computation | async-start | bytes 1048576 | tf_op jit(solution)/shard_map/all_to_all | solution.py:568
  45.3 1.3 copy-start.4
  59.9 6.0 %copy-start.8 = (bf16[2,48,1024]{2,1,0:T(8,128)(2,1)S(1)}, bf16[2,48,1024]{2,1,0:T(8,128)(2,1)}, u32[]{:S(2)}) copy-start(bf16[2,48,1024]{2,1,0:T(8,128)(2,1)} %get-tuple-element.48) | copy-start | bytes 589828
  59.9 7.1 %copy-start.7 = (bf16[2,48,1024]{2,1,0:T(8,128)(2,1)S(1)}, bf16[2,48,1024]{2,1,0:T(8,128)(2,1)}, u32[]{:S(2)}) copy-start(bf16[2,48,1024]{2,1,0:T(8,128)(2,1)} %get-tuple-element.49) | copy-start | bytes 589828
  59.9 7.1 %copy-start.10 = (bf16[2,16,1024]{2,1,0:T(8,128)(2,1)S(1)}, bf16[2,16,1024]{2,1,0:T(8,128)(2,1)}, u32[]{:S(2)}) copy-start(bf16[2,16,1024]{2,1,0:T(8,128)(2,1)} %get-tuple-element.50) | copy-start | bytes 196612
  59.9 64.9 %copy-start = (bf16[1,16,16,1024]{3,2,1,0:T(8,128)(2,1)S(1)}, bf16[1,16,16,1024]{3,2,1,0:T(8,128)(2,1)}, u32[]{:S(2)}) copy-start(bf16[1,16,16,1024]{3,2,1,0:T(8,128)(2,1)} %param.20) | copy-start | bytes 1572868
  59.9 64.9 %copy-start.1 = (bf16[1,16,16,1024]{3,2,1,0:T(8,128)(2,1)S(1)}, bf16[1,16,16,1024]{3,2,1,0:T(8,128)(2,1)}, u32[]{:S(2)}) copy-start(bf16[1,16,16,1024]{3,2,1,0:T(8,128)(2,1)} %param.21) | copy-start | bytes 1572868
  59.9 64.9 %copy-start.2 = (bf16[2,256,1024]{2,1,0:T(8,128)(2,1)S(1)}, bf16[2,256,1024]{2,1,0:T(8,128)(2,1)}, u32[]{:S(2)}) copy-start(bf16[2,256,1024]{2,1,0:T(8,128)(2,1)} %get-tuple-element.47.own) | copy-start | bytes 3145732
  59.9 64.9 %copy-start.3 = (bf16[256,112]{1,0:T(8,128)(2,1)S(1)}, bf16[256,112]{1,0:T(8,128)(2,1)}, u32[]{:S(2)}) copy-start(bf16[256,112]{1,0:T(8,128)(2,1)} %constant.69.clone.spread) | copy-start | bytes 172036
  59.9 66.2 %all-to-all-start.1 = ((bf16[128,8,2304]{2,1,0:T(8,128)(2,1)}), bf16[128,8,2304]{2,1,0:T(8,128)(2,1)}, u32[]{:S(2)}, u32[]{:S(2)}) async-start(bf16[128,8,2304]{2,1,0:T(8,128)(2,1)} %broadcast_dynamic-update-slice_fusion), calls=%async_computation.1 | async-start | bytes 9437184 | tf_op jit(solution)/shard_map/all_to_all | solution.py:585
  65.9 58.9 %collective-permute-start.3 = (bf16[2,48,1024]{2,1,0:T(8,128)(2,1)S(1)}, bf16[2,48,1024]{2,1,0:T(8,128)(2,1)S(1)}, u32[]{:S(2)}, u32[]{:S(2)}) collective-permute-start(bf16[2,48,1024]{2,1,0:T(8,128)(2,1)S(1)} %copy-done.8), channel_id=1, source_target_pairs={{0,32},{1,33},{2,34},{3,35},{4,36},{5,37},{6,38},{7,39},{8,40},{9,... | collective-permute-start | bytes 589832 | tf_op jit(solution)/shard_map/ppermute | solution.py:569
  67.0 57.8 %collective-permute-start.4 = (bf16[2,48,1024]{2,1,0:T(8,128)(2,1)S(1)}, bf16[2,48,1024]{2,1,0:T(8,128)(2,1)S(1)}, u32[]{:S(2)}, u32[]{:S(2)}) collective-permute-start(bf16[2,48,1024]{2,1,0:T(8,128)(2,1)S(1)} %copy-done.7), channel_id=1, source_target_pairs={{0,1},{1,2},{2,3},{3,4},{4,5},{5,6},{6,7},{7,8},{8,9},{9,10},{10,1... | collective-permute-start | bytes 589832 | tf_op jit(solution)/shard_map/ppermute | solution.py:570
  67.0 57.8 %collective-permute-start.5 = (bf16[2,16,1024]{2,1,0:T(8,128)(2,1)S(1)}, bf16[2,16,1024]{2,1,0:T(8,128)(2,1)S(1)}, u32[]{:S(2)}, u32[]{:S(2)}) collective-permute-start(bf16[2,16,1024]{2,1,0:T(8,128)(2,1)S(1)} %copy-done.10), channel_id=1, source_target_pairs={{0,33},{1,34},{2,35},{3,36},{4,37},{5,38},{6,39},{7,40},{8,41},{9,... | collective-permute-start | bytes 196616 | tf_op jit(solution)/shard_map/ppermute | solution.py:571
